TPU v7x, 32 devices: a whole 2x2x4 slice. The times are simulated.
32 devices in a mesh: expert: 8 (over z, x), fsdp: 4 (over y, core).
Axes of the slice: x: 2, y: 2, z: 4, core: 2. Of those that a mesh axis runs over, the one named last changes fastest.
Arguments:
- tokens_in: bfloat16 [8192, 768], P(('expert', 'fsdp')), may hold values from -6 to 6
- seg_ids: int32 [8192], P(('expert', 'fsdp')), may hold values from 0 to 2, as said below
- routes: int32 [8192, 2], P(('expert', 'fsdp')), may hold values from 0 to 7, all different within a row; in each aligned block of 256 rows (0 to 255, 256 to 511, ...) at most 96 rows name the same one
- buckets: int32 [1024], replicated, may hold values from 0 to 31, as said below
- attn_gain: bfloat16 [768], P('fsdp'), may hold values from 0.5 to 1.5
- w_query: bfloat16 [768, 768], P('fsdp'), may hold values from -0.3125 to 0.3125
- w_key: bfloat16 [768, 768], P('fsdp'), may hold values from -0.3125 to 0.3125
- w_value: bfloat16 [768, 768], P('fsdp'), may hold values from -0.21875 to 0.21875
- w_output: bfloat16 [768, 768], P('fsdp'), may hold values from -0.875 to 0.875
- bias_table: bfloat16 [32, 12], P('fsdp'), may hold values from -4 to 4
- ffn_gain: bfloat16 [768], P('fsdp'), may hold values from 0.5 to 1.5
- w_router: bfloat16 [768, 8], P('fsdp'), may hold values from -0.15625 to 0.15625
- w_in: bfloat16 [8, 768, 3072], P('expert'), may hold values from -0.21875 to 0.21875
- w_out: bfloat16 [8, 3072, 768], P('expert'), may hold values from -0.109375 to 0.109375
- cotangent: bfloat16 [8192, 768], P(('expert', 'fsdp')), may hold values from -6 to 6
Outputs:
- block_out: bfloat16 [8192, 768], P(('expert', 'fsdp'))
- grad_tokens: float32 [8192, 768], P(('expert', 'fsdp'))
- grad_attn_gain: float32 [768], P('fsdp')
- grad_query: float32 [768, 768], P('fsdp')
- grad_key: float32 [768, 768], P('fsdp')
- grad_value: float32 [768, 768], P('fsdp')
- grad_output: float32 [768, 768], P('fsdp')
- grad_bias_table: float32 [32, 12], P('fsdp')
- grad_ffn_gain: float32 [768], P('fsdp')
- grad_router: float32 [768, 8], P('fsdp')
- grad_w_in: float32 [8, 768, 3072], P('expert', 'fsdp')
- grad_w_out: float32 [8, 3072, 768], P('expert', 'fsdp')
Inputs may be any that keep to these rules, and one draw needn't show every extreme that they name: `seg_ids`: each sequence of 1024 tokens holds three documents in order: document 0 from position 0, document 1 beginning among the first 128 positions, document 2 beginning among the last 128 positions; each has at least one token. `routes`: each row names 2 different experts; among the tokens of one device no expert is named more than 96 times. `buckets`: never falls as the distance grows; distance d has bucket d for d < 16; the largest distance has bucket 32 - 1.
All inputs are finite; a program needn't handle non-finite values.
Results may differ from a plain program's by a relative error of at most 0.023.
Values may be sent and summed in bfloat16 or wider, within the bound.
No kernel may reach another device: no remote copies, remote signals or barrier semaphores. Data moves between devices by JAX's collectives and lax.ppermute only.
A program may use at most 192 MiB of HBM per device.

v0:
```python
from functools import partial

import jax
import jax.numpy as jnp
from jax import lax
from jax.sharding import PartitionSpec as P

eps = 1e-06


def contract(left_side, right_side, left_dim, right_dim):
    return lax.dot_general(
        left_side,
        right_side,
        (((left_dim,), (right_dim,)), ((), ())),
        preferred_element_type=jnp.float32,
    )


def rows_at(source_array, row_begin, row_count):
    return lax.dynamic_slice_in_dim(source_array, row_begin, row_count, 0)


def norm_forward(values, scales):
    inverse = lax.rsqrt(jnp.mean(values * values, axis=-1, keepdims=True) + eps)
    return (values * inverse * scales, inverse)


def norm_backward(values, inverse, scales, upstream):
    scaled = upstream * scales
    inner = jnp.mean(scaled * values, axis=-1, keepdims=True)
    grad_values = inverse * scaled - values * inverse**3 * inner
    grad_scales = jnp.sum(upstream * values * inverse, axis=0)
    return (grad_values, grad_scales)


def band(extended, offset, row_count, col_count):
    head_count = extended.shape[0]
    length = row_count + col_count - 1
    window = lax.dynamic_slice_in_dim(extended, offset - (col_count - 1), length, 1)
    repeated = jnp.concatenate(
        [jnp.tile(window, (1, row_count)), jnp.zeros((head_count, row_count), jnp.float32)], axis=1
    )
    return repeated.reshape(head_count, row_count, length + 1)[:, :, :col_count][:, :, ::-1]


def band_grad(grad_scores, row_count, col_count):
    head_count = grad_scores.shape[0]
    length = row_count + col_count - 1
    padded = jnp.pad(grad_scores[:, :, ::-1], ((0, 0), (0, 0), (0, row_count)))
    folded = padded.reshape(head_count, row_count * (length + 1))[:, : row_count * length]
    return jnp.sum(folded.reshape(head_count, row_count, length), axis=1)


def score_block(query_heads, key_heads, extended, offset, score_scale):
    products = jnp.einsum(
        "qhd,khd->hqk", query_heads, key_heads, preferred_element_type=jnp.float32
    )
    return products * score_scale + band(extended, offset, query_heads.shape[0], key_heads.shape[0])


def per_device(
    tokens_in,
    seg_ids,
    routes,
    buckets,
    attn_gain,
    w_query,
    w_key,
    w_value,
    w_output,
    bias_table,
    ffn_gain,
    w_router,
    w_in,
    w_out,
    cotangent,
):
    gathered = (
        lax.all_gather(attn_gain, "fsdp", axis=0, tiled=True),
        lax.all_gather(w_query, "fsdp", axis=0, tiled=True),
        lax.all_gather(w_key, "fsdp", axis=0, tiled=True),
        lax.all_gather(w_value, "fsdp", axis=0, tiled=True),
        lax.all_gather(w_output, "fsdp", axis=0, tiled=True),
        lax.all_gather(bias_table, "fsdp", axis=0, tiled=True),
        lax.all_gather(ffn_gain, "fsdp", axis=0, tiled=True),
        lax.all_gather(w_router, "fsdp", axis=0, tiled=True),
    )
    gain_attn = gathered[0].astype(jnp.float32)
    full_query, full_key, full_value, full_output = (
        gathered[1],
        gathered[2],
        gathered[3],
        gathered[4],
    )
    bias_rows = gathered[5].astype(jnp.float32)
    gain_ffn = gathered[6].astype(jnp.float32)
    full_router = gathered[7]
    tokens, model_width = tokens_in.shape
    bucket_count, head_count = bias_rows.shape
    head_dim = model_width // head_count
    seq_length = buckets.shape[0]
    block_rows = min(seq_length, 512)
    block_count = seq_length // block_rows
    score_scale = head_dim ** (-0.5)
    query_start = lax.axis_index("fsdp") * tokens
    query_pos = query_start + jnp.arange(tokens, dtype=jnp.int32)
    blocks = jnp.arange(block_count, dtype=jnp.int32)
    inputs = tokens_in.astype(jnp.float32)
    normed_full, inverse_attn = norm_forward(inputs, gain_attn)
    normed = normed_full.astype(jnp.bfloat16)
    queries = jnp.dot(normed, full_query, preferred_element_type=jnp.float32).astype(jnp.bfloat16)
    keys_local = jnp.dot(normed, full_key, preferred_element_type=jnp.float32).astype(jnp.bfloat16)
    values_local = jnp.dot(normed, full_value, preferred_element_type=jnp.float32).astype(
        jnp.bfloat16
    )
    all_keys, all_values, all_segments = (
        lax.all_gather(keys_local, "fsdp", axis=0, tiled=True),
        lax.all_gather(values_local, "fsdp", axis=0, tiled=True),
        lax.all_gather(seg_ids, "fsdp", axis=0, tiled=True),
    )
    bucket_hot = (buckets[:, None] == jnp.arange(bucket_count, dtype=jnp.int32)[None, :]).astype(
        jnp.float32
    )
    by_distance = jnp.dot(
        bucket_hot, bias_rows, precision=lax.Precision.HIGHEST, preferred_element_type=jnp.float32
    ).T
    extended = jnp.concatenate(
        [jnp.zeros((head_count, seq_length), jnp.float32), by_distance], axis=1
    )
    query_heads = queries.reshape(tokens, head_count, head_dim)

    def key_block(block_index):
        key_first = block_index * block_rows
        key_piece = rows_at(all_keys, key_first, block_rows).reshape(
            block_rows, head_count, head_dim
        )
        value_piece = rows_at(all_values, key_first, block_rows).reshape(
            block_rows, head_count, head_dim
        )
        segments = rows_at(all_segments, key_first, block_rows)
        key_pos = key_first + jnp.arange(block_rows, dtype=jnp.int32)
        scores = score_block(
            query_heads, key_piece, extended, query_start - key_first + seq_length, score_scale
        )
        allowed = (key_pos[None, :] <= query_pos[:, None]) & (segments[None, :] == seg_ids[:, None])
        return (scores, allowed[None], key_piece, value_piece)

    def running_max(running_sums, block_index):
        top_score, row_total = running_sums
        scores, allowed, key_piece, value_piece = key_block(block_index)
        masked = jnp.where(allowed, scores, -1e30)
        new_top = jnp.maximum(top_score, jnp.max(masked, axis=2))
        fresh = jnp.sum(jnp.where(allowed, jnp.exp(scores - new_top[:, :, None]), 0.0), axis=2)
        return ((new_top, row_total * jnp.exp(top_score - new_top) + fresh), None)

    start_top = jnp.full((head_count, tokens), -1e30, jnp.float32)
    (top_score, row_total), unused = lax.scan(
        running_max, (start_top, jnp.zeros((head_count, tokens), jnp.float32)), blocks
    )
    log_total = top_score + jnp.log(row_total)

    def weighted_sum(context, block_index):
        scores, allowed, key_piece, value_piece = key_block(block_index)
        probs_full = jnp.where(allowed, jnp.exp(scores - log_total[:, :, None]), 0.0)
        context = context + jnp.einsum(
            "hqk,khd->qhd",
            probs_full.astype(jnp.bfloat16),
            value_piece,
            preferred_element_type=jnp.float32,
        )
        return (context, None)

    context, unused = lax.scan(
        weighted_sum, jnp.zeros((tokens, head_count, head_dim), jnp.float32), blocks
    )
    context = context.reshape(tokens, model_width)
    context_low = context.astype(jnp.bfloat16)
    residual = inputs + jnp.dot(context_low, full_output, preferred_element_type=jnp.float32)
    ffn_full, inverse_ffn = norm_forward(residual, gain_ffn)
    ffn_low = ffn_full.astype(jnp.bfloat16)
    logits = jnp.dot(ffn_low, full_router, preferred_element_type=jnp.float32)
    expert_count = logits.shape[1]
    top_count = routes.shape[1]
    chosen_hot = routes[:, :, None] == jnp.arange(expert_count, dtype=jnp.int32)[None, None, :]
    chosen = jnp.sum(jnp.where(chosen_hot, logits[:, None, :], 0.0), axis=2)
    gate_weights = jax.nn.softmax(chosen, axis=1)
    capacity = 3 * top_count * tokens // (2 * expert_count)
    flat_hot = chosen_hot.reshape(tokens * top_count, expert_count).astype(jnp.int32)
    earlier = jnp.cumsum(flat_hot, axis=0) - flat_hot
    slot_index = jnp.sum(earlier * flat_hot, axis=1)
    destination = routes.reshape(-1) * capacity + slot_index
    outgoing = (
        jnp.zeros((expert_count * capacity, model_width), jnp.bfloat16)
        .at[destination]
        .set(jnp.repeat(ffn_low, top_count, axis=0))
    )
    outgoing = outgoing.reshape(expert_count, capacity, model_width)
    expert_in = w_in[0]
    expert_out = w_out[0]
    arrived = lax.all_to_all(outgoing, "expert", split_axis=0, concat_axis=0, tiled=True)
    flat_rows = arrived.reshape(-1, model_width)
    hidden = jnp.dot(flat_rows, expert_in, preferred_element_type=jnp.float32)
    active = jax.nn.gelu(hidden, approximate=False).astype(jnp.bfloat16)
    produced = (
        jnp.dot(active, expert_out, preferred_element_type=jnp.float32)
        .astype(jnp.bfloat16)
        .reshape(arrived.shape)
    )
    returned = lax.all_to_all(produced, "expert", split_axis=0, concat_axis=0, tiled=True)
    picked = (
        returned.reshape(expert_count * capacity, model_width)[destination]
        .reshape(tokens, top_count, model_width)
        .astype(jnp.float32)
    )
    block_out = (residual + jnp.sum(gate_weights[:, :, None] * picked, axis=1)).astype(jnp.bfloat16)
    upstream = cotangent.astype(jnp.float32)
    grad_gates = jnp.sum(picked * upstream[:, None, :], axis=2)
    grad_produced = (
        (gate_weights[:, :, None] * upstream[:, None, :])
        .astype(jnp.bfloat16)
        .reshape(tokens * top_count, model_width)
    )
    grad_buffer = (
        jnp.zeros((expert_count * capacity, model_width), jnp.bfloat16)
        .at[destination]
        .set(grad_produced)
    )
    grad_arrived = lax.all_to_all(
        grad_buffer.reshape(expert_count, capacity, model_width),
        "expert",
        split_axis=0,
        concat_axis=0,
        tiled=True,
    )
    arrived_rows = lax.all_to_all(outgoing, "expert", split_axis=0, concat_axis=0, tiled=True)
    flat_rows = arrived_rows.reshape(-1, model_width)
    grad_flat = grad_arrived.reshape(-1, model_width)
    hidden = jnp.dot(flat_rows, expert_in, preferred_element_type=jnp.float32)
    active, gelu_back = jax.vjp(partial(jax.nn.gelu, approximate=False), hidden)
    active_low = active.astype(jnp.bfloat16)
    grad_active = contract(grad_flat, expert_out, 1, 1)
    grad_hidden = gelu_back(grad_active)[0].astype(jnp.bfloat16)
    grad_rows = (
        contract(grad_hidden, expert_in, 1, 1).astype(jnp.bfloat16).reshape(arrived_rows.shape)
    )
    grad_back = lax.all_to_all(grad_rows, "expert", split_axis=0, concat_axis=0, tiled=True)
    grad_in_part = contract(flat_rows, grad_hidden, 0, 0)
    grad_out_part = contract(active_low, grad_flat, 0, 0)
    grad_in_rows, grad_out_rows = (
        lax.psum_scatter(
            grad_in_part.astype(jnp.bfloat16), "fsdp", scatter_dimension=0, tiled=True
        ).astype(jnp.float32),
        lax.psum_scatter(
            grad_out_part.astype(jnp.bfloat16), "fsdp", scatter_dimension=0, tiled=True
        ).astype(jnp.float32),
    )
    mean_grad = jnp.sum(gate_weights * grad_gates, axis=1, keepdims=True)
    grad_chosen = gate_weights * (grad_gates - mean_grad)
    grad_logits = jnp.sum(jnp.where(chosen_hot, grad_chosen[:, :, None], 0.0), axis=1).astype(
        jnp.bfloat16
    )
    grad_router = contract(ffn_low, grad_logits, 0, 0)
    returned_grad = (
        grad_back.reshape(expert_count * capacity, model_width)[destination]
        .reshape(tokens, top_count, model_width)
        .astype(jnp.float32)
    )
    grad_ffn_in = jnp.sum(returned_grad, axis=1) + contract(grad_logits, full_router, 1, 1)
    grad_norm_ffn, grad_gain_ffn = norm_backward(residual, inverse_ffn, gain_ffn, grad_ffn_in)
    grad_residual = upstream + grad_norm_ffn
    grad_branch = grad_residual.astype(jnp.bfloat16)
    grad_wo = contract(context_low, grad_branch, 0, 0)
    grad_context = contract(grad_branch, full_output, 1, 1).astype(jnp.bfloat16)
    grad_context_heads = grad_context.reshape(tokens, head_count, head_dim)
    row_delta = jnp.sum(
        (grad_context.astype(jnp.float32) * context).reshape(tokens, head_count, head_dim), axis=2
    ).T

    def query_side(running_sums, block_index):
        grad_query_acc, grad_ext = running_sums
        scores, allowed, key_piece, value_piece = key_block(block_index)
        probs_full = jnp.where(allowed, jnp.exp(scores - log_total[:, :, None]), 0.0)
        grad_probs = jnp.einsum(
            "qhd,khd->hqk", grad_context_heads, value_piece, preferred_element_type=jnp.float32
        )
        grad_scores = (probs_full * (grad_probs - row_delta[:, :, None])).astype(jnp.bfloat16)
        grad_query_acc = grad_query_acc + jnp.einsum(
            "hqk,khd->qhd", grad_scores, key_piece, preferred_element_type=jnp.float32
        )
        offset = query_start - block_index * block_rows + seq_length
        ext_begin = offset - (block_rows - 1)
        band_sum = band_grad(grad_scores.astype(jnp.float32), tokens, block_rows)
        current = lax.dynamic_slice_in_dim(grad_ext, ext_begin, tokens + block_rows - 1, 1)
        grad_ext = lax.dynamic_update_slice_in_dim(grad_ext, current + band_sum, ext_begin, 1)
        key_part = jnp.einsum(
            "hqk,qhd->khd", grad_scores, query_heads, preferred_element_type=jnp.float32
        )
        value_part = jnp.einsum(
            "hqk,qhd->khd",
            probs_full.astype(jnp.bfloat16),
            grad_context_heads,
            preferred_element_type=jnp.float32,
        )
        return ((grad_query_acc, grad_ext), (key_part, value_part))

    start_sums = (
        jnp.zeros((tokens, head_count, head_dim), jnp.float32),
        jnp.zeros((head_count, 2 * seq_length), jnp.float32),
    )
    (grad_query_acc, grad_ext), block_parts = lax.scan(query_side, start_sums, blocks)
    grad_keys, grad_values = (
        lax.psum_scatter(
            block_parts[0].reshape(seq_length, model_width).astype(jnp.bfloat16),
            "fsdp",
            scatter_dimension=0,
            tiled=True,
        ).astype(jnp.float32),
        lax.psum_scatter(
            block_parts[1].reshape(seq_length, model_width).astype(jnp.bfloat16),
            "fsdp",
            scatter_dimension=0,
            tiled=True,
        ).astype(jnp.float32),
    )
    grad_query_low = (grad_query_acc.reshape(tokens, model_width) * score_scale).astype(
        jnp.bfloat16
    )
    grad_key_low = (grad_keys * score_scale).astype(jnp.bfloat16)
    grad_value_low = grad_values.astype(jnp.bfloat16)
    grad_wq = contract(normed, grad_query_low, 0, 0)
    grad_wk = contract(normed, grad_key_low, 0, 0)
    grad_wv = contract(normed, grad_value_low, 0, 0)
    grad_normed = (
        contract(grad_query_low, full_query, 1, 1)
        + contract(grad_key_low, full_key, 1, 1)
        + contract(grad_value_low, full_value, 1, 1)
    )
    grad_norm_attn, grad_gain_attn = norm_backward(inputs, inverse_attn, gain_attn, grad_normed)
    grad_tokens = grad_residual + grad_norm_attn
    grad_by_distance = grad_ext[:, seq_length:]
    grad_bias = lax.dot_general(
        bucket_hot,
        grad_by_distance,
        (((0,), (1,)), ((), ())),
        precision=lax.Precision.HIGHEST,
        preferred_element_type=jnp.float32,
    )
    shards = (
        lax.psum_scatter(
            grad_gain_attn.astype(jnp.bfloat16), "fsdp", scatter_dimension=0, tiled=True
        ).astype(jnp.float32),
        lax.psum_scatter(
            grad_wq.astype(jnp.bfloat16), "fsdp", scatter_dimension=0, tiled=True
        ).astype(jnp.float32),
        lax.psum_scatter(
            grad_wk.astype(jnp.bfloat16), "fsdp", scatter_dimension=0, tiled=True
        ).astype(jnp.float32),
        lax.psum_scatter(
            grad_wv.astype(jnp.bfloat16), "fsdp", scatter_dimension=0, tiled=True
        ).astype(jnp.float32),
        lax.psum_scatter(
            grad_wo.astype(jnp.bfloat16), "fsdp", scatter_dimension=0, tiled=True
        ).astype(jnp.float32),
        lax.psum_scatter(
            grad_bias.astype(jnp.bfloat16), "fsdp", scatter_dimension=0, tiled=True
        ).astype(jnp.float32),
        lax.psum_scatter(
            grad_gain_ffn.astype(jnp.bfloat16), "fsdp", scatter_dimension=0, tiled=True
        ).astype(jnp.float32),
        lax.psum_scatter(
            grad_router.astype(jnp.bfloat16), "fsdp", scatter_dimension=0, tiled=True
        ).astype(jnp.float32),
    )
    summed = (
        lax.psum(shards[0].astype(jnp.bfloat16), "expert").astype(jnp.float32),
        lax.psum(shards[1].astype(jnp.bfloat16), "expert").astype(jnp.float32),
        lax.psum(shards[2].astype(jnp.bfloat16), "expert").astype(jnp.float32),
        lax.psum(shards[3].astype(jnp.bfloat16), "expert").astype(jnp.float32),
        lax.psum(shards[4].astype(jnp.bfloat16), "expert").astype(jnp.float32),
        lax.psum(shards[5].astype(jnp.bfloat16), "expert").astype(jnp.float32),
        lax.psum(shards[6].astype(jnp.bfloat16), "expert").astype(jnp.float32),
        lax.psum(shards[7].astype(jnp.bfloat16), "expert").astype(jnp.float32),
    )
    return (
        block_out,
        grad_tokens,
        summed[0],
        summed[1],
        summed[2],
        summed[3],
        summed[4],
        summed[5],
        summed[6],
        summed[7],
        grad_in_rows[None],
        grad_out_rows[None],
    )


def solution(mesh):
    return jax.shard_map(
        per_device,
        mesh=mesh,
        in_specs=(
            P(("expert", "fsdp"), None),
            P(("expert", "fsdp")),
            P(("expert", "fsdp"), None),
            P(),
            P("fsdp"),
            P("fsdp", None),
            P("fsdp", None),
            P("fsdp", None),
            P("fsdp", None),
            P("fsdp", None),
            P("fsdp"),
            P("fsdp", None),
            P("expert", None, None),
            P("expert", None, None),
            P(("expert", "fsdp"), None),
        ),
        out_specs=(
            P(("expert", "fsdp"), None),
            P(("expert", "fsdp"), None),
            P("fsdp"),
            P("fsdp", None),
            P("fsdp", None),
            P("fsdp", None),
            P("fsdp", None),
            P("fsdp", None),
            P("fsdp"),
            P("fsdp", None),
            P("expert", "fsdp", None),
            P("expert", "fsdp", None),
        ),
        check_vma=False,
    )
```

profile of v0, /device:TPU:0, one launch (start us, length us, event | category | flops | bytes accessed | tf_op | source)
XLA Modules:
  0.0 1611.2 jit_solution(14479879051935926026)
XLA Ops:
  32.6 16.3 %all-gather.9.cloned.1.call-done = bf16[768,768]{1,0:T(8,128)(2,1)} async-done(((bf16[192,768]{1,0:T(8,128)(2,1)}), bf16[768,768]{1,0:T(8,128)(2,1)}) %all-gather.9.cloned.1.call-update) | async-done | bytes 1179664 | tf_op jit(solution)/shard_map/all_gather | solution.py:83
  69.9 19.7 %all-gather.15.cloned.1.call-done = bf16[1024,768]{1,0:T(8,128)(2,1)} async-done(((bf16[256,768]{1,0:T(8,128)(2,1)}), bf16[1024,768]{1,0:T(8,128)(2,1)}) %all-gather.15.cloned.1.call-update) | async-done | bytes 1572880 | tf_op jit(solution)/shard_map/all_gather | solution.py:118
  91.4 224.6 %while.59 = (s32[]{:T(128)}, f32[12,256]{1,0:T(8,128)S(1)}, f32[12,256]{1,0:T(8,128)S(1)}, s32[2]{0:T(128)S(1)}, s32[1024]{0:T(1024)S(1)}, /*index=5*/s32[256]{0...) while((s32[]{:T(128)}, f32[12,256]{1,0:T(8,128)S(1)}, ...), condition=%wide.region_4.5_spmd.clone.clone.clone, body=%wide.region_1.4_spmd.clone.clone.clone.sunk | while | flops 212746000 | bytes 132355240 | solution.py:158
  98.1 16.8 %tile.70 = f32[12,196352]{1,0:T(8,128)} reshape(f32[12,256,767]{2,1,0:T(8,128)} %tile.69) | data formatting | bytes 18849792 | tf_op jit(solution)/shard_map/while/body/eval_jaxpr/tile | solution.py:42
  114.9 10.1 concatenate.25
  125.0 12.9 copy.189
  150.7 48.2 %rev.52 = f32[12,256,512]{1,2,0:T(8,128)} reverse(f32[12,256,512]{1,2,0:T(8,128)} %copy.190), dimensions={2} | reverse | bytes 12582912 | tf_op jit(solution)/shard_map/while/body/eval_jaxpr/rev | solution.py:44
  210.3 16.5 %tile.70 = f32[12,196352]{1,0:T(8,128)} reshape(f32[12,256,767]{2,1,0:T(8,128)} %tile.69) | data formatting | bytes 18849792 | tf_op jit(solution)/shard_map/while/body/eval_jaxpr/tile | solution.py:42
  226.7 10.1 concatenate.25
  236.8 12.8 copy.189
  262.4 48.2 %rev.52 = f32[12,256,512]{1,2,0:T(8,128)} reverse(f32[12,256,512]{1,2,0:T(8,128)} %copy.190), dimensions={2} | reverse | bytes 12582912 | tf_op jit(solution)/shard_map/while/body/eval_jaxpr/rev | solution.py:44
  319.0 235.1 %while.60 = (s32[]{:T(128)}, f32[256,12,64]{0,2,1:T(8,128)}, s32[2]{0:T(128)}, bf16[1024,768]{0,1:T(8,128)(2,1)S(1)}, s32[1024]{0:T(1024)}, /*index=5*/s32[256]{...) while((s32[]{:T(128)}, f32[256,12,64]{0,2,1:T(8,128)}, ...), condition=%wide.region_6.7_spmd.clone.clone.clone, body=%wide.region_5.6_spmd.clone.clone.clone.sunk | while | flops 411304704 | bytes 123425952 | solution.py:174
  329.8 16.5 %tile.72 = f32[12,196352]{1,0:T(8,128)} reshape(f32[12,256,767]{2,1,0:T(8,128)} %tile.71) | data formatting | bytes 18849792 | tf_op jit(solution)/shard_map/while/body/eval_jaxpr/tile | solution.py:42
  346.3 10.1 concatenate.26
  356.3 12.8 copy.191
  381.9 48.2 %rev.53 = f32[12,256,512]{1,2,0:T(8,128)} reverse(f32[12,256,512]{1,2,0:T(8,128)} %copy.192), dimensions={2} | reverse | bytes 12582912 | tf_op jit(solution)/shard_map/while/body/eval_jaxpr/rev | solution.py:44
  447.2 16.5 %tile.72 = f32[12,196352]{1,0:T(8,128)} reshape(f32[12,256,767]{2,1,0:T(8,128)} %tile.71) | data formatting | bytes 18849792 | tf_op jit(solution)/shard_map/while/body/eval_jaxpr/tile | solution.py:42
  463.6 10.1 concatenate.26
  473.7 12.8 copy.191
  499.3 48.2 %rev.53 = f32[12,256,512]{1,2,0:T(8,128)} reverse(f32[12,256,512]{1,2,0:T(8,128)} %copy.192), dimensions={2} | reverse | bytes 12582912 | tf_op jit(solution)/shard_map/while/body/eval_jaxpr/rev | solution.py:44
  607.5 26.9 %multiply_convert_fusion = (bf16[768,3072]{1,0:T(8,128)(2,1)}, f32[768,3072]{1,0:T(8,128)}, f32[768,3072]{1,0:T(8,128)}) fusion(bf16[768,768]{1,0:T(8,128)(2,1)} %bitcast.12, bf16[1,768,3072]{2,1,0:T(8,128)(2,1)} %param.33), kind=kOutput, calls=%fused_computation.58 | convolution fusion | flops 3777232896 | bytes 29491200 | tf_op jit(solution)/shard_map/dot_general | solution.py:203
  636.2 11.2 add_convert_fusion
  669.3 19.6 %all-to-all-done.3 = bf16[8,96,768]{2,1,0:T(8,128)(2,1)S(1)} async-done(((bf16[8,96,768]{2,1,0:T(8,128)(2,1)}), bf16[8,96,768]{2,1,0:T(8,128)(2,1)S(1)}, u32[]{:S(2)}, u32[]{:S(2)}) %all-to-all-start.3) | async-done | bytes 1179680 | tf_op jit(solution)/shard_map/all_to_all | solution.py:247
  703.0 18.2 %all-to-all-done.1 = bf16[8,96,768]{2,1,0:T(8,128)(2,1)S(1)} async-done(((bf16[8,96,768]{2,1,0:T(8,128)(2,1)}), bf16[8,96,768]{2,1,0:T(8,128)(2,1)S(1)}, u32[]{:S(2)}, u32[]{:S(2)}) %all-to-all-start.1) | async-done | bytes 1179680 | tf_op jit(solution)/shard_map/all_to_all | solution.py:210
  740.9 475.8 %while.61 = (s32[]{:T(128)}, f32[256,12,64]{0,2,1:T(8,128)}, f32[12,2048]{1,0:T(8,128)}, bf16[2,512,12,64]{1,3,2,0:T(8,128)(2,1)}, bf16[2,512,12,64]{1,3,2,0:T(8...) while((s32[]{:T(128)}, f32[256,12,64]{0,2,1:T(8,128)}, ...), condition=%wide.region_25.26_spmd.clone.clone.clone, body=%wide.region_23.25_spmd.clone.clone.clone.sunk | while | flops 1022359296 | bytes 308856096 | solution.py:311
  774.3 16.5 %tile.74 = f32[12,196352]{1,0:T(8,128)} reshape(f32[12,256,767]{2,1,0:T(8,128)} %tile.73) | data formatting | bytes 18849792 | tf_op jit(solution)/shard_map/while/body/eval_jaxpr/tile | solution.py:42
  800.8 12.8 copy.193
  826.4 48.2 %rev.54 = f32[12,256,512]{1,2,0:T(8,128)} reverse(f32[12,256,512]{1,2,0:T(8,128)} %copy.194), dimensions={2} | reverse | bytes 12582912 | tf_op jit(solution)/shard_map/while/body/eval_jaxpr/rev | solution.py:44
  886.9 31.1 %rev.55 = f32[12,256,512]{1,2,0:T(8,128)} reverse(bf16[12,256,512]{1,2,0:T(8,128)(2,1)S(1)} %fusion.178), dimensions={2} | reverse | bytes 9437184 | tf_op jit(solution)/shard_map/while/body/eval_jaxpr/rev | solution.py:50
  934.2 16.4 %copy.196 = f32[2,8,256,768]{3,1,2,0:T(8,128)} copy(f32[2,8,256,768]{3,2,1,0:T(8,128)} %bitcast.253) | data formatting | bytes 25165824 | tf_op jit(solution)/shard_map/while
  960.6 20.0 %reshape.665 = f32[12,256,767]{2,1,0:T(8,128)} reshape(f32[12,196352]{1,0:T(8,128)} %slice.85) | data formatting | bytes 18849792 | tf_op jit(solution)/shard_map/while/body/eval_jaxpr/reshape | solution.py:52
  997.0 16.5 %tile.74 = f32[12,196352]{1,0:T(8,128)} reshape(f32[12,256,767]{2,1,0:T(8,128)} %tile.73) | data formatting | bytes 18849792 | tf_op jit(solution)/shard_map/while/body/eval_jaxpr/tile | solution.py:42
  1023.5 12.8 copy.193
  1049.1 48.2 %rev.54 = f32[12,256,512]{1,2,0:T(8,128)} reverse(f32[12,256,512]{1,2,0:T(8,128)} %copy.194), dimensions={2} | reverse | bytes 12582912 | tf_op jit(solution)/shard_map/while/body/eval_jaxpr/rev | solution.py:44
  1109.5 31.1 %rev.55 = f32[12,256,512]{1,2,0:T(8,128)} reverse(bf16[12,256,512]{1,2,0:T(8,128)(2,1)S(1)} %fusion.178), dimensions={2} | reverse | bytes 9437184 | tf_op jit(solution)/shard_map/while/body/eval_jaxpr/rev | solution.py:50
  1156.8 16.4 %copy.196 = f32[2,8,256,768]{3,1,2,0:T(8,128)} copy(f32[2,8,256,768]{3,2,1,0:T(8,128)} %bitcast.253) | data formatting | bytes 25165824 | tf_op jit(solution)/shard_map/while
  1183.2 20.0 %reshape.665 = f32[12,256,767]{2,1,0:T(8,128)} reshape(f32[12,196352]{1,0:T(8,128)} %slice.85) | data formatting | bytes 18849792 | tf_op jit(solution)/shard_map/while/body/eval_jaxpr/reshape | solution.py:52
  1229.6 18.2 %reduce-scatter.14.cloned.1.call-done = bf16[256,768]{0,1:T(8,128)(2,1)} async-done(((bf16[1024,768]{0,1:T(8,128)(2,1)}), bf16[256,768]{0,1:T(8,128)(2,1)}) %reduce-scatter.14.cloned.1.call-update) | async-done | bytes 393232 | tf_op jit(solution)/shard_map/reduce_scatter | solution.py:319
  1250.5 28.8 %reduce-scatter.12.cloned.1.call-done = bf16[256,768]{0,1:T(8,128)(2,1)} async-done(((bf16[1024,768]{0,1:T(8,128)(2,1)}), bf16[256,768]{0,1:T(8,128)(2,1)}) %reduce-scatter.12.cloned.1.call-update) | async-done | bytes 393232 | tf_op jit(solution)/shard_map/reduce_scatter | solution.py:313
  1283.1 24.5 %reduce-scatter.22.cloned.1.call-done = bf16[192,768]{1,0:T(8,128)(2,1)} async-done(((bf16[768,768]{1,0:T(8,128)(2,1)}), bf16[192,768]{1,0:T(8,128)(2,1)}) %reduce-scatter.22.cloned.1.call-update) | async-done | bytes 294928 | tf_op jit(solution)/shard_map/reduce_scatter | solution.py:362
  1307.6 28.9 %reduce-scatter.16.cloned.1.call-done = bf16[192,768]{1,0:T(8,128)(2,1)} async-done(((bf16[768,768]{1,0:T(8,128)(2,1)}), bf16[192,768]{1,0:T(8,128)(2,1)}) %reduce-scatter.16.cloned.1.call-update) | async-done | bytes 294928 | tf_op jit(solution)/shard_map/reduce_scatter | solution.py:353
  1336.6 28.3 %reduce-scatter.20.cloned.1.call-done = bf16[192,768]{1,0:T(8,128)(2,1)} async-done(((bf16[768,768]{1,0:T(8,128)(2,1)}), bf16[192,768]{1,0:T(8,128)(2,1)}) %reduce-scatter.20.cloned.1.call-update) | async-done | bytes 294928 | tf_op jit(solution)/shard_map/reduce_scatter | solution.py:359
  1364.9 28.9 %reduce-scatter.18.cloned.1.call-done = bf16[192,768]{1,0:T(8,128)(2,1)} async-done(((bf16[768,768]{1,0:T(8,128)(2,1)}), bf16[192,768]{1,0:T(8,128)(2,1)}) %reduce-scatter.18.cloned.1.call-update) | async-done | bytes 294928 | tf_op jit(solution)/shard_map/reduce_scatter | solution.py:356
  1421.2 10.5 all-reduce.12
  1431.9 21.7 %all-reduce.10 = (bf16[192]{0:T(256)(128)(2,1)S(1)}, bf16[8,12]{1,0:T(8,128)(2,1)S(1)}, bf16[192]{0:T(256)(128)(2,1)S(1)}, bf16[192,8]{0,1:T(8,128)(2,1)S(1)}) all-reduce(bf16[192]{0:T(256)(128)(2,1)S(1)} %dynamic-slice.3, bf16[8,12]{1,0:T(8,128)(2,1)S(1)} %constant_dynamic-slice_fusion.8, ...), channel_id=1, replica_groups=mesh['expert'=8,'fsdp'=4] {'expert'}, use_global_device_ids=true, to_apply=%region_31.32 | all-reduce | flops 2016 | bytes 8064 | tf_op jit(solution)/shard_map/psum | solution.py:376
  1457.0 44.7 %all-reduce.16.cloned.1.call-done = (bf16[192,768]{1,0:T(8,128)(2,1)}, bf16[192,768]{1,0:T(8,128)(2,1)}, bf16[192,768]{1,0:T(8,128)(2,1)}, bf16[192,768]{1,0:T(8,128)(2,1)}) async-done(((bf16[192,768]{1,0:T(8,128)(2,1)}, bf16[192,768]{1,0:T(8,128)(2,1)}, bf16[192,768]{1,0:T(8,128)(2,1)}, bf16[192,768]{1,0:T(8,128)(2,1)}), (bf16[192,768]{1,0:T(8,128)(2,1)}, bf16[192,768]{1,0:T(8,128)(2,1)}, ...) | async-done | bytes 1179664 | tf_op jit(solution)/shard_map/psum | solution.py:377
  1509.0 42.3 %reduce-scatter.24.cloned.1.call-done = bf16[192,3072]{1,0:T(8,128)(2,1)} async-done(((bf16[768,3072]{1,0:T(8,128)(2,1)}), bf16[192,3072]{1,0:T(8,128)(2,1)}) %reduce-scatter.24.cloned.1.call-update) | async-done | bytes 1179664 | tf_op jit(solution)/shard_map/reduce_scatter | solution.py:251
  1554.2 47.3 %reduce-scatter.26.cloned.1.call-done = bf16[768,768]{1,0:T(8,128)(2,1)} async-done(((bf16[3072,768]{1,0:T(8,128)(2,1)}), bf16[768,768]{1,0:T(8,128)(2,1)}) %reduce-scatter.26.cloned.1.call-update) | async-done | bytes 1179664 | tf_op jit(solution)/shard_map/reduce_scatter | solution.py:254
  (411 shorter events, 481.6 us)
Async XLA Ops:
  7.2 60.8 %copy-start.12 = (bf16[256,768]{1,0:T(8,128)(2,1)S(1)}, bf16[256,768]{1,0:T(8,128)(2,1)}, u32[]{:S(2)}) copy-start(bf16[256,768]{1,0:T(8,128)(2,1)} %param.21) | copy-start | bytes 1179652
  7.2 45.0 %copy-start.49 = (s32[256,2]{0,1:T(2,128)S(1)}, s32[256,2]{0,1:T(2,128)}, u32[]{:S(2)}) copy-start(s32[256,2]{0,1:T(2,128)} %param.23) | copy-start | bytes 6148
  7.2 46.0 %copy-start.37 = (s32[256]{0:T(256)S(1)}, s32[256]{0:T(256)}, u32[]{:S(2)}) copy-start(s32[256]{0:T(256)} %param.22) | copy-start | bytes 3076
  7.2 51.1 %copy-start.61 = (bf16[8,12]{1,0:T(8,128)(2,1)S(1)}, bf16[8,12]{1,0:T(8,128)(2,1)}, u32[]{:S(2)}) copy-start(bf16[8,12]{1,0:T(8,128)(2,1)} %param.30) | copy-start | bytes 580
  7.2 57.9 %copy-start.62 = (s32[1024]{0:T(1024)S(1)}, s32[1024]{0:T(1024)}, u32[]{:S(2)}) copy-start(s32[1024]{0:T(1024)} %param.24) | copy-start | bytes 12292
  7.2 22.6 %all-gather.13.cloned.1.call-start = ((), (), s32[]{:S(2)}) async-start(), calls=%async_computation.15 | async-start | bytes 1474560 | tf_op jit(solution)/shard_map/all_gather | solution.py:82
  8.0 40.9 %all-gather.9.cloned.1.call-start = ((), (), s32[]{:S(2)}) async-start(), calls=%async_computation.13 | async-start | bytes 1474560 | tf_op jit(solution)/shard_map/all_gather | solution.py:83
  8.7 59.3 %all-gather.17.cloned.1.call-start = ((), (), s32[]{:S(2)}) async-start(), calls=%async_computation.17 | async-start | bytes 1474560 | tf_op jit(solution)/shard_map/all_gather | solution.py:81
  9.5 80.2 %all-gather.15.cloned.1.call-start = ((), (), s32[]{:S(2)}) async-start(), calls=%async_computation.16 | async-start | bytes 1966080 | tf_op jit(solution)/shard_map/all_gather | solution.py:118
  21.5 69.8 %copy-start.40 = (f32[768]{0:T(1024)}, f32[768]{0:T(1024)S(1)}, u32[]{:S(2)}) copy-start(f32[768]{0:T(1024)S(1)} %convert_element_type.226) | copy-start | bytes 9220
  23.3 68.1 %copy-start.45 = (f32[256]{0:T(256)}, f32[256]{0:T(256)S(1)}, u32[]{:S(2)}) copy-start(f32[256]{0:T(256)S(1)} %get-tuple-element.1450) | copy-start | bytes 3076
  32.5 284.2 %all-gather.11.cloned.1.call-start = ((), (), s32[]{:S(2)}) async-start(), calls=%async_computation.14 | async-start | bytes 1966080 | tf_op jit(solution)/shard_map/all_gather | solution.py:119
  51.6 502.6 %all-gather.19.cloned.1.call-start = ((), (), s32[]{:S(2)}) async-start(), calls=%async_computation.18 | async-start | bytes 1474560 | tf_op jit(solution)/shard_map/all_gather | solution.py:84
  554.1 30.1 %copy-start.2 = (bf16[1024,768]{0,1:T(8,128)(2,1)}, bf16[1024,768]{0,1:T(8,128)(2,1)S(1)}, u32[]{:S(2)}) copy-start(bf16[1024,768]{0,1:T(8,128)(2,1)S(1)} %get-tuple-element.1897) | copy-start | bytes 4718596
  554.1 30.1 %copy-start.3 = (bf16[256,12,64]{0,2,1:T(8,128)(2,1)}, bf16[256,12,64]{0,2,1:T(8,128)(2,1)S(1)}, u32[]{:S(2)}) copy-start(bf16[256,12,64]{0,2,1:T(8,128)(2,1)S(1)} %get-tuple-element.1899) | copy-start | bytes 1179652
  554.1 30.1 %copy-start.6 = (bf16[1024,768]{0,1:T(8,128)(2,1)}, bf16[1024,768]{0,1:T(8,128)(2,1)S(1)}, u32[]{:S(2)}) copy-start(bf16[1024,768]{0,1:T(8,128)(2,1)S(1)} %get-tuple-element.1900) | copy-start | bytes 4718596
  554.1 80.2 %copy-start.33 = (f32[12,256]{1,0:T(8,128)}, f32[12,256]{1,0:T(8,128)S(1)}, u32[]{:S(2)}) copy-start(f32[12,256]{1,0:T(8,128)S(1)} %get-tuple-element.1938) | copy-start | bytes 36868
  568.7 34.7 %all-to-all-start = ((bf16[8,96,768]{2,1,0:T(8,128)(2,1)}), bf16[8,96,768]{2,1,0:T(8,128)(2,1)}, u32[]{:S(2)}, u32[]{:S(2)}) async-start(bf16[8,96,768]{2,1,0:T(8,128)(2,1)} %bitcast.275), calls=%async_computation | async-start | bytes 2359296 | tf_op jit(solution)/shard_map/all_to_all | solution.py:201
  590.6 12.8 copy-start.28
  603.4 32.8 %all-to-all-start.2 = ((bf16[8,96,768]{2,1,0:T(8,128)(2,1)}), bf16[8,96,768]{2,1,0:T(8,128)(2,1)S(1)}, u32[]{:S(2)}, u32[]{:S(2)}) async-start(bf16[8,96,768]{2,1,0:T(8,128)(2,1)} %bitcast.17), calls=%async_computation.2 | async-start | bytes 2359296 | tf_op jit(solution)/shard_map/all_to_all | solution.py:229
  636.2 11.3 copy-start.27
  656.4 32.5 %all-to-all-start.3 = ((bf16[8,96,768]{2,1,0:T(8,128)(2,1)}), bf16[8,96,768]{2,1,0:T(8,128)(2,1)S(1)}, u32[]{:S(2)}, u32[]{:S(2)}) async-start(bf16[8,96,768]{2,1,0:T(8,128)(2,1)} %bitcast.19), calls=%async_computation.3 | async-start | bytes 2359296 | tf_op jit(solution)/shard_map/all_to_all | solution.py:247
  660.6 31.9 %copy-start.23 = (bf16[256,768]{1,0:T(8,128)(2,1)S(1)}, bf16[256,768]{1,0:T(8,128)(2,1)}, u32[]{:S(2)}) copy-start(bf16[256,768]{1,0:T(8,128)(2,1)} %param.35) | copy-start | bytes 1179652
  660.6 32.9 %copy-start.58 = (s32[512,1]{0,1:T(1,128)S(1)}, s32[512,1]{0,1:T(1,128)}, u32[]{:S(2)}) copy-start(s32[512,1]{0,1:T(1,128)} %compare_select_fusion) | copy-start | bytes 6148
  660.6 32.9 %copy-start.18 = (f32[256,12,64]{0,2,1:T(8,128)S(1)}, f32[256,12,64]{0,2,1:T(8,128)}, u32[]{:S(2)}) copy-start(f32[256,12,64]{0,2,1:T(8,128)} %get-tuple-element.803) | copy-start | bytes 2359300
  688.9 32.3 %all-to-all-start.1 = ((bf16[8,96,768]{2,1,0:T(8,128)(2,1)}), bf16[8,96,768]{2,1,0:T(8,128)(2,1)S(1)}, u32[]{:S(2)}, u32[]{:S(2)}) async-start(bf16[8,96,768]{2,1,0:T(8,128)(2,1)} %bitcast.281), calls=%async_computation.1 | async-start | bytes 2359296 | tf_op jit(solution)/shard_map/all_to_all | solution.py:210
  692.5 555.3 %reduce-scatter.14.cloned.1.call-start = ((), (), s32[]{:S(2)}) async-start(), calls=%async_computation.20 | async-start | bytes 1966080 | tf_op jit(solution)/shard_map/reduce_scatter | solution.py:319
  698.8 27.3 %copy-start.29 = (f32[256,2]{1,0:T(8,128)S(1)}, f32[256,2]{1,0:T(8,128)}, u32[]{:S(2)}) copy-start(f32[256,2]{1,0:T(8,128)} %copy-done.28) | copy-start | bytes 6148
  721.2 10.0 copy-start.50
  721.2 10.0 copy-start.15
  763.7 115.5 %copy-start.7 = (bf16[256,12,64]{0,2,1:T(8,128)(2,1)}, bf16[256,12,64]{0,2,1:T(8,128)(2,1)S(1)}, u32[]{:S(2)}) copy-start(bf16[256,12,64]{0,2,1:T(8,128)(2,1)S(1)} %get-tuple-element.1864) | copy-start | bytes 1179652 | tf_op jit(solution)/shard_map/while
  769.9 104.7 %copy-start = (bf16[512,768]{0,1:T(8,128)(2,1)}, bf16[512,768]{0,1:T(8,128)(2,1)S(1)}, u32[]{:S(2)}) copy-start(bf16[512,768]{0,1:T(8,128)(2,1)S(1)} %get-tuple-element.1697) | copy-start | bytes 2359300 | tf_op jit(solution)/shard_map/while
  986.4 115.4 %copy-start.7 = (bf16[256,12,64]{0,2,1:T(8,128)(2,1)}, bf16[256,12,64]{0,2,1:T(8,128)(2,1)S(1)}, u32[]{:S(2)}) copy-start(bf16[256,12,64]{0,2,1:T(8,128)(2,1)S(1)} %get-tuple-element.1864) | copy-start | bytes 1179652 | tf_op jit(solution)/shard_map/while
  992.6 104.7 %copy-start = (bf16[512,768]{0,1:T(8,128)(2,1)}, bf16[512,768]{0,1:T(8,128)(2,1)S(1)}, u32[]{:S(2)}) copy-start(bf16[512,768]{0,1:T(8,128)(2,1)S(1)} %get-tuple-element.1697) | copy-start | bytes 2359300 | tf_op jit(solution)/shard_map/while
  1221.4 58.0 %reduce-scatter.12.cloned.1.call-start = ((), (), s32[]{:S(2)}) async-start(), calls=%async_computation.19 | async-start | bytes 1966080 | tf_op jit(solution)/shard_map/reduce_scatter | solution.py:313
  1226.1 81.5 %reduce-scatter.22.cloned.1.call-start = ((), (), s32[]{:S(2)}) async-start(), calls=%async_computation.24 | async-start | bytes 1474560 | tf_op jit(solution)/shard_map/reduce_scatter | solution.py:362
  1227.7 54.3 %copy-start.21 = (bf16[256,768]{1,0:T(8,128)(2,1)S(1)}, bf16[256,768]{1,0:T(8,128)(2,1)}, u32[]{:S(2)}) copy-start(bf16[256,768]{1,0:T(8,128)(2,1)} %copy-done.20) | copy-start | bytes 1179652
  1227.7 54.3 %copy-start.48 = (bf16[256,8]{0,1:T(8,128)(2,1)S(1)}, bf16[256,8]{0,1:T(8,128)(2,1)}, u32[]{:S(2)}) copy-start(bf16[256,8]{0,1:T(8,128)(2,1)} %copy-done.47) | copy-start | bytes 12292
  1227.7 108.8 %reduce-scatter.16.cloned.1.call-start = ((), (), s32[]{:S(2)}) async-start(), calls=%async_computation.21 | async-start | bytes 1474560 | tf_op jit(solution)/shard_map/reduce_scatter | solution.py:353
  1229.6 135.3 %reduce-scatter.20.cloned.1.call-start = ((), (), s32[]{:S(2)}) async-start(), calls=%async_computation.23 | async-start | bytes 1474560 | tf_op jit(solution)/shard_map/reduce_scatter | solution.py:359
  1250.5 143.3 %reduce-scatter.18.cloned.1.call-start = ((), (), s32[]{:S(2)}) async-start(), calls=%async_computation.22 | async-start | bytes 1474560 | tf_op jit(solution)/shard_map/reduce_scatter | solution.py:356
  1282.0 134.6 %reduce-scatter.28.cloned.1.call-start = ((), (), s32[]{:S(2)}) async-start(), calls=%async_computation.27 | async-start | bytes 245760
  1283.1 218.7 %all-reduce.16.cloned.1.call-start = ((), (), s32[]{:S(2)}) async-start(), calls=%async_computation.28 | async-start | bytes 2359296 | tf_op jit(solution)/shard_map/psum | solution.py:377
  1393.8 157.5 %reduce-scatter.24.cloned.1.call-start = ((), (), s32[]{:S(2)}) async-start(), calls=%async_computation.25 | async-start | bytes 5898240 | tf_op jit(solution)/shard_map/reduce_scatter | solution.py:251
  1402.6 10.4 copy-start.32
  1402.6 10.4 copy-start.63
  1402.6 198.9 %reduce-scatter.26.cloned.1.call-start = ((), (), s32[]{:S(2)}) async-start(), calls=%async_computation.26 | async-start | bytes 5898240 | tf_op jit(solution)/shard_map/reduce_scatter | solution.py:254
  1411.8 44.1 %copy-start.59 = (f32[256]{0:T(256)S(1)}, f32[256]{0:T(256)}, u32[]{:S(2)}) copy-start(f32[256]{0:T(256)} %get-tuple-element.1449) | copy-start | bytes 3076
  (48 other events, 233.8 us)
Sparse Core Ops, SparseCore 0:
  9.6 20.1 all-gather.12
  31.4 17.4 all-gather.8
  50.4 17.4 all-gather.16
  70.0 19.6 all-gather.14
  91.6 19.6 all-gather.10
  112.8 17.4 all-gather.18
  1221.5 26.2 reduce-scatter.13
  1251.1 28.1 reduce-scatter.11
  1281.9 25.7 reduce-scatter.21
  1310.8 25.7 reduce-scatter.15
  1339.1 25.7 reduce-scatter.19
  1368.1 25.6 reduce-scatter.17
  1396.8 19.7 reduce-scatter.27
  1420.3 81.4 all-reduce.15
  1504.3 46.9 reduce-scatter.23
  1553.7 47.8 reduce-scatter.25
where the time goes:
time: 1640 us; the launch traced here: 1610 us
  local copies, waits for them, and re-layouts  893 us (54%)
  waiting for transfers between devices  388 us (24%)
  matrix products  148 us (9%)
  blocking collectives  56.1 us (3%)
  other arithmetic  55.4 us (3%)
  loops' own time  35.8 us (2%)
  starting transfers between devices  18.3 us (1%)
  between operations  16.9 us (1%)
    rev x6, local copies, waits for them, and re-layouts, band(): repeated.reshape(head_count, row_count, length + 1)[:, :, :col_count]  289 us
    while x64, local copies, waits for them, and re-layouts  177 us
    another operation x12, local copies, waits for them, and re-layouts, band(): jnp.tile(window, (1, row_count))  125 us
    rev x2, local copies, waits for them, and re-layouts, band_grad(): padded = jnp.pad(grad_scores[:, :, ::-1], ((0, 0), (0, 0), (0, row_count)))  62.3 us
    concatenate x6, local copies, waits for them, and re-layouts, band(): jnp.concatenate([jnp.tile(window, (1, row_count)), jnp.zeros((head_count,...  60.5 us
    dot_general x14, matrix products, contract(): lax.dot_general(left_side, right_side, (((left_dim,), (right_dim,)), ((),...  56.1 us
    reduce_scatter x1, waiting for transfers between devices, per_device(): lax.psum_scatter(grad_out_part.astype(jnp.bfloat16), 'fsdp', scatter_dime...  47.3 us
    psum x1, waiting for transfers between devices, per_device(): lax.psum(shards[1].astype(jnp.bfloat16), 'expert').astype(jnp.float32)  44.7 us
  transfers between devices with their start and end apart: 20, of which 18 were waited for; matrix products, arithmetic and copies ran while one was open for 37% of the time, Pallas kernels for 0%

commit v1 on v0

v1 whole, which is shorter than its diff:
```python
import math

import jax
import jax.numpy as jnp
from jax import lax
from jax.experimental import pallas as pl
from jax.experimental.pallas import tpu as pltpu
from jax.sharding import PartitionSpec as P

eps = 1e-06
log2e = math.log2(math.e)
masked_score = -1e30
f32 = jnp.float32
bf16 = jnp.bfloat16
tile = 128
extra_rows = 16


def mm(left_side, right_side):
    return lax.dot_general(
        left_side, right_side, (((1,), (0,)), ((), ())), preferred_element_type=f32
    )


def mm_t(left_side, right_side):
    return lax.dot_general(
        left_side, right_side, (((1,), (1,)), ((), ())), preferred_element_type=f32
    )


def t_mm(left_side, right_side):
    return lax.dot_general(
        left_side, right_side, (((0,), (0,)), ((), ())), preferred_element_type=f32
    )


def swap(value, axis_name, axis_size, bit):
    return lax.ppermute(value, axis_name, [(i, i ^ bit) for i in range(axis_size)])


def params(megabytes=56):
    return pltpu.CompilerParams(vmem_limit_bytes=megabytes << 20)


def cost(flops, moved):
    return pl.CostEstimate(flops=int(flops) >> 8, bytes_accessed=int(moved) >> 8, transcendentals=0)


def shape_of(dims, dtype):
    return jax.ShapeDtypeStruct(dims, dtype)


def whole_spec(dims):
    return pl.BlockSpec(dims, lambda *unused: (0,) * len(dims))


def to_column(row):
    return jnp.broadcast_to(row, (tile, row.shape[1])).T


def route_kernel(capacity, routes_ref, cot_ref, map_ref, back0_ref, back1_ref, out_ref, slot_ref):
    tokens = routes_ref.shape[0]
    slots = map_ref.shape[0]
    experts = slots // capacity
    routes = routes_ref[...]
    first, second = routes[:, 0:1], routes[:, 1:2]
    numbers = lax.broadcasted_iota(jnp.int32, (tokens, experts), 1)
    hot0 = (first == numbers).astype(f32)
    hot1 = (second == numbers).astype(f32)
    rows = lax.broadcasted_iota(jnp.int32, (tokens, tokens), 0)
    cols = lax.broadcasted_iota(jnp.int32, (tokens, tokens), 1)
    before = (cols < rows).astype(f32).astype(bf16)
    earlier = mm(before, (hot0 + hot1).astype(bf16))
    slot0 = jnp.sum(hot0 * earlier, axis=1, keepdims=True)
    slot1 = jnp.sum(hot1 * (earlier + hot0), axis=1, keepdims=True)
    slot_ref[...] = jnp.concatenate([slot0, slot1], axis=1)
    dest0 = first.astype(f32) * capacity + slot0
    dest1 = second.astype(f32) * capacity + slot1
    lane_slot = lax.broadcasted_iota(jnp.int32, (tokens, slots), 1).astype(f32)
    back0_ref[...] = (lane_slot == dest0).astype(f32).astype(bf16)
    back1_ref[...] = (lane_slot == dest1).astype(f32).astype(bf16)
    row0 = jnp.broadcast_to(dest0, (tokens, tile)).T[0:1, :]
    row1 = jnp.broadcast_to(dest1, (tokens, tile)).T[0:1, :]
    row_slot = lax.broadcasted_iota(jnp.int32, (slots, tokens), 0).astype(f32)
    hot = ((row_slot == row0).astype(f32) + (row_slot == row1).astype(f32)).astype(bf16)
    map_ref[...] = hot
    rows = mm(hot, cot_ref[...]).astype(bf16)
    others = back0_ref[...].astype(f32) * second.astype(f32) + back1_ref[...].astype(f32) * first.astype(f32)
    others = jnp.broadcast_to(jnp.sum(others, axis=0, keepdims=True), (extra_rows, slots))
    width = rows.shape[1]
    for expert in range(experts):
        at = expert * capacity
        lanes = pltpu.roll(others, (slots - at) % slots, 1)[:, :tile]
        lanes = jnp.concatenate([lanes, jnp.zeros((extra_rows, width - tile), f32)], axis=1)
        out_ref[expert, :capacity, :] = rows[at : at + capacity, :]
        out_ref[expert, capacity:, :] = lanes.astype(bf16)


def route_call(routes, cotangent, capacity, experts):
    tokens, width = cotangent.shape
    slots = experts * capacity
    return pl.pallas_call(
        lambda *refs: route_kernel(capacity, *refs),
        out_shape=(
            shape_of((slots, tokens), bf16),
            shape_of((tokens, slots), bf16),
            shape_of((tokens, slots), bf16),
            shape_of((experts, capacity + extra_rows, width), bf16),
            shape_of((tokens, 2), f32),
        ),
        compiler_params=params(),
        cost_estimate=cost(2 * slots * tokens * width, 4 * slots * width),
        name="route",
    )(routes, cotangent)


def pack_call(me, weights, tokens_in, seg_row, gains, table, router, small, width):
    shards = weights[0].shape[0]
    tokens = tokens_in.shape[0]
    experts, heads = router.shape[0], table.shape[1]
    used = experts + heads + 3

    def placed(me_ref, rows):
        at = lax.broadcasted_iota(jnp.int32, (rows, width), 1)
        own = lax.broadcasted_iota(jnp.int32, (rows, width), 0) + me_ref[0] * rows
        return (at == own).astype(f32).astype(bf16)

    def kernel(me_ref, wq_ref, wk_ref, wv_ref, x_ref, seg_ref, gain_ref, table_ref, router_ref, out_ref):
        for at, ref in enumerate((wq_ref, wk_ref, wv_ref)):
            out_ref[at * shards : (at + 1) * shards, :] = ref[...]
        out_ref[3 * shards : 3 * shards + tokens, :] = x_ref[...]
        columns = placed(me_ref, shards)
        rows = [
            mm(router_ref[...], columns),
            t_mm(table_ref[...], placed(me_ref, table_ref.shape[0])),
            mm(gain_ref[...], columns),
            jnp.zeros((small - used, width), f32),
            jnp.concatenate([seg_ref[...].astype(f32), jnp.zeros((1, width - tokens), f32)], axis=1),
        ]
        out_ref[3 * shards + tokens :, :] = jnp.concatenate(rows, axis=0).astype(bf16)

    vmem = pl.BlockSpec(memory_space=pltpu.VMEM)
    return pl.pallas_call(
        kernel,
        in_specs=[pl.BlockSpec(memory_space=pltpu.SMEM)] + [vmem] * 8,
        out_shape=shape_of((3 * shards + tokens + small, width), bf16),
        compiler_params=params(),
        cost_estimate=cost(1, 4 * shards * width),
        name="pack",
    )(me, *weights, tokens_in, seg_row, gains, table, router)


def project_call(me, blocks, shards, small, bucket_window, heads, buckets, experts):
    count = len(blocks)
    rows, width = blocks[0].shape
    tokens = rows - 3 * shards - small
    seq = count * tokens
    window = bucket_window.shape[1]

    def kernel(me_ref, *refs):
        block_refs = refs[:count]
        (bucket_ref, q_ref, k_ref, v_ref, normed_ref, tok_ref, wq_ref, wk_ref, wv_ref, small_ref, bias_ref, mask_ref) = refs[count:]
        me_index = me_ref[0]
        totals = jnp.zeros((small, width), f32)
        own_docs = block_refs[0][rows - small :, :].astype(f32)[small - 1 :, :tokens]
        for offset in range(count):
            place = lax.bitwise_xor(me_index, offset)
            row = pl.multiple_of(place * shards, shards)
            for part, full_ref in enumerate((wq_ref, wk_ref, wv_ref)):
                full_ref[pl.ds(row, shards), :] = block_refs[offset][part * shards : (part + 1) * shards, :]
            token_row = pl.multiple_of(place * tokens, tokens)
            tok_ref[pl.ds(token_row, tokens), :] = block_refs[offset][3 * shards : rows - small, :]
            extra = block_refs[offset][rows - small :, :].astype(f32)
            totals = totals + extra
            docs = to_column(extra[small - 1 :, :tokens])
            docs = jnp.concatenate([docs] * (tokens // tile), axis=1)
            mask_ref[pl.ds(token_row, tokens), :] = jnp.where(docs == own_docs, 0.0, masked_score)
        small_ref[...] = totals
        gain = totals[experts + heads : experts + heads + 1, :]
        table = totals[experts : experts + heads, :buckets].astype(bf16)
        numbers = lax.broadcasted_iota(jnp.int32, (buckets, window), 0)
        hot = (numbers == bucket_ref[...]).astype(f32).astype(bf16)
        by_distance = mm(table, hot) * log2e
        by_distance = jnp.where(bucket_ref[...] < 0, masked_score, by_distance)
        for head in range(heads):
            bias_ref[head] = by_distance[head : head + 1, :]

        @pl.loop(0, count)
        def chunk(index):
            rows = pl.ds(pl.multiple_of(index * tokens, tokens), tokens)
            values = tok_ref[rows, :].astype(f32)
            inverse = lax.rsqrt(jnp.mean(values * values, axis=-1, keepdims=True) + eps)
            normed = (values * inverse * gain).astype(bf16)
            normed_ref[rows, :] = normed
            k_ref[rows, :] = mm(normed, wk_ref[...]).astype(bf16)
            v_ref[rows, :] = mm(normed, wv_ref[...]).astype(bf16)

        own = normed_ref[pl.ds(pl.multiple_of(me_index * tokens, tokens), tokens), :]
        q_ref[...] = mm(own, wq_ref[...]).astype(bf16)

    vmem = pl.BlockSpec(memory_space=pltpu.VMEM)
    return pl.pallas_call(
        kernel,
        in_specs=[pl.BlockSpec(memory_space=pltpu.SMEM)] + [vmem] * (count + 1),
        out_shape=(
            shape_of((tokens, width), bf16),
            shape_of((seq, width), bf16),
            shape_of((seq, width), bf16),
            shape_of((seq, width), bf16),
            shape_of((seq, width), bf16),
            shape_of((width, width), bf16),
            shape_of((width, width), bf16),
            shape_of((width, width), bf16),
            shape_of((small, width), f32),
            shape_of((heads, 1, window), f32),
            shape_of((seq, tokens), f32),
        ),
        compiler_params=params(),
        cost_estimate=cost(2 * width * width * (2 * seq + tokens), 20 * seq * width),
        name="project",
    )(me, *blocks, bucket_window)


def skewed(bias_row, window):
    spread = jnp.broadcast_to(bias_row, (tile, window))
    return pltpu.roll(spread, 0, 1, stride=1, stride_axis=0)


def attend_call(queries, keys, values, bias, mask, head_dim):
    tokens, width = queries.shape
    seq = keys.shape[0]
    heads, _, window = bias.shape
    pairs = width // tile
    per_step = heads // pairs
    key_blocks = seq // tile
    scale = head_dim**-0.5 * log2e

    def kernel(q_ref, k_ref, v_ref, bias_ref, mask_ref, ctx_ref, lse_ref, score_ref, prob_ref, skew_ref):
        lane = lax.broadcasted_iota(jnp.int32, (tokens, tile), 1)
        row = lax.broadcasted_iota(jnp.int32, (tile, tokens), 0)
        query = q_ref[...]
        values_t = v_ref[...].T
        result = jnp.zeros((tile, tokens), f32)
        for half in range(per_step):
            mine = jnp.where(lane // head_dim == half, query, jnp.zeros_like(query))
            skew_ref[...] = skewed(bias_ref[half], window)
            top = jnp.full((8, tokens), -3e38, f32)
            for block in range(key_blocks):
                rows = pl.ds(block * tile, tile)
                begin = tile * (key_blocks - block)
                scores = mm_t(k_ref[rows, :], mine) * scale
                scores = scores + (skew_ref[:, begin : begin + tokens] + mask_ref[rows, :])
                score_ref[rows, :] = scores
                top = jnp.maximum(top, jnp.max(scores.reshape(tile // 8, 8, tokens), axis=0))
            top = jnp.max(top, axis=0, keepdims=True)
            total = jnp.zeros((8, tokens), f32)
            for block in range(key_blocks):
                rows = pl.ds(block * tile, tile)
                probs = jnp.exp2(score_ref[rows, :] - top)
                prob_ref[rows, :] = probs.astype(bf16)
                total = total + jnp.sum(probs.reshape(tile // 8, 8, tokens), axis=0)
            total = jnp.sum(total, axis=0, keepdims=True)
            lse_ref[half] = top + jnp.log2(total)
            mixed = mm(values_t, prob_ref[...]) * (1.0 / total)
            result = jnp.where(row // head_dim == half, mixed, result)
        ctx_ref[...] = result.T

    return pl.pallas_call(
        kernel,
        grid=(pairs,),
        in_specs=[
            pl.BlockSpec((tokens, tile), lambda p: (0, p)),
            pl.BlockSpec((seq, tile), lambda p: (0, p)),
            pl.BlockSpec((seq, tile), lambda p: (0, p)),
            pl.BlockSpec((per_step, 1, window), lambda p: (p, 0, 0)),
            pl.BlockSpec((seq, tokens), lambda p: (0, 0)),
        ],
        out_specs=(
            pl.BlockSpec((tokens, tile), lambda p: (0, p)),
            pl.BlockSpec((per_step, 1, tokens), lambda p: (p, 0, 0)),
        ),
        out_shape=(shape_of((tokens, width), f32), shape_of((heads, 1, tokens), f32)),
        scratch_shapes=[
            pltpu.VMEM((seq, tokens), f32),
            pltpu.VMEM((seq, tokens), bf16),
            pltpu.VMEM((tile, window), f32),
        ],
        compiler_params=params(),
        cost_estimate=cost(16 * heads * tokens * seq * tile, 4 * seq * width),
        name="attend",
    )(queries, keys, values, bias, mask)


def unskewed(total):
    window = total.shape[1]
    rows = total.shape[0]
    while rows > 8:
        rows = rows // 2
        total = total[:rows, :] + pltpu.roll(total[rows:, :], window - rows, 1)
    step = 4
    while step:
        moved = pltpu.roll(pltpu.roll(total, 8 - step, 0), window - step, 1)
        total = total + moved
        step = step // 2
    return total[0:1, :]


def attend_back_call(queries, keys, values, bias, mask, lse, context, grad_context, bucket_window, buckets, head_dim, first, pairs):
    tokens, width = queries.shape
    seq = keys.shape[0]
    heads, _, window = bias.shape
    per_step = heads // (width // tile)
    key_blocks = seq // tile
    scale = head_dim**-0.5

    def kernel(
        q_ref, k_ref, v_ref, bias_ref, mask_ref, lse_ref, ctx_ref, grad_ref, bucket_ref,
        dq_ref, dk_ref, dv_ref, table_ref, prob_ref, ds_ref, skew_ref, sum_ref,
    ):
        lane = lax.broadcasted_iota(jnp.int32, (tokens, tile), 1)
        row = lax.broadcasted_iota(jnp.int32, (tile, tokens), 0)
        query = q_ref[...]
        grad = grad_ref[...]
        keys_t = k_ref[...].T
        products = (grad.astype(f32) * ctx_ref[...]).T
        result = jnp.zeros((tile, tokens), f32)
        numbers = lax.broadcasted_iota(jnp.int32, (buckets, window), 0)
        hot = (numbers == bucket_ref[...]).astype(f32)
        mine_q, mine_g = [], []
        for half in range(per_step):
            mine_q.append(jnp.where(lane // head_dim == half, query, jnp.zeros_like(query)))
            mine_g.append(jnp.where(lane // head_dim == half, grad, jnp.zeros_like(grad)))
        for half in range(per_step):
            delta = jnp.sum(
                products[half * head_dim : (half + 1) * head_dim, :], axis=0, keepdims=True
            )
            lse_row = lse_ref[half]
            skew_ref[...] = skewed(bias_ref[half], window)
            sum_ref[...] = jnp.zeros((tile, window), f32)
            cols = slice(half * tokens, (half + 1) * tokens)
            for block in range(key_blocks):
                rows = pl.ds(block * tile, tile)
                begin = tile * (key_blocks - block)
                scores = mm_t(k_ref[rows, :], mine_q[half]) * (scale * log2e)
                scores = scores + (skew_ref[:, begin : begin + tokens] + mask_ref[rows, :])
                probs = jnp.exp2(scores - lse_row)
                grad_probs = mm_t(v_ref[rows, :], mine_g[half])
                grad_scores = (probs * (grad_probs - delta)).astype(bf16)
                prob_ref[rows, cols] = probs.astype(bf16)
                ds_ref[rows, cols] = grad_scores
                sum_ref[:, begin : begin + tokens] += grad_scores.astype(f32)
            grad_q = mm(keys_t, ds_ref[:, cols])
            result = jnp.where(row // head_dim == half, grad_q, result)
            by_distance = unskewed(sum_ref[...])
            table_ref[half] = jnp.sum(hot * by_distance, axis=1, keepdims=True)
        dq_ref[...] = (result * scale).T.astype(bf16)
        dk_ref[...] = (mm(ds_ref[...], jnp.concatenate(mine_q, axis=0)) * scale).astype(bf16)
        dv_ref[...] = mm(prob_ref[...], jnp.concatenate(mine_g, axis=0)).astype(bf16)

    narrow = pl.BlockSpec((tokens, tile), lambda p: (0, p + first))
    tall = pl.BlockSpec((seq, tile), lambda p: (0, p + first))
    narrow_out = pl.BlockSpec((tokens, tile), lambda p: (0, p))
    tall_out = pl.BlockSpec((seq, tile), lambda p: (0, p))
    return pl.pallas_call(
        kernel,
        grid=(pairs,),
        in_specs=[
            narrow,
            tall,
            tall,
            pl.BlockSpec((per_step, 1, window), lambda p: (p + first, 0, 0)),
            pl.BlockSpec((seq, tokens), lambda p: (0, 0)),
            pl.BlockSpec((per_step, 1, tokens), lambda p: (p + first, 0, 0)),
            narrow,
            narrow,
            pl.BlockSpec((1, window), lambda p: (0, 0)),
        ],
        out_specs=(
            narrow_out,
            tall_out,
            tall_out,
            pl.BlockSpec((per_step, buckets, 1), lambda p: (p, 0, 0)),
        ),
        out_shape=(
            shape_of((tokens, pairs * tile), bf16),
            shape_of((seq, pairs * tile), bf16),
            shape_of((seq, pairs * tile), bf16),
            shape_of((pairs * per_step, buckets, 1), f32),
        ),
        scratch_shapes=[
            pltpu.VMEM((seq, per_step * tokens), bf16),
            pltpu.VMEM((seq, per_step * tokens), bf16),
            pltpu.VMEM((tile, window), f32),
            pltpu.VMEM((tile, window), f32),
        ],
        compiler_params=params(),
        cost_estimate=cost(40 * pairs * per_step * tokens * seq * tile, 8 * seq * pairs * tile),
        name="attend_back",
    )(queries, keys, values, bias, mask, lse, context, grad_context, bucket_window)


def chosen_logits(routes, logits):
    numbers = lax.broadcasted_iota(jnp.int32, logits.shape, 1)
    hot0 = routes[:, 0:1] == numbers
    hot1 = routes[:, 1:2] == numbers
    return hot0, hot1


def dispatch_call(me, context, out_blocks, tokens_in, smalls, routes, slot_map, heads):
    tokens, width = tokens_in.shape
    count = len(out_blocks)
    shards = out_blocks[0].shape[0]
    slots = slot_map.shape[0]

    def make(experts):
        def kernel(me_ref, ctx_ref, *refs):
            block_refs = refs[:count]
            (x_ref, small_ref, routes_ref, map_ref, wo_ref, low_ref, res_ref, ffn_ref, gate_ref, rows_ref) = refs[count:]
            for offset in range(count):
                place = lax.bitwise_xor(me_ref[0], offset)
                wo_ref[pl.ds(pl.multiple_of(place * shards, shards), shards), :] = block_refs[offset][...]
            context_low = ctx_ref[...].astype(bf16)
            low_ref[...] = context_low
            residual = x_ref[...].astype(f32) + mm(context_low, wo_ref[...])
            res_ref[...] = residual
            gain = small_ref[experts + heads + 1 : experts + heads + 2, :]
            inverse = lax.rsqrt(jnp.mean(residual * residual, axis=-1, keepdims=True) + eps)
            ffn_low = (residual * inverse * gain).astype(bf16)
            ffn_ref[...] = ffn_low
            rows_ref[...] = mm(map_ref[...], ffn_low).astype(bf16)
            logits = mm_t(ffn_low, small_ref[0:experts, :].astype(bf16))
            hot0, hot1 = chosen_logits(routes_ref[...], logits)
            first = jnp.sum(jnp.where(hot0, logits, 0.0), axis=1, keepdims=True)
            second = jnp.sum(jnp.where(hot1, logits, 0.0), axis=1, keepdims=True)
            top = jnp.maximum(first, second)
            weight0 = jnp.exp(first - top)
            weight1 = jnp.exp(second - top)
            whole = weight0 + weight1
            gate0 = weight0 / whole
            gate1 = weight1 / whole
            gate_ref[...] = jnp.concatenate([gate0, gate1], axis=1)

        return kernel

    def run(experts):
        vmem = pl.BlockSpec(memory_space=pltpu.VMEM)
        return pl.pallas_call(
            make(experts),
            in_specs=[pl.BlockSpec(memory_space=pltpu.SMEM)] + [vmem] * (count + 5),
            out_shape=(
                shape_of((width, width), bf16),
                shape_of((tokens, width), bf16),
                shape_of((tokens, width), f32),
                shape_of((tokens, width), bf16),
                shape_of((tokens, 2), f32),
                shape_of((slots, width), bf16),
            ),
            compiler_params=params(),
            cost_estimate=cost(4 * tokens * width * width, 8 * width * width),
            name="dispatch",
        )(me, context, *out_blocks, tokens_in, smalls, routes, slot_map)

    return run


def expert_call(rows, grads, expert_in, expert_out, experts):
    count, width = rows.shape
    capacity = count // experts
    stride = capacity + extra_rows
    hidden_width = expert_in.shape[1]
    step_width = 512
    chunk_rows = 256
    steps = hidden_width // step_width
    half_root = math.sqrt(0.5)
    density = 1.0 / math.sqrt(2.0 * math.pi)

    def kernel(x_ref, g_ref, in_ref, out_ref, active_ref, gh_ref, made_ref, back_ref, made_sum, back_sum):
        step = pl.program_id(0)

        @pl.when(step == 0)
        def start():
            made_sum[...] = jnp.zeros((count, width), f32)
            back_sum[...] = jnp.zeros((count, width), f32)

        @pl.loop(0, count // chunk_rows)
        def chunk(index):
            at = pl.ds(pl.multiple_of(index * chunk_rows, chunk_rows), chunk_rows)
            hidden = mm(x_ref[at, :], in_ref[...])
            upstream = mm_t(g_ref[at, :], out_ref[...])
            share = 0.5 + 0.5 * lax.erf(hidden * half_root)
            active = (hidden * share).astype(bf16)
            slope = share + hidden * (jnp.exp(hidden * hidden * -0.5) * density)
            grad_hidden = (upstream * slope).astype(bf16)
            active_ref[at, :] = active
            gh_ref[at, :] = grad_hidden
            made_sum[at, :] += mm(active, out_ref[...])
            back_sum[at, :] += mm_t(grad_hidden, in_ref[...])

        @pl.when(step == steps - 1)
        def finish():
            made = made_sum[...].astype(bf16)
            made_ref[...] = made
            products = made.astype(f32) * g_ref[...].astype(f32)
            folded = products[:, :tile]
            for at in range(tile, width, tile):
                folded = folded + products[:, at : at + tile]
            dots = jnp.broadcast_to(jnp.sum(folded.T, axis=0, keepdims=True), (8, count))
            coarse = dots.astype(bf16).astype(f32)
            fine = dots - coarse
            for expert in range(experts):
                at = expert * capacity
                shift = (count - at) % count
                lanes = [pltpu.roll(half, shift, 1)[:, :tile] for half in (coarse, fine)]
                lanes = jnp.concatenate(lanes, axis=0)
                lanes = jnp.concatenate([lanes, jnp.zeros((extra_rows, width - tile), f32)], axis=1)
                back_ref[expert, :capacity, :] = back_sum[at : at + capacity, :].astype(bf16)
                back_ref[expert, capacity:, :] = lanes.astype(bf16)

    full = whole_spec((count, width))
    return pl.pallas_call(
        kernel,
        grid=(steps,),
        in_specs=[
            full,
            full,
            pl.BlockSpec((width, step_width), lambda s: (0, s)),
            pl.BlockSpec((step_width, width), lambda s: (s, 0)),
        ],
        out_specs=(
            pl.BlockSpec((count, step_width), lambda s: (0, s)),
            pl.BlockSpec((count, step_width), lambda s: (0, s)),
            full,
            whole_spec((experts, stride, width)),
        ),
        out_shape=(
            shape_of((count, hidden_width), bf16),
            shape_of((count, hidden_width), bf16),
            shape_of((count, width), bf16),
            shape_of((experts, stride, width), bf16),
        ),
        scratch_shapes=[pltpu.VMEM((count, width), f32), pltpu.VMEM((count, width), f32)],
        compiler_params=params(),
        cost_estimate=cost(8 * count * width * hidden_width, 8 * width * hidden_width),
        name="experts",
    )(rows, grads, expert_in, expert_out)


def offset_place(offsets, step, me_ref):
    offset = offsets[0]
    for at in range(1, len(offsets)):
        offset = jnp.where(step == at, offsets[at], offset)
    return lax.bitwise_xor(me_ref[0], offset)


def gate_column(me_ref, rows_ref, router_ref, others_ref):
    logits = mm_t(router_ref[...].astype(bf16), rows_ref[...])
    numbers = lax.broadcasted_iota(jnp.int32, logits.shape, 0).astype(f32)
    mine = jnp.sum(jnp.where(numbers == me_ref[1].astype(f32), logits, 0.0), axis=0, keepdims=True)
    other = jnp.sum(
        jnp.where(numbers == others_ref[...].astype(f32), logits, 0.0), axis=0, keepdims=True
    )
    return to_column(1.0 / (1.0 + jnp.exp(other - mine)))[:, 0:1]


def expert_grads_call(me, rows_t, rows_in, grads, active, grad_hidden, router, others, offsets):
    width, rows = rows_t.shape
    hidden_width = grad_hidden.shape[1]
    count = len(offsets)
    half = count // 2
    in_rows, out_rows = width // count, hidden_width // count

    def kernel(
        me_ref, xt_ref, rows_ref, g_ref, active_ref, gh_ref, router_ref, others_ref,
        in_give_ref, in_keep_ref, out_give_ref, out_keep_ref, gh_scr, g_scr,
    ):
        step = pl.program_id(0)

        @pl.when(step == 0)
        def start():
            column = gate_column(me_ref, rows_ref, router_ref, others_ref)
            g_scr[...] = (g_ref[...].astype(f32) * column).astype(bf16)
            for at in range(0, hidden_width, width):
                gh_scr[:, at : at + width] = (gh_ref[:, at : at + width].astype(f32) * column).astype(bf16)

        def shard(in_ref, out_ref):
            for at in range(0, hidden_width, width):
                in_ref[0, :, at : at + width] = mm(xt_ref[...], gh_scr[:, at : at + width]).astype(bf16)
            out_ref[0] = t_mm(active_ref[...], g_scr[...]).astype(bf16)

        @pl.when(step < half)
        def first():
            shard(in_give_ref, out_give_ref)

        @pl.when(step >= half)
        def second():
            shard(in_keep_ref, out_keep_ref)

    def give_at(s, me_ref):
        return (jnp.minimum(s, half - 1), 0, 0)

    def keep_at(s, me_ref):
        return (jnp.maximum(s - half, 0), 0, 0)

    return pl.pallas_call(
        kernel,
        grid_spec=pltpu.PrefetchScalarGridSpec(
            num_scalar_prefetch=1,
            grid=(count,),
            in_specs=[
                pl.BlockSpec((in_rows, rows), lambda s, me_ref: (offset_place(offsets, s, me_ref), 0)),
                whole_spec((rows, width)),
                whole_spec((rows, width)),
                pl.BlockSpec((rows, out_rows), lambda s, me_ref: (0, offset_place(offsets, s, me_ref))),
                whole_spec((rows, hidden_width)),
                whole_spec(router.shape),
                whole_spec((1, rows)),
            ],
            out_specs=(
                pl.BlockSpec((1, in_rows, hidden_width), give_at),
                pl.BlockSpec((1, in_rows, hidden_width), keep_at),
                pl.BlockSpec((1, out_rows, width), give_at),
                pl.BlockSpec((1, out_rows, width), keep_at),
            ),
            scratch_shapes=[pltpu.VMEM((rows, hidden_width), bf16), pltpu.VMEM((rows, width), bf16)],
        ),
        out_shape=(
            shape_of((half, in_rows, hidden_width), bf16),
            shape_of((half, in_rows, hidden_width), bf16),
            shape_of((half, out_rows, width), bf16),
            shape_of((half, out_rows, width), bf16),
        ),
        compiler_params=params(),
        cost_estimate=cost(4 * rows * width * hidden_width, 8 * width * hidden_width),
        name="expert_grads",
    )(me, rows_t, rows_in, grads, active, grad_hidden, router, others)


def combine_call(experts, heads, rows, places, gates, routes, cotangent, residual, ffn_low, smalls, w_output):
    tokens, width = cotangent.shape
    stride = rows.shape[0] // experts
    capacity = stride - extra_rows

    def kernel(
        rows_ref, place_ref, gate_ref, routes_ref, cot_ref, res_ref, ffn_ref, small_ref, wo_ref,
        grad_res_ref, branch_ref, ctx_ref, router_ref, gain_ref,
    ):
        gate0, gate1 = gate_ref[:, 0:1], gate_ref[:, 1:2]
        lane_row = lax.broadcasted_iota(jnp.int32, (tokens, stride * experts), 1).astype(f32)
        lane_slot = lax.broadcasted_iota(jnp.int32, (tokens, tile), 1).astype(f32)
        grad_ffn = jnp.zeros((tokens, width), f32)
        grad_gate = []
        for k, gate in enumerate((gate0, gate1)):
            first_row = routes_ref[:, k : k + 1].astype(f32) * stride
            place = place_ref[:, k : k + 1]
            back = (lane_row == first_row + place).astype(f32).astype(bf16)
            grad_ffn = grad_ffn + mm(back, rows_ref[...]) * gate
            coarse = (lane_row == first_row + capacity).astype(f32)
            fine = (lane_row == first_row + (capacity + 8)).astype(f32)
            dots = mm((coarse + fine).astype(bf16), rows_ref[:, :tile])
            grad_gate.append(jnp.sum(jnp.where(lane_slot == place, dots, 0.0), axis=1, keepdims=True))
        grad_gate0, grad_gate1 = grad_gate
        mean_grad = gate0 * grad_gate0 + gate1 * grad_gate1
        chosen0 = gate0 * (grad_gate0 - mean_grad)
        chosen1 = gate1 * (grad_gate1 - mean_grad)
        numbers = lax.broadcasted_iota(jnp.int32, (tokens, experts), 1)
        hot0 = routes_ref[:, 0:1] == numbers
        hot1 = routes_ref[:, 1:2] == numbers
        grad_logits = jnp.where(hot0, chosen0, 0.0) + jnp.where(hot1, chosen1, 0.0)
        grad_logits = grad_logits.astype(bf16)
        router_ref[...] = t_mm(grad_logits, ffn_ref[...])
        grad_ffn = grad_ffn + mm(grad_logits, small_ref[0:experts, :].astype(bf16))
        gain = small_ref[experts + heads + 1 : experts + heads + 2, :]
        residual = res_ref[...]
        inverse = lax.rsqrt(jnp.mean(residual * residual, axis=-1, keepdims=True) + eps)
        scaled = grad_ffn * gain
        inner = jnp.mean(scaled * residual, axis=-1, keepdims=True)
        gain_ref[...] = jnp.sum(grad_ffn * residual * inverse, axis=0, keepdims=True)
        grad_res = cot_ref[...].astype(f32) + inverse * scaled - residual * (inverse * inverse * inverse * inner)
        grad_res_ref[...] = grad_res
        branch = grad_res.astype(bf16)
        branch_ref[...] = branch
        ctx_ref[...] = mm_t(branch, wo_ref[...]).astype(bf16)

    return pl.pallas_call(
        kernel,
        out_shape=(
            shape_of((tokens, width), f32),
            shape_of((tokens, width), bf16),
            shape_of((tokens, width), bf16),
            shape_of((experts, width), f32),
            shape_of((1, width), f32),
        ),
        compiler_params=params(),
        cost_estimate=cost(6 * tokens * width * width, 8 * width * width),
        name="combine",
    )(rows, places, gates, routes, cotangent, residual, ffn_low, smalls, w_output)


def split_rows(full_ref, me_index, count, shards, give_ref, keep_ref):
    for offset in range(count):
        place = lax.bitwise_xor(me_index, offset)
        target = give_ref if offset & 1 else keep_ref
        target[offset // 2, :shards, :] = full_ref[
            pl.ds(pl.multiple_of(place * shards, shards), shards), :
        ].astype(bf16)


def output_grad_call(me, context_low, branch, count):
    tokens, width = branch.shape
    shards = width // count

    def kernel(me_ref, ctx_ref, branch_ref, give_ref, keep_ref, full_ref):
        full_ref[...] = t_mm(ctx_ref[...], branch_ref[...])
        split_rows(full_ref, me_ref[0], count, shards, give_ref, keep_ref)

    vmem = pl.BlockSpec(memory_space=pltpu.VMEM)
    return pl.pallas_call(
        kernel,
        in_specs=[pl.BlockSpec(memory_space=pltpu.SMEM), vmem, vmem],
        out_shape=(shape_of((count // 2, shards, width), bf16),) * 2,
        scratch_shapes=[pltpu.VMEM((width, width), f32)],
        compiler_params=params(),
        cost_estimate=cost(2 * tokens * width * width, 4 * width * width),
        name="output_grad",
    )(me, context_low, branch)


def projection_grad_call(me, dq, dk, dv, normed_t, count):
    tokens, part = dq.shape
    width, seq = normed_t.shape
    shards = width // count

    def kernel(me_ref, dq_ref, dk_ref, dv_ref, normed_ref, give_ref, keep_ref, full_ref):
        own = pl.ds(pl.multiple_of(me_ref[0] * tokens, tokens), tokens)
        full_ref[:, :part] = mm(normed_ref[:, own], dq_ref[...])
        full_ref[:, part : 2 * part] = mm(normed_ref[...], dk_ref[...])
        full_ref[:, 2 * part :] = mm(normed_ref[...], dv_ref[...])
        split_rows(full_ref, me_ref[0], count, shards, give_ref, keep_ref)

    vmem = pl.BlockSpec(memory_space=pltpu.VMEM)
    return pl.pallas_call(
        kernel,
        in_specs=[pl.BlockSpec(memory_space=pltpu.SMEM)] + [vmem] * 4,
        out_shape=(shape_of((count // 2, shards, 3 * part), bf16),) * 2,
        scratch_shapes=[pltpu.VMEM((width, 3 * part), f32)],
        compiler_params=params(),
        cost_estimate=cost(5 * seq * width * part, 10 * seq * width),
        name="projection_grad",
    )(me, dq, dk, dv, normed_t)


def project_back_call(me, first, second, normed_t, sequence, weights, tables, grad_router, grad_gain_ffn, count, small):
    tokens, part = second[0].shape
    width, seq = normed_t.shape
    shards = width // count
    experts = grad_router.shape[0]
    heads, buckets = 2 * tables[0].shape[0], tables[0].shape[1]

    def kernel(
        me_ref, dq1_ref, dk1_ref, dv1_ref, dq2_ref, dk2_ref, dv2_ref, normed_ref, tok_ref, wq_ref, wk_ref, wv_ref,
        table1_ref, table2_ref, router_ref, gain_ffn_ref, give_ref, keep_ref, rows_give_ref, rows_keep_ref, full_ref,
    ):
        own = pl.ds(pl.multiple_of(me_ref[0] * tokens, tokens), tokens)
        full_ref[:, :part] = mm(normed_ref[:, own], dq2_ref[...])
        full_ref[:, part : 2 * part] = mm(normed_ref[...], dk2_ref[...])
        full_ref[:, 2 * part :] = mm(normed_ref[...], dv2_ref[...])
        split_rows(full_ref, me_ref[0], count, shards, give_ref, keep_ref)
        gain = jnp.zeros((1, width), f32)
        for offset in range(count):
            place = lax.bitwise_xor(me_ref[0], offset)
            at = pl.ds(pl.multiple_of(place * tokens, tokens), tokens)
            total = mm_t(dk1_ref[at, :], wk_ref[:, :part]) + mm_t(dk2_ref[at, :], wk_ref[:, part:])
            total = total + mm_t(dv1_ref[at, :], wv_ref[:, :part]) + mm_t(dv2_ref[at, :], wv_ref[:, part:])
            if offset == 0:
                total = total + mm_t(dq1_ref[...], wq_ref[:, :part]) + mm_t(dq2_ref[...], wq_ref[:, part:])
            target = rows_give_ref if offset & 1 else rows_keep_ref
            target[offset // 2] = total.astype(bf16)
            values = tok_ref[at, :].astype(f32)
            inverse = lax.rsqrt(jnp.mean(values * values, axis=-1, keepdims=True) + eps)
            gain = gain + jnp.sum(total * values * inverse, axis=0, keepdims=True)
        wide = jnp.concatenate(
            [router_ref[...], gain, gain_ffn_ref[...], jnp.zeros((small - experts - 2, width), f32)],
            axis=0,
        )
        table = jnp.concatenate([table1_ref[...], table2_ref[...]], axis=0)
        table = jnp.concatenate([table, jnp.zeros((small - heads, buckets), f32)], axis=0)
        extra = jnp.concatenate([table, jnp.zeros((small, 3 * part - width - buckets), f32)], axis=1)
        extra = jnp.concatenate([wide, extra], axis=1).astype(bf16)
        for at in range(count // 2):
            give_ref[at, shards:, :] = extra
            keep_ref[at, shards:, :] = extra

    vmem = pl.BlockSpec(memory_space=pltpu.VMEM)
    return pl.pallas_call(
        kernel,
        in_specs=[pl.BlockSpec(memory_space=pltpu.SMEM)] + [vmem] * 15,
        out_shape=(
            shape_of((count // 2, shards + small, 3 * part), bf16),
            shape_of((count // 2, shards + small, 3 * part), bf16),
            shape_of((count // 2, tokens, width), bf16),
            shape_of((count // 2, tokens, width), bf16),
        ),
        scratch_shapes=[pltpu.VMEM((width, 3 * part), f32)],
        compiler_params=params(),
        cost_estimate=cost(10 * seq * width * width, 10 * seq * width),
        name="project_back",
    )(me, *first, *second, normed_t, sequence, *weights, *tables, grad_router, grad_gain_ffn)


def gather_blocks(value, axis_size):
    blocks = {0: value}
    bit = 2
    while bit < axis_size:
        for offset in sorted(blocks):
            blocks[offset | bit] = swap(blocks[offset], "fsdp", axis_size, bit)
        bit *= 2
    for offset in sorted(blocks):
        blocks[offset | 1] = swap(blocks[offset], "fsdp", axis_size, 1)
    return [blocks[offset] for offset in range(axis_size)]


def scatter_bits(axis_size):
    bits, bit = [1], axis_size // 2
    while bit > 1:
        bits.append(bit)
        bit //= 2
    return [bit for bit in bits if bit < axis_size]


def added(left_side, right_side):
    return left_side.astype(f32) + right_side.astype(f32)


def scatter_sum(given, kept, axis_size, after_cores=None):
    total = added(kept, swap(given, "fsdp", axis_size, 1))
    pieces = {2 * at: total[at] for at in range(axis_size // 2)}
    for bit in scatter_bits(axis_size):
        if bit == 1:
            continue
        left = {}
        for offset in sorted(pieces):
            if offset & bit:
                continue
            leaving = pieces[offset | bit].astype(bf16)
            if after_cores is not None:
                leaving = after_cores(leaving)
            left[offset] = added(pieces[offset], swap(leaving, "fsdp", axis_size, bit))
        pieces = left
    return pieces[0]


def all_sum_expert(value, axis_size, index):
    rows = value.shape[0]
    parts = jnp.pad(value.astype(bf16), ((0, -rows % (axis_size // 2)), (0, 0)))
    bit, bits = 1, []
    while bit < axis_size:
        bits.append(bit)
        bit *= 2
    inner = bits.pop()
    for bit in bits:
        low_half, high_half = jnp.split(parts, 2, axis=0)
        upper = (index & bit) != 0
        keep = jnp.where(upper, high_half, low_half)
        give = jnp.where(upper, low_half, high_half)
        parts = added(keep, swap(give, "expert", axis_size, bit)).astype(bf16)
    parts = added(parts, swap(parts, "expert", axis_size, inner)).astype(bf16)
    for bit in reversed(bits):
        other = swap(parts, "expert", axis_size, bit)
        upper = (index & bit) != 0
        parts = jnp.concatenate(
            [jnp.where(upper, other, parts), jnp.where(upper, parts, other)], axis=0
        )
    return parts[:rows]


def ordered(*values):
    return lax.optimization_barrier(values)


def build(count, expert_ranks):
    def per_device(
        tokens_in,
        seg_ids,
        routes,
        buckets,
        attn_gain,
        w_query,
        w_key,
        w_value,
        w_output,
        bias_table,
        ffn_gain,
        w_router,
        w_in,
        w_out,
        cotangent,
    ):
        tokens, width = tokens_in.shape
        shards, experts = w_router.shape
        bucket_rows, heads = bias_table.shape
        bucket_count = bucket_rows * count
        head_dim = width // heads
        seq = buckets.shape[0]
        top_count = routes.shape[1]
        capacity = 3 * top_count * tokens // (2 * experts)
        slots = experts * capacity
        fsdp_index = lax.axis_index("fsdp")
        expert_index = lax.axis_index("expert")
        me = jnp.stack([fsdp_index, expert_index]).astype(jnp.int32)

        used = experts + heads + 3
        small_rows = -(-used // 16) * 16
        packed = pack_call(
            me, (w_query, w_key, w_value), tokens_in, seg_ids[None, :],
            jnp.stack([attn_gain, ffn_gain]), bias_table, w_router.T, small_rows, width,
        )
        blocks = gather_blocks(packed, count)
        out_blocks = gather_blocks(ordered(w_output, blocks[-2])[0], count)
        routes, blocks[1] = ordered(routes, blocks[1])
        padded_buckets = jnp.concatenate([jnp.full((seq,), -1, jnp.int32), buckets])
        bucket_window = lax.dynamic_slice_in_dim(
            padded_buckets, fsdp_index * tokens, seq + tokens, 0
        )[None, :]

        slot_map, back0, back1, grad_rows_out, places = route_call(routes, cotangent, capacity, experts)
        grad_rows_in = lax.all_to_all(
            grad_rows_out, "expert", split_axis=0, concat_axis=0, tiled=True
        )
        others = grad_rows_in[:, capacity, :capacity].reshape(1, slots)
        grad_rows_in = grad_rows_in[:, :capacity, :].reshape(slots, width)

        (queries, keys, values, normed, sequence, wq, wk, wv, smalls, bias, mask) = project_call(
            me, blocks, shards, small_rows, bucket_window, heads, bucket_count, experts
        )
        queries, grad_rows_in, others = ordered(queries, grad_rows_in, others)
        context, lse = attend_call(queries, keys, values, bias, mask, head_dim)
        wo, context_low, residual, ffn_low, gates, rows_out = dispatch_call(
            me, context, out_blocks, tokens_in, smalls, routes, slot_map, heads
        )(experts)
        rows_in = lax.all_to_all(
            rows_out.reshape(experts, capacity, width),
            "expert",
            split_axis=0,
            concat_axis=0,
            tiled=True,
        ).reshape(slots, width)
        active, grad_hidden, made, row_grads = expert_call(
            rows_in, grad_rows_in, w_in[0], w_out[0], experts
        )
        row_grads_back = lax.all_to_all(
            row_grads, "expert", split_axis=0, concat_axis=0, tiled=True
        ).reshape(-1, width)

        rows_t = rows_in.T
        normed_t = normed.T
        give = [offset for offset in range(count) if offset & 1]
        keep = [offset for offset in range(count) if not offset & 1]
        router = smalls[:experts]
        in_give, in_keep, out_give, out_keep = expert_grads_call(
            me, rows_t, rows_in, grad_rows_in, active, grad_hidden, router, others, give + keep
        )
        in_total = added(in_keep, swap(in_give, "fsdp", count, 1)).astype(bf16)
        out_total = added(out_keep, swap(out_give, "fsdp", count, 1)).astype(bf16)
        row_grads_back, in_total = ordered(row_grads_back, in_total)

        grad_residual, branch, grad_context, grad_router, grad_gain_ffn = combine_call(
            experts, heads, row_grads_back, places, gates, routes, cotangent,
            residual, ffn_low, smalls, wo,
        )
        made_back = lax.all_to_all(
            made.reshape(experts, capacity, width),
            "expert",
            split_axis=0,
            concat_axis=0,
            tiled=True,
        ).reshape(slots, width)
        wo_give, wo_keep = output_grad_call(me, context_low, branch, count)
        grad_context, wo_give, wo_keep = ordered(grad_context, wo_give, wo_keep)

        def far_sum(total, early, late):
            pieces = {2 * at: total[at] for at in range(count // 2)}
            for bit in scatter_bits(count):
                if bit == 1:
                    continue
                left = {}
                for offset in sorted(pieces):
                    if offset & bit:
                        continue
                    leaving = pieces[offset | bit].astype(bf16)
                    if early is not None:
                        leaving = ordered(leaving, early)[0]
                    arrived = swap(leaving, "fsdp", count, bit)
                    if late is not None:
                        arrived = ordered(arrived, late)[0]
                    left[offset] = added(pieces[offset], arrived)
                pieces = left
            return pieces[0]

        pairs = width // tile
        near = pairs // 2
        part1 = attend_back_call(
            queries, keys, values, bias, mask, lse, context, grad_context, bucket_window,
            bucket_count, head_dim, 0, near,
        )
        part2 = attend_back_call(
            queries, keys, values, bias, mask, lse, context, grad_context, bucket_window,
            bucket_count, head_dim, near, pairs - near,
        )
        parts = [part1, part2]
        in_sum = far_sum(in_total, None, part1[0])
        small_grad_rows = -(-max(experts + 2, heads) // 32) * 32
        give1, keep1 = projection_grad_call(me, *parts[0][:3], normed_t, count)
        normed_last, in_sum, give1 = ordered(normed_t, in_sum, give1)
        give2, keep2, rows_give, rows_keep = project_back_call(
            me, parts[0][:3], parts[1][:3], normed_last, sequence, (wq, wk, wv),
            (parts[0][3][:, :, 0], parts[1][3][:, :, 0]), grad_router, grad_gain_ffn, count, small_grad_rows,
        )

        wo_sum = scatter_sum(wo_give, wo_keep, count)
        sum1 = scatter_sum(give1, keep1, count)
        sum2 = scatter_sum(give2, keep2, count)
        grad_shards = [in_sum, far_sum(out_total, sum2, None)]
        chain1 = all_sum_expert(jnp.concatenate([wo_sum, sum1], axis=1), expert_ranks, expert_index)
        chain2 = all_sum_expert(sum2, expert_ranks, expert_index)
        chain1 = chain1.astype(f32)
        chain2 = chain2.astype(f32)
        half_cols = near * tile

        grad_normed = scatter_sum(rows_give, rows_keep, count, lambda value: ordered(value, sum2)[0])
        inputs = tokens_in.astype(f32)
        inverse = lax.rsqrt(jnp.mean(inputs * inputs, axis=-1, keepdims=True) + eps)
        gain_attn = smalls[experts + heads]
        scaled = grad_normed * gain_attn
        inner = jnp.mean(scaled * inputs, axis=-1, keepdims=True)
        grad_tokens = grad_residual + inverse * scaled - inputs * inverse**3 * inner

        made_back = ordered(made_back, part2[0])[0]
        picked0 = mm(back0, made_back)
        picked1 = mm(back1, made_back)
        block_out = (residual + gates[:, 0:1] * picked0 + gates[:, 1:2] * picked1).astype(bf16)

        shards_out = []
        for part in range(3):
            left = chain1[:, width + part * half_cols : width + (part + 1) * half_cols]
            rest = width - half_cols
            right = chain2[:shards, part * rest : (part + 1) * rest]
            shards_out.append(jnp.concatenate([left, right], axis=1))
        shards_out.append(chain1[:, :width])
        small_out = chain2[shards:]
        cols = lax.dynamic_slice_in_dim(small_out[:, :width], fsdp_index * shards, shards, 1)
        table_cols = lax.dynamic_slice_in_dim(
            small_out[:heads, width:], fsdp_index * bucket_rows, bucket_rows, 1
        )
        return (
            block_out,
            grad_tokens,
            cols[experts],
            shards_out[0],
            shards_out[1],
            shards_out[2],
            shards_out[3],
            table_cols.T,
            cols[experts + 1],
            cols[:experts].T,
            grad_shards[0][None],
            grad_shards[1][None],
        )

    return per_device


def solution(mesh):
    return jax.shard_map(
        build(mesh.shape["fsdp"], mesh.shape["expert"]),
        mesh=mesh,
        in_specs=(
            P(("expert", "fsdp"), None),
            P(("expert", "fsdp")),
            P(("expert", "fsdp"), None),
            P(),
            P("fsdp"),
            P("fsdp", None),
            P("fsdp", None),
            P("fsdp", None),
            P("fsdp", None),
            P("fsdp", None),
            P("fsdp"),
            P("fsdp", None),
            P("expert", None, None),
            P("expert", None, None),
            P(("expert", "fsdp"), None),
        ),
        out_specs=(
            P(("expert", "fsdp"), None),
            P(("expert", "fsdp"), None),
            P("fsdp"),
            P("fsdp", None),
            P("fsdp", None),
            P("fsdp", None),
            P("fsdp", None),
            P("fsdp", None),
            P("fsdp"),
            P("fsdp", None),
            P("expert", "fsdp", None),
            P("expert", "fsdp", None),
        ),
        check_vma=False,
    )
```

time: 1640 us -> 327 us (0.20); the launches traced: 1610 us -> 326 us
  local copies, waits for them, and re-layouts: 893 us -> 17.9 us
  waiting for transfers between devices: 388 us -> 90.3 us
  matrix products: 148 us -> 2.84 us
  Pallas kernels: 0 us -> 113 us
  loops' own time: 35.8 us -> 0 us
  other arithmetic: 55.4 us -> 25.2 us
  starting transfers between devices: 18.3 us -> 39.2 us
  blocking collectives: 56.1 us -> 35.7 us
    rev x8 -> x0, local copies, waits for them, and re-layouts: 351 us -> none  [the longest x6 289 us: band(): repeated.reshape(head_count, row_count, length + 1)[:, :, :col_count]]
    reduce_scatter x8 -> x0, waiting for transfers between devices: 247 us -> none  [the longest x1 47.3 us: per_device(): lax.psum_scatter(grad_out_part.astype(jnp.bfloat16), 'fsdp', scatter_dime...]
    while x64 -> x0, local copies, waits for them, and re-layouts: 177 us -> none
    dot_general x37 -> x2, matrix products: 148 us -> 2.84 us  [mm(): lax.dot_general(left_side, right_side, (((1,), (0,)), ((), ())), preferre...]
    another operation x13 -> x3, local copies, waits for them, and re-layouts: 125 us -> 1.98 us  [the longest x2 1.32 us: per_device(): jnp.stack([attn_gain, ffn_gain])]
    pallas_call x0 -> x13, Pallas kernels: none -> 113 us  [the longest x1 23.4 us: expert_call(): pl.pallas_call(kernel, grid=(steps,), in_specs=[full, full, pl.BlockSpec(...]
    ppermute x0 -> x28, waiting for transfers between devices: none -> 78.4 us  [swap(): lax.ppermute(value, axis_name, [(i, i ^ bit) for i in range(axis_size)])]
    concatenate x7 -> x0, local copies, waits for them, and re-layouts: 60.5 us -> none  [the longest x6 60.5 us: band(): jnp.concatenate([jnp.tile(window, (1, row_count)), jnp.zeros((head_count,...]
  transfers between devices with their start and end apart: 20 -> 31, of which waited for: 18 -> 15; matrix products, arithmetic and copies ran while one was open for 37% -> 11% of each run, Pallas kernels for 0% -> 22%
where the time goes in v1:
time: 327 us; the launch traced here: 326 us
  Pallas kernels  113 us (35%)
  waiting for transfers between devices  90.3 us (28%)
  starting transfers between devices  39.2 us (12%)
  blocking collectives  35.7 us (11%)
  other arithmetic  25.2 us (8%)
  local copies, waits for them, and re-layouts  17.9 us (5%)
    ppermute x28, waiting for transfers between devices, swap(): lax.ppermute(value, axis_name, [(i, i ^ bit) for i in range(axis_size)])  78.4 us
    all_to_all x1, blocking collectives, per_device(): lax.all_to_all(rows_out.reshape(experts, capacity, width), 'expert', spli...  35.7 us
    ppermute x28, starting transfers between devices, swap(): lax.ppermute(value, axis_name, [(i, i ^ bit) for i in range(axis_size)])  24.3 us
    pallas_call x1, Pallas kernels, expert_call(): pl.pallas_call(kernel, grid=(steps,), in_specs=[full, full, pl.BlockSpec(...  23.4 us
    pallas_call x2, Pallas kernels, attend_back_call(): pl.pallas_call(kernel, grid=(pairs,), in_specs=[narrow, tall, tall, pl.Bl...  16.7 us
    pallas_call x1, Pallas kernels, expert_grads_call(): pl.pallas_call(kernel, grid_spec=pltpu.PrefetchScalarGridSpec(num_scalar_...  16.3 us
    pallas_call x1, Pallas kernels, project_back_call(): pl.pallas_call(kernel, in_specs=[pl.BlockSpec(memory_space=pltpu.SMEM)] +...  11.6 us
    all_to_all x1, waiting for transfers between devices, per_device(): lax.all_to_all(row_grads, 'expert', split_axis=0, concat_axis=0, tiled=True)  10.3 us
  transfers between devices with their start and end apart: 31, of which 15 were waited for; matrix products, arithmetic and copies ran while one was open for 11% of the time, Pallas kernels for 22%

profile of v1, /device:TPU:0, one launch (start us, length us, event | category | flops | bytes accessed | tf_op | source)
XLA Modules:
  0.0 325.7 jit_solution(16403192842283487610)
XLA Ops:
  3.2 2.6 pack.1.refs_0_
  6.3 2.5 collective-permute-start.1
  10.2 3.5 %route.1 = (bf16[768,256]{1,0:T(8,128)(2,1)}, bf16[256,768]{1,0:T(8,128)(2,1)}, bf16[256,768]{1,0:T(8,128)(2,1)}, bf16[8,112,768]{2,1,0:T(8,128)(2,1)}, f32[256,2]{1,0:T(8,128)}) custom-call(s32[256,2]{1,0:T(8,128)} %copy.33.refs_0_.refs_6_.routes_ref, bf16[256,768]{1,0:T(8,128)(2,1)} %cot_ref.1), custom_call_target="tpu_custom_call" | custom-call | flops 1179648 | bytes 9216 | tf_op jit(solution)/shard_map/route/pallas_call | solution.py:102
  13.6 7.2 %all-to-all-start = ((bf16[8,112,768]{2,1,0:T(8,128)(2,1)}), bf16[8,112,768]{2,1,0:T(8,128)(2,1)S(1)}, u32[]{:S(2)}, u32[]{:S(2)}) async-start(bf16[8,112,768]{2,1,0:T(8,128)(2,1)} %get-tuple-element.86), calls=%async_computation | async-start | bytes 2752512 | tf_op jit(solution)/shard_map/all_to_all | solution.py:926
  20.8 18.1 %collective-permute-done.1.refs_2_ = bf16[864,768]{1,0:T(8,128)(2,1)} collective-permute-done((bf16[864,768]{1,0:T(8,128)(2,1)}, bf16[864,768]{1,0:T(8,128)(2,1)}, u32[]{:S(2)}, u32[]{:S(2)}) %collective-permute-start.1) | collective-permute-done | bytes 1327136 | tf_op jit(solution)/shard_map/ppermute | solution.py:38
  38.9 1.7 collective-permute-start.4
  40.9 7.4 %collective-permute-done.4.refs_2_ = bf16[192,768]{1,0:T(8,128)(2,1)S(1)} collective-permute-done((bf16[192,768]{1,0:T(8,128)(2,1)S(1)}, bf16[192,768]{1,0:T(8,128)(2,1)S(1)}, u32[]{:S(2)}, u32[]{:S(2)}) %collective-permute-start.4) | collective-permute-done | bytes 294944 | tf_op jit(solution)/shard_map/ppermute | solution.py:38
  50.1 10.1 %project.1 = (bf16[256,768]{1,0:T(8,128)(2,1)}, bf16[1024,768]{1,0:T(8,128)(2,1)}, bf16[1024,768]{1,0:T(8,128)(2,1)}, bf16[1024,768]{1,0:T(8,128)(2,1)}, bf16[10...) custom-call(s32[2]{0:T(128)} %pad_add_fusion.me_ref, ...), custom_call_target="tpu_custom_call" | custom-call | flops 10616832 | bytes 61440 | tf_op jit(solution)/shard_map/project/pallas_call | solution.py:202
  62.1 10.2 %attend.1 = (f32[256,768]{1,0:T(8,128)}, f32[12,1,256]{2,1,0:T(1,128)}) custom-call(bf16[256,768]{1,0:T(8,128)(2,1)} %get-tuple-element.87.q_ref, bf16[1024,768]{1,0:T(8,128)(2,1)} %get-tuple-element.88.k_ref, bf16[1024,768]{1,0:T(8,128)(2,1)} %get-tuple-element.89.v_ref, f32[12,1,1280]{2,1,0:T(1,128)} %get-tuple-element.90.bias_ref, ...), custom_call_target="tpu_custom_call" | custom-call | flops 25165824 | bytes 12288 | tf_op jit(solution)/shard_map/attend/pallas_call | solution.py:268
  72.3 4.2 %dispatch.1 = (bf16[768,768]{1,0:T(8,128)(2,1)}, bf16[256,768]{1,0:T(8,128)(2,1)}, f32[256,768]{1,0:T(8,128)}, bf16[256,768]{1,0:T(8,128)(2,1)}, f32[256,2]{1,0:T(8,128)}, /*index=5*/bf16[768,768]{1,0:T(8,128)(2,1)}) custom-call(s32[2]{0:T(128)} %pad_add_fusion.me_ref, f32[256,768]{1,0:T(8,128)} %get-tuple-element.92.ctx_ref, bf16[192,768]{1,0:T(8,128)(2,1)} %refs_0_, ...), custom_call_target="tpu_custom_call" | custom-call | flops 2359296 | bytes 18432 | tf_op jit(solution)/shard_map/dispatch/pallas_call | solution.py:447
  76.5 35.7 %all_to_all.20 = bf16[8,96,768]{2,1,0:T(8,128)(2,1)} all-to-all(bf16[8,96,768]{2,1,0:T(8,128)(2,1)} %bitcast.88), channel_id=1, replica_groups=mesh['expert'=8,'fsdp'=4] {'expert'}, dimensions={0} | all-to-all | bytes 2359296 | tf_op jit(solution)/shard_map/all_to_all | solution.py:940
  112.2 23.4 %experts.1 = (bf16[768,3072]{1,0:T(8,128)(2,1)}, bf16[768,3072]{1,0:T(8,128)(2,1)}, bf16[768,768]{1,0:T(8,128)(2,1)}, bf16[8,112,768]{2,1,0:T(8,128)(2,1)}) custom-call(bf16[768,768]{1,0:T(8,128)(2,1)} %bitcast.74, bf16[768,768]{1,0:T(8,128)(2,1)} %bitcast.79, bf16[768,3072]{1,0:T(8,128)(2,1)} %bitcast.84, bf16[3072,768]{1,0:T(8,128)(2,1)} %bitcast.85), custom_call_target="tpu_custom_call" | custom-call | flops 56623104 | bytes 73728 | tf_op jit(solution)/shard_map/experts/pallas_call | solution.py:520
  135.6 3.9 %all-to-all-start.3 = ((bf16[8,112,768]{2,1,0:T(8,128)(2,1)}), bf16[8,112,768]{2,1,0:T(8,128)(2,1)S(1)}, u32[]{:S(2)}, u32[]{:S(2)}) async-start(bf16[8,112,768]{2,1,0:T(8,128)(2,1)} %get-tuple-element.103), calls=%async_computation.3 | async-start | bytes 2752512 | tf_op jit(solution)/shard_map/all_to_all | solution.py:950
  142.3 16.3 %expert_grads.1 = (bf16[2,192,3072]{2,1,0:T(8,128)(2,1)}, bf16[2,192,3072]{2,1,0:T(8,128)(2,1)}, bf16[2,768,768]{2,1,0:T(8,128)(2,1)}, bf16[2,768,768]{2,1,0:T(8,128)(2,1)}) custom-call(s32[2]{0:T(128)} %pad_add_fusion.me_ref, bf16[768,768]{1,0:T(8,128)(2,1)} %copy.35.xt_ref, bf16[768,768]{1,0:T(8,128)(2,1)} %bitcast.75, bf16[768,768]{1,0:T(8,128)(2,1)} %bitcast.80, ...), custom_call_target="tpu_custom_call" | custom-call | flops 28311552 | bytes 73728 | tf_op jit(solution)/shard_map/expert_grads/pallas_call | solution.py:604
  159.2 1.6 copy.37
  161.8 10.3 %all-to-all-done.3 = bf16[8,112,768]{2,1,0:T(8,128)(2,1)S(1)} async-done(((bf16[8,112,768]{2,1,0:T(8,128)(2,1)}), bf16[8,112,768]{2,1,0:T(8,128)(2,1)S(1)}, u32[]{:S(2)}, u32[]{:S(2)}) %all-to-all-start.3) | async-done | bytes 1376288 | tf_op jit(solution)/shard_map/all_to_all | solution.py:950
  172.1 3.8 %all-to-all-start.2 = ((bf16[8,96,768]{2,1,0:T(8,128)(2,1)}), bf16[8,96,768]{2,1,0:T(8,128)(2,1)S(1)}, u32[]{:S(2)}, u32[]{:S(2)}) async-start(bf16[8,96,768]{2,1,0:T(8,128)(2,1)} %bitcast.87), calls=%async_computation.2 | async-start | bytes 2359296 | tf_op jit(solution)/shard_map/all_to_all | solution.py:970
  175.9 3.3 %add_convert_fusion.1 = bf16[2,192,3072]{2,1,0:T(8,128)(2,1)S(1)} fusion(bf16[2,192,3072]{2,1,0:T(8,128)(2,1)} %collective-permute-done.6, bf16[2,192,3072]{2,1,0:T(8,128)(2,1)} %get-tuple-element.107), kind=kLoop, calls=%fused_computation.1 | loop fusion | flops 4718592 | bytes 7077888 | tf_op jit(solution)/shard_map/convert_element_type | solution.py:962
  179.2 6.6 %combine.1 = (f32[256,768]{1,0:T(8,128)}, bf16[256,768]{1,0:T(8,128)(2,1)}, bf16[256,768]{1,0:T(8,128)(2,1)}, f32[8,768]{1,0:T(8,128)}, f32[1,768]{1,0:T(1,128)}) custom-call(bf16[896,768]{1,0:T(8,128)(2,1)} %bitcast.83, f32[256,2]{1,0:T(8,128)} %get-tuple-element.110.place_ref, f32[256,2]{1,0:T(8,128)} %get-tuple-element.97.gate_ref, ...), custom_call_target="tpu_custom_call" | custom-call | flops 3538944 | bytes 18432 | tf_op jit(solution)/shard_map/combine/pallas_call | solution.py:684
  185.8 2.9 output_grad.1
  189.8 1.5 collective-permute-start.7
  191.3 2.2 add_convert_fusion
  194.6 8.4 %attend_back.2 = (bf16[256,384]{1,0:T(8,128)(2,1)}, bf16[1024,384]{1,0:T(8,128)(2,1)}, bf16[1024,384]{1,0:T(8,128)(2,1)}, f32[6,32,1]{2,1,0:T(8,128)}) custom-call(bf16[256,768]{1,0:T(8,128)(2,1)} %get-tuple-element.87.q_ref, bf16[1024,768]{1,0:T(8,128)(2,1)} %get-tuple-element.88.k_ref, bf16[1024,768]{1,0:T(8,128)(2,1)} %get-tuple-element.89.v_ref, ...), custom_call_target="tpu_custom_call" | custom-call | flops 31457280 | bytes 12288 | tf_op jit(solution)/shard_map/attend_back/pallas_call | solution.py:364
  203.0 1.5 all-to-all-done.2
  204.5 8.3 %attend_back.3 = (bf16[256,384]{1,0:T(8,128)(2,1)}, bf16[1024,384]{1,0:T(8,128)(2,1)}, bf16[1024,384]{1,0:T(8,128)(2,1)}, f32[6,32,1]{2,1,0:T(8,128)}) custom-call(bf16[256,768]{1,0:T(8,128)(2,1)} %get-tuple-element.87.q_ref, bf16[1024,768]{1,0:T(8,128)(2,1)} %get-tuple-element.88.k_ref, bf16[1024,768]{1,0:T(8,128)(2,1)} %get-tuple-element.89.v_ref, ...), custom_call_target="tpu_custom_call" | custom-call | flops 31457280 | bytes 12288 | tf_op jit(solution)/shard_map/attend_back/pallas_call | solution.py:364
  212.8 1.6 reduce.3.table1_ref
  214.4 1.6 reduce.4.table2_ref
  216.0 5.3 %projection_grad.1 = (bf16[2,192,1152]{2,1,0:T(8,128)(2,1)}, bf16[2,192,1152]{2,1,0:T(8,128)(2,1)}) custom-call(s32[2]{0:T(128)} %pad_add_fusion.me_ref, bf16[256,384]{1,0:T(8,128)(2,1)} %get-tuple-element.123.dq_ref.dq1_ref, bf16[1024,384]{1,0:T(8,128)(2,1)} %get-tuple-element.124.dk_ref.dk1_ref, bf16[1024,384]{1,0:T(8,128)(2,1)} %get-tuple-element.125.dv_ref.dv1_ref, ...), custom_call_target="tpu_custom_call" | custom-call | flops 5898240 | bytes 30720 | tf_op jit(solution)/shard_map/projection_grad/pallas_call | solution.py:741
  223.7 3.0 convert_add_fusion.1
  226.7 11.6 %project_back.1 = (bf16[2,224,1152]{2,1,0:T(8,128)(2,1)}, bf16[2,224,1152]{2,1,0:T(8,128)(2,1)}, bf16[2,256,768]{2,1,0:T(8,128)(2,1)}, bf16[2,256,768]{2,1,0:T(8,128)(2,1)}) custom-call(s32[2]{0:T(128)} %pad_add_fusion.me_ref, bf16[256,384]{1,0:T(8,128)(2,1)} %get-tuple-element.123.dq_ref.dq1_ref, bf16[1024,384]{1,0:T(8,128)(2,1)} %get-tuple-element.124.dk_ref.dk1_ref, ...), custom_call_target="tpu_custom_call" | custom-call | flops 23592960 | bytes 30720 | tf_op jit(solution)/shard_map/project_back/pallas_call | solution.py:794
  238.4 1.6 collective-permute-start.18
  240.2 2.4 add_convert_fusion.2
  242.6 5.3 %collective-permute-done.18 = bf16[192,768]{1,0:T(8,128)(2,1)S(1)} collective-permute-done((bf16[192,768]{1,0:T(8,128)(2,1)S(1)}, bf16[192,768]{1,0:T(8,128)(2,1)S(1)}, u32[]{:S(2)}, u32[]{:S(2)}) %collective-permute-start.18) | collective-permute-done | bytes 294944 | tf_op jit(solution)/shard_map/ppermute | solution.py:38
  249.5 1.6 collective-permute-start.20
  252.5 10.0 %collective-permute-done.20 = bf16[192,1152]{1,0:T(8,128)(2,1)S(1)} collective-permute-done((bf16[192,1152]{1,0:T(8,128)(2,1)S(1)}, bf16[192,1152]{1,0:T(8,128)(2,1)S(1)}, u32[]{:S(2)}, u32[]{:S(2)}) %collective-permute-start.20) | collective-permute-done | bytes 442400 | tf_op jit(solution)/shard_map/ppermute | solution.py:38
  264.1 9.1 %collective-permute-done.10 = bf16[224,1152]{1,0:T(8,128)(2,1)S(1)} collective-permute-done((bf16[224,1152]{1,0:T(8,128)(2,1)S(1)}, bf16[224,1152]{1,0:T(8,128)(2,1)S(1)}, u32[]{:S(2)}, u32[]{:S(2)}) %collective-permute-start.10) | collective-permute-done | bytes 516128 | tf_op jit(solution)/shard_map/ppermute | solution.py:38
  273.3 1.6 collective-permute-start.11
  277.5 5.0 %collective-permute-done.12 = bf16[112,1152]{1,0:T(8,128)(2,1)S(1)} collective-permute-done((bf16[112,1152]{1,0:T(8,128)(2,1)S(1)}, bf16[112,1152]{1,0:T(8,128)(2,1)S(1)}, u32[]{:S(2)}, u32[]{:S(2)}) %collective-permute-start.12) | collective-permute-done | bytes 258080 | tf_op jit(solution)/shard_map/ppermute | solution.py:38
  282.8 2.0 collective-permute-start.23
  284.9 4.2 %collective-permute-done.13 = bf16[56,1152]{1,0:T(8,128)(2,1)S(1)} collective-permute-done((bf16[56,1152]{1,0:T(8,128)(2,1)S(1)}, bf16[56,1152]{1,0:T(8,128)(2,1)S(1)}, u32[]{:S(2)}, u32[]{:S(2)}) %collective-permute-start.13) | collective-permute-done | bytes 129056 | tf_op jit(solution)/shard_map/ppermute | solution.py:38
  290.7 7.7 %collective-permute-done.14 = bf16[56,1152]{1,0:T(8,128)(2,1)S(1)} collective-permute-done((bf16[56,1152]{1,0:T(8,128)(2,1)S(1)}, bf16[56,1152]{1,0:T(8,128)(2,1)S(1)}, u32[]{:S(2)}, u32[]{:S(2)}) %collective-permute-start.14) | collective-permute-done | bytes 129056 | tf_op jit(solution)/shard_map/ppermute | solution.py:38
  298.6 2.1 collective-permute-start.24
  300.6 3.9 %collective-permute-done.15 = bf16[56,1152]{1,0:T(8,128)(2,1)S(1)} collective-permute-done((bf16[56,1152]{1,0:T(8,128)(2,1)S(1)}, bf16[56,1152]{1,0:T(8,128)(2,1)S(1)}, u32[]{:S(2)}, u32[]{:S(2)}) %collective-permute-start.15) | collective-permute-done | bytes 129056 | tf_op jit(solution)/shard_map/ppermute | solution.py:38
  304.6 1.5 collective-permute-start.16
  307.3 1.5 collective-permute-start.25
  308.7 5.0 %collective-permute-done.16 = bf16[112,1152]{1,0:T(8,128)(2,1)S(1)} collective-permute-done((bf16[112,1152]{1,0:T(8,128)(2,1)S(1)}, bf16[112,1152]{1,0:T(8,128)(2,1)S(1)}, u32[]{:S(2)}, u32[]{:S(2)}) %collective-permute-start.16) | collective-permute-done | bytes 258080 | tf_op jit(solution)/shard_map/ppermute | solution.py:38
  316.7 2.0 collective-permute-done.25
  322.8 2.9 fusion
  (141 shorter events, 34.9 us)
Async XLA Ops:
  0.6 8.5 %copy-start.21 = (s32[256,2]{0,1:T(2,128)S(1)}, s32[256,2]{0,1:T(2,128)}, u32[]{:S(2)}) copy-start(s32[256,2]{0,1:T(2,128)} %param.17) | copy-start | bytes 6148
  5.8 3.3 %collective-permute-start = (bf16[864,768]{1,0:T(8,128)(2,1)}, bf16[864,768]{1,0:T(8,128)(2,1)S(1)}, u32[]{:S(2)}, u32[]{:S(2)}) collective-permute-start(bf16[864,768]{1,0:T(8,128)(2,1)} %pack.1.refs_0_), channel_id=1, source_target_pairs={{0,1},{1,0},{2,3},{3,2},{4,5},{5,4},{6,7},{7,6},{8,9},{9,8},{10,11... | collective-permute-start | bytes 3981320 | tf_op jit(solution)/shard_map/ppermute | solution.py:38
  6.3 32.6 %collective-permute-start.1 = (bf16[864,768]{1,0:T(8,128)(2,1)}, bf16[864,768]{1,0:T(8,128)(2,1)}, u32[]{:S(2)}, u32[]{:S(2)}) collective-permute-start(bf16[864,768]{1,0:T(8,128)(2,1)} %pack.1.refs_0_), channel_id=1, source_target_pairs={{0,2},{1,3},{2,0},{3,1},{4,6},{5,7},{6,4},{7,5},{8,10},{9,11},{10,... | collective-permute-start | bytes 3981320 | tf_op jit(solution)/shard_map/ppermute | solution.py:38
  9.2 4.5 %copy-start.8 = (bf16[864,768]{1,0:T(8,128)(2,1)}, bf16[864,768]{1,0:T(8,128)(2,1)S(1)}, u32[]{:S(2)}) copy-start(bf16[864,768]{1,0:T(8,128)(2,1)S(1)} %collective-permute-done.refs_1_) | copy-start | bytes 3981316
  10.2 28.7 %copy-start.18 = (bf16[192,768]{1,0:T(8,128)(2,1)S(1)}, bf16[192,768]{1,0:T(8,128)(2,1)}, u32[]{:S(2)}) copy-start(bf16[192,768]{1,0:T(8,128)(2,1)} %refs_0_) | copy-start | bytes 884740
  10.2 38.2 %copy-start.20 = (s32[1024]{0:T(1024)S(1)}, s32[1024]{0:T(1024)}, u32[]{:S(2)}) copy-start(s32[1024]{0:T(1024)} %param.18) | copy-start | bytes 12292
  13.6 46.6 %all-to-all-start = ((bf16[8,112,768]{2,1,0:T(8,128)(2,1)}), bf16[8,112,768]{2,1,0:T(8,128)(2,1)S(1)}, u32[]{:S(2)}, u32[]{:S(2)}) async-start(bf16[8,112,768]{2,1,0:T(8,128)(2,1)} %get-tuple-element.86), calls=%async_computation | async-start | bytes 2752512 | tf_op jit(solution)/shard_map/all_to_all | solution.py:926
  38.9 10.1 %collective-permute-start.2 = (bf16[864,768]{1,0:T(8,128)(2,1)}, bf16[864,768]{1,0:T(8,128)(2,1)S(1)}, u32[]{:S(2)}, u32[]{:S(2)}) collective-permute-start(bf16[864,768]{1,0:T(8,128)(2,1)} %collective-permute-done.1.refs_2_), channel_id=1, source_target_pairs={{0,1},{1,0},{2,3},{3,2},{4,5},{5,4},{6,7},{7,6},{8,9},{9,8},{10,11... | collective-permute-start | bytes 3981320 | tf_op jit(solution)/shard_map/ppermute | solution.py:38
  38.9 9.4 %collective-permute-start.4 = (bf16[192,768]{1,0:T(8,128)(2,1)S(1)}, bf16[192,768]{1,0:T(8,128)(2,1)S(1)}, u32[]{:S(2)}, u32[]{:S(2)}) collective-permute-start(bf16[192,768]{1,0:T(8,128)(2,1)S(1)} %copy-done.18), channel_id=1, source_target_pairs={{0,2},{1,3},{2,0},{3,1},{4,6},{5,7},{6,4},{7,5},{8,10},{9,11},{10,... | collective-permute-start | bytes 884744 | tf_op jit(solution)/shard_map/ppermute | solution.py:38
  40.6 31.6 %collective-permute-start.3 = (bf16[192,768]{1,0:T(8,128)(2,1)S(1)}, bf16[192,768]{1,0:T(8,128)(2,1)}, u32[]{:S(2)}, u32[]{:S(2)}) collective-permute-start(bf16[192,768]{1,0:T(8,128)(2,1)S(1)} %copy-done.18), channel_id=1, source_target_pairs={{0,1},{1,0},{2,3},{3,2},{4,5},{5,4},{6,7},{7,6},{8,9},{9,8},{10,11... | collective-permute-start | bytes 884744 | tf_op jit(solution)/shard_map/ppermute | solution.py:38
  48.3 23.9 %copy-start.19 = (bf16[192,768]{1,0:T(8,128)(2,1)}, bf16[192,768]{1,0:T(8,128)(2,1)S(1)}, u32[]{:S(2)}) copy-start(bf16[192,768]{1,0:T(8,128)(2,1)S(1)} %collective-permute-done.4.refs_2_) | copy-start | bytes 884740
  48.3 24.0 %collective-permute-start.5 = (bf16[192,768]{1,0:T(8,128)(2,1)S(1)}, bf16[192,768]{1,0:T(8,128)(2,1)}, u32[]{:S(2)}, u32[]{:S(2)}) collective-permute-start(bf16[192,768]{1,0:T(8,128)(2,1)S(1)} %collective-permute-done.4.refs_2_), channel_id=1, source_target_pairs={{0,1},{1,0},{2,3},{3,2},{4,5},{5,4},{6,7},{7,6},{8,9},{9,8},{10,11... | collective-permute-start | bytes 884744 | tf_op jit(solution)/shard_map/ppermute | solution.py:38
  135.6 5.3 %copy-start = (bf16[8,96,768]{2,1,0:T(8,128)(2,1)S(1)}, bf16[8,96,768]{2,1,0:T(8,128)(2,1)}, u32[]{:S(2)}) copy-start(bf16[8,96,768]{2,1,0:T(8,128)(2,1)} %all_to_all.20) | copy-start | bytes 3538948
  135.6 36.5 %all-to-all-start.3 = ((bf16[8,112,768]{2,1,0:T(8,128)(2,1)}), bf16[8,112,768]{2,1,0:T(8,128)(2,1)S(1)}, u32[]{:S(2)}, u32[]{:S(2)}) async-start(bf16[8,112,768]{2,1,0:T(8,128)(2,1)} %get-tuple-element.103), calls=%async_computation.3 | async-start | bytes 2752512 | tf_op jit(solution)/shard_map/all_to_all | solution.py:950
  142.3 16.8 %copy-start.7 = (bf16[1024,768]{1,0:T(8,128)(2,1)S(1)}, bf16[1024,768]{1,0:T(8,128)(2,1)}, u32[]{:S(2)}) copy-start(bf16[1024,768]{1,0:T(8,128)(2,1)} %get-tuple-element.128) | copy-start | bytes 4718596
  158.6 17.3 %collective-permute-start.6 = (bf16[2,192,3072]{2,1,0:T(8,128)(2,1)}, bf16[2,192,3072]{2,1,0:T(8,128)(2,1)}, u32[]{:S(2)}, u32[]{:S(2)}) collective-permute-start(bf16[2,192,3072]{2,1,0:T(8,128)(2,1)} %get-tuple-element.108), channel_id=1, source_target_pairs={{0,1},{1,0},{2,3},{3,2},{4,5},{5,4},{6,7},{7,6},{8,9},{9,8},{10,11... | collective-permute-start | bytes 7077896 | tf_op jit(solution)/shard_map/ppermute | solution.py:38
  158.6 32.7 %collective-permute-start.26 = (bf16[2,768,768]{2,1,0:T(8,128)(2,1)}, bf16[2,768,768]{2,1,0:T(8,128)(2,1)}, u32[]{:S(2)}, u32[]{:S(2)}) collective-permute-start(bf16[2,768,768]{2,1,0:T(8,128)(2,1)} %get-tuple-element.152), channel_id=1, source_target_pairs={{0,1},{1,0},{2,3},{3,2},{4,5},{5,4},{6,7},{7,6},{8,9},{9,8},{10,11... | collective-permute-start | bytes 7077896 | tf_op jit(solution)/shard_map/ppermute | solution.py:38
  159.2 2.4 copy-start.10
  172.1 7.1 %copy-start.4 = (bf16[8,112,768]{2,1,0:T(8,128)(2,1)}, bf16[8,112,768]{2,1,0:T(8,128)(2,1)S(1)}, u32[]{:S(2)}) copy-start(bf16[8,112,768]{2,1,0:T(8,128)(2,1)S(1)} %all-to-all-done.3) | copy-start | bytes 4128772
  172.1 32.4 %all-to-all-start.2 = ((bf16[8,96,768]{2,1,0:T(8,128)(2,1)}), bf16[8,96,768]{2,1,0:T(8,128)(2,1)S(1)}, u32[]{:S(2)}, u32[]{:S(2)}) async-start(bf16[8,96,768]{2,1,0:T(8,128)(2,1)} %bitcast.87), calls=%async_computation.2 | async-start | bytes 2359296 | tf_op jit(solution)/shard_map/all_to_all | solution.py:970
  179.2 9.5 %copy-start.1 = (bf16[2,192,3072]{2,1,0:T(8,128)(2,1)}, bf16[2,192,3072]{2,1,0:T(8,128)(2,1)S(1)}, u32[]{:S(2)}) copy-start(bf16[2,192,3072]{2,1,0:T(8,128)(2,1)S(1)} %add_convert_fusion.1) | copy-start | bytes 7077892
  185.8 5.5 %copy-start.6 = (bf16[2,768,768]{2,1,0:T(8,128)(2,1)S(1)}, bf16[2,768,768]{2,1,0:T(8,128)(2,1)}, u32[]{:S(2)}) copy-start(bf16[2,768,768]{2,1,0:T(8,128)(2,1)} %get-tuple-element.151) | copy-start | bytes 7077892
  189.8 33.9 %collective-permute-start.7 = (bf16[192,3072]{1,0:T(8,128)(2,1)}, bf16[192,3072]{1,0:T(8,128)(2,1)}, u32[]{:S(2)}, u32[]{:S(2)}) collective-permute-start(bf16[192,3072]{1,0:T(8,128)(2,1)} %slice_bitcast_fusion.2), channel_id=1, source_target_pairs={{0,2},{1,3},{2,0},{3,1},{4,6},{5,7},{6,4},{7,5},{8,10},{9,11},{10,... | collective-permute-start | bytes 3538952 | tf_op jit(solution)/shard_map/ppermute | solution.py:38
  191.3 30.5 %collective-permute-start.17 = (bf16[2,192,768]{2,1,0:T(8,128)(2,1)}, bf16[2,192,768]{2,1,0:T(8,128)(2,1)}, u32[]{:S(2)}, u32[]{:S(2)}) collective-permute-start(bf16[2,192,768]{2,1,0:T(8,128)(2,1)} %get-tuple-element.147), channel_id=1, source_target_pairs={{0,1},{1,0},{2,3},{3,2},{4,5},{5,4},{6,7},{7,6},{8,9},{9,8},{10,11... | collective-permute-start | bytes 1769480 | tf_op jit(solution)/shard_map/ppermute | solution.py:38
  216.0 5.3 %copy-start.17 = (bf16[256,768]{1,0:T(8,128)(2,1)S(1)}, bf16[256,768]{1,0:T(8,128)(2,1)}, u32[]{:S(2)}) copy-start(bf16[256,768]{1,0:T(8,128)(2,1)} %get-tuple-element.98) | copy-start | bytes 1179652
  226.7 13.5 %copy-start.5 = (f32[256,768]{1,0:T(8,128)S(1)}, f32[256,768]{1,0:T(8,128)}, u32[]{:S(2)}) copy-start(f32[256,768]{1,0:T(8,128)} %get-tuple-element.96.res_ref) | copy-start | bytes 2359300
  238.4 9.7 %collective-permute-start.8 = (bf16[2,256,768]{2,1,0:T(8,128)(2,1)}, bf16[2,256,768]{2,1,0:T(8,128)(2,1)S(1)}, u32[]{:S(2)}, u32[]{:S(2)}) collective-permute-start(bf16[2,256,768]{2,1,0:T(8,128)(2,1)} %get-tuple-element.142), channel_id=1, source_target_pairs={{0,1},{1,0},{2,3},{3,2},{4,5},{5,4},{6,7},{7,6},{8,9},{9,8},{10,11... | collective-permute-start | bytes 2359304 | tf_op jit(solution)/shard_map/ppermute | solution.py:38
  238.4 9.5 %collective-permute-start.18 = (bf16[192,768]{1,0:T(8,128)(2,1)S(1)}, bf16[192,768]{1,0:T(8,128)(2,1)S(1)}, u32[]{:S(2)}, u32[]{:S(2)}) collective-permute-start(bf16[192,768]{1,0:T(8,128)(2,1)S(1)} %fusion.16), channel_id=1, source_target_pairs={{0,2},{1,3},{2,0},{3,1},{4,6},{5,7},{6,4},{7,5},{8,10},{9,11},{10,... | collective-permute-start | bytes 884744 | tf_op jit(solution)/shard_map/ppermute | solution.py:38
  240.0 8.3 %collective-permute-start.19 = (bf16[2,192,1152]{2,1,0:T(8,128)(2,1)}, bf16[2,192,1152]{2,1,0:T(8,128)(2,1)S(1)}, u32[]{:S(2)}, u32[]{:S(2)}) collective-permute-start(bf16[2,192,1152]{2,1,0:T(8,128)(2,1)} %get-tuple-element.149), channel_id=1, source_target_pairs={{0,1},{1,0},{2,3},{3,2},{4,5},{5,4},{6,7},{7,6},{8,9},{9,8},{10,11... | collective-permute-start | bytes 2654216 | tf_op jit(solution)/shard_map/ppermute | solution.py:38
  240.2 7.7 %copy-start.22 = (bf16[2,224,1152]{2,1,0:T(8,128)(2,1)S(1)}, bf16[2,224,1152]{2,1,0:T(8,128)(2,1)}, u32[]{:S(2)}) copy-start(bf16[2,224,1152]{2,1,0:T(8,128)(2,1)} %get-tuple-element.144) | copy-start | bytes 3096580
  240.2 7.8 %copy-start.15 = (bf16[2,256,768]{2,1,0:T(8,128)(2,1)S(1)}, bf16[2,256,768]{2,1,0:T(8,128)(2,1)}, u32[]{:S(2)}) copy-start(bf16[2,256,768]{2,1,0:T(8,128)(2,1)} %get-tuple-element.141) | copy-start | bytes 2359300
  247.9 3.2 collective-permute-start.9
  249.5 13.0 %collective-permute-start.20 = (bf16[192,1152]{1,0:T(8,128)(2,1)S(1)}, bf16[192,1152]{1,0:T(8,128)(2,1)S(1)}, u32[]{:S(2)}, u32[]{:S(2)}) collective-permute-start(bf16[192,1152]{1,0:T(8,128)(2,1)S(1)} %fusion.13), channel_id=1, source_target_pairs={{0,2},{1,3},{2,0},{3,1},{4,6},{5,7},{6,4},{7,5},{8,10},{9,11},{10,... | collective-permute-start | bytes 1327112 | tf_op jit(solution)/shard_map/ppermute | solution.py:38
  251.4 21.8 %collective-permute-start.10 = (bf16[224,1152]{1,0:T(8,128)(2,1)S(1)}, bf16[224,1152]{1,0:T(8,128)(2,1)S(1)}, u32[]{:S(2)}, u32[]{:S(2)}) collective-permute-start(bf16[224,1152]{1,0:T(8,128)(2,1)S(1)} %fusion.12), channel_id=1, source_target_pairs={{0,2},{1,3},{2,0},{3,1},{4,6},{5,7},{6,4},{7,5},{8,10},{9,11},{10,... | collective-permute-start | bytes 1548296 | tf_op jit(solution)/shard_map/ppermute | solution.py:38
  262.7 14.1 %collective-permute-start.21 = (bf16[96,1920]{1,0:T(8,128)(2,1)S(1)}, bf16[96,1920]{1,0:T(8,128)(2,1)S(1)}, u32[]{:S(2)}, u32[]{:S(2)}) collective-permute-start(bf16[96,1920]{1,0:T(8,128)(2,1)S(1)} %broadcast_select_fusion.2), channel_id=1, source_target_pairs={{0,4},{4,0},{8,12},{12,8},{16,20},{20,16},{24,28},{28,24},{1,5},{5... | collective-permute-start | bytes 1105928 | tf_op jit(solution)/shard_map/ppermute | solution.py:38
  273.3 15.9 %collective-permute-start.11 = (bf16[256,768]{1,0:T(8,128)(2,1)S(1)}, bf16[256,768]{1,0:T(8,128)(2,1)S(1)}, u32[]{:S(2)}, u32[]{:S(2)}) collective-permute-start(bf16[256,768]{1,0:T(8,128)(2,1)S(1)} %fusion.14), channel_id=1, source_target_pairs={{0,2},{1,3},{2,0},{3,1},{4,6},{5,7},{6,4},{7,5},{8,10},{9,11},{10,... | collective-permute-start | bytes 1179656 | tf_op jit(solution)/shard_map/ppermute | solution.py:38
  274.9 7.6 %collective-permute-start.12 = (bf16[112,1152]{1,0:T(8,128)(2,1)S(1)}, bf16[112,1152]{1,0:T(8,128)(2,1)S(1)}, u32[]{:S(2)}, u32[]{:S(2)}) collective-permute-start(bf16[112,1152]{1,0:T(8,128)(2,1)S(1)} %broadcast_select_fusion.5), channel_id=1, source_target_pairs={{0,4},{4,0},{8,12},{12,8},{16,20},{20,16},{24,28},{28,24},{1,5},{5... | collective-permute-start | bytes 774152 | tf_op jit(solution)/shard_map/ppermute | solution.py:38
  276.3 46.5 %collective-permute-start.27 = (bf16[768,768]{1,0:T(8,128)(2,1)}, bf16[768,768]{1,0:T(8,128)(2,1)}, u32[]{:S(2)}, u32[]{:S(2)}) collective-permute-start(bf16[768,768]{1,0:T(8,128)(2,1)} %slice_bitcast_fusion), channel_id=1, source_target_pairs={{0,2},{1,3},{2,0},{3,1},{4,6},{5,7},{6,4},{7,5},{8,10},{9,11},{10,... | collective-permute-start | bytes 3538952 | tf_op jit(solution)/shard_map/ppermute | solution.py:38
  277.0 12.2 %copy-start.3 = (bf16[256,768]{1,0:T(8,128)(2,1)S(1)}, bf16[256,768]{1,0:T(8,128)(2,1)}, u32[]{:S(2)}) copy-start(bf16[256,768]{1,0:T(8,128)(2,1)} %refs_4_.1) | copy-start | bytes 1179652
  277.0 5.7 %collective-permute-start.22 = (bf16[48,1920]{1,0:T(8,128)(2,1)S(1)}, bf16[48,1920]{1,0:T(8,128)(2,1)S(1)}, u32[]{:S(2)}, u32[]{:S(2)}) collective-permute-start(bf16[48,1920]{1,0:T(8,128)(2,1)S(1)} %broadcast_select_fusion.8), channel_id=1, source_target_pairs={{0,8},{4,12},{8,0},{12,4},{16,24},{20,28},{24,16},{28,20},{1,9},{5... | collective-permute-start | bytes 552968 | tf_op jit(solution)/shard_map/ppermute | solution.py:38
  282.6 6.9 %copy-start.14 = (f32[256,768]{1,0:T(8,128)S(1)}, f32[256,768]{1,0:T(8,128)}, u32[]{:S(2)}) copy-start(f32[256,768]{1,0:T(8,128)} %get-tuple-element.122) | copy-start | bytes 2359300
  282.7 6.4 %collective-permute-start.13 = (bf16[56,1152]{1,0:T(8,128)(2,1)S(1)}, bf16[56,1152]{1,0:T(8,128)(2,1)S(1)}, u32[]{:S(2)}, u32[]{:S(2)}) collective-permute-start(bf16[56,1152]{1,0:T(8,128)(2,1)S(1)} %broadcast_select_fusion.11), channel_id=1, source_target_pairs={{0,8},{4,12},{8,0},{12,4},{16,24},{20,28},{24,16},{28,20},{1,9},{5... | collective-permute-start | bytes 387080 | tf_op jit(solution)/shard_map/ppermute | solution.py:38
  282.8 15.7 %collective-permute-start.23 = (bf16[48,1920]{1,0:T(8,128)(2,1)S(1)}, bf16[48,1920]{1,0:T(8,128)(2,1)S(1)}, u32[]{:S(2)}, u32[]{:S(2)}) collective-permute-start(bf16[48,1920]{1,0:T(8,128)(2,1)S(1)} %add_convert_fusion.6), channel_id=1, source_target_pairs={{0,16},{4,20},{8,24},{12,28},{16,0},{20,4},{24,8},{28,12},{1,17},{... | collective-permute-start | bytes 552968 | tf_op jit(solution)/shard_map/ppermute | solution.py:38
  289.1 9.3 %collective-permute-start.14 = (bf16[56,1152]{1,0:T(8,128)(2,1)S(1)}, bf16[56,1152]{1,0:T(8,128)(2,1)S(1)}, u32[]{:S(2)}, u32[]{:S(2)}) collective-permute-start(bf16[56,1152]{1,0:T(8,128)(2,1)S(1)} %add_convert_fusion.8), channel_id=1, source_target_pairs={{0,16},{4,20},{8,24},{12,28},{16,0},{20,4},{24,8},{28,12},{1,17},{... | collective-permute-start | bytes 387080 | tf_op jit(solution)/shard_map/ppermute | solution.py:38
  298.4 6.1 %collective-permute-start.15 = (bf16[56,1152]{1,0:T(8,128)(2,1)S(1)}, bf16[56,1152]{1,0:T(8,128)(2,1)S(1)}, u32[]{:S(2)}, u32[]{:S(2)}) collective-permute-start(bf16[56,1152]{1,0:T(8,128)(2,1)S(1)} %add_convert_fusion.7), channel_id=1, source_target_pairs={{0,8},{4,12},{8,0},{12,4},{16,24},{20,28},{24,16},{28,20},{1,9},{5... | collective-permute-start | bytes 387080 | tf_op jit(solution)/shard_map/ppermute | solution.py:38
  298.6 7.9 %collective-permute-start.24 = (bf16[48,1920]{1,0:T(8,128)(2,1)S(1)}, bf16[48,1920]{1,0:T(8,128)(2,1)S(1)}, u32[]{:S(2)}, u32[]{:S(2)}) collective-permute-start(bf16[48,1920]{1,0:T(8,128)(2,1)S(1)} %add_convert_fusion.5), channel_id=1, source_target_pairs={{0,8},{4,12},{8,0},{12,4},{16,24},{20,28},{24,16},{28,20},{1,9},{5... | collective-permute-start | bytes 552968 | tf_op jit(solution)/shard_map/ppermute | solution.py:38
  304.6 9.2 %collective-permute-start.16 = (bf16[112,1152]{1,0:T(8,128)(2,1)S(1)}, bf16[112,1152]{1,0:T(8,128)(2,1)S(1)}, u32[]{:S(2)}, u32[]{:S(2)}) collective-permute-start(bf16[112,1152]{1,0:T(8,128)(2,1)S(1)} %pad_maximum_fusion.6), channel_id=1, source_target_pairs={{0,4},{4,0},{8,12},{12,8},{16,20},{20,16},{24,28},{28,24},{1,5},{5... | collective-permute-start | bytes 774152 | tf_op jit(solution)/shard_map/ppermute | solution.py:38
  307.3 11.4 %collective-permute-start.25 = (bf16[96,1920]{1,0:T(8,128)(2,1)}, bf16[96,1920]{1,0:T(8,128)(2,1)}, u32[]{:S(2)}, u32[]{:S(2)}) collective-permute-start(bf16[96,1920]{1,0:T(8,128)(2,1)} %pad_maximum_fusion.4), channel_id=1, source_target_pairs={{0,4},{4,0},{8,12},{12,8},{16,20},{20,16},{24,28},{28,24},{1,5},{5... | collective-permute-start | bytes 1105928 | tf_op jit(solution)/shard_map/ppermute | solution.py:38
  (6 other events, 8.1 us)

commit v2 on v1

--- a/solution.py
+++ b/solution.py
@@ -352,7 +352,8 @@
             grad_q = mm(keys_t, ds_ref[:, cols])
             result = jnp.where(row // head_dim == half, grad_q, result)
             by_distance = unskewed(sum_ref[...])
-            table_ref[half] = jnp.sum(hot * by_distance, axis=1, keepdims=True)
+            column = jnp.sum(hot * by_distance, axis=1, keepdims=True)
+            table_ref[half] = jnp.broadcast_to(column, (buckets, tile)).T[0:1, :]
         dq_ref[...] = (result * scale).T.astype(bf16)
         dk_ref[...] = (mm(ds_ref[...], jnp.concatenate(mine_q, axis=0)) * scale).astype(bf16)
         dv_ref[...] = mm(prob_ref[...], jnp.concatenate(mine_g, axis=0)).astype(bf16)
@@ -379,13 +380,13 @@
             narrow_out,
             tall_out,
             tall_out,
-            pl.BlockSpec((per_step, buckets, 1), lambda p: (p, 0, 0)),
+            pl.BlockSpec((per_step, 1, buckets), lambda p: (p, 0, 0)),
         ),
         out_shape=(
             shape_of((tokens, pairs * tile), bf16),
             shape_of((seq, pairs * tile), bf16),
             shape_of((seq, pairs * tile), bf16),
-            shape_of((pairs * per_step, buckets, 1), f32),
+            shape_of((pairs * per_step, 1, buckets), f32),
         ),
         scratch_shapes=[
             pltpu.VMEM((seq, per_step * tokens), bf16),
@@ -637,7 +638,7 @@
 
 def combine_call(experts, heads, rows, places, gates, routes, cotangent, residual, ffn_low, smalls, w_output):
     tokens, width = cotangent.shape
-    stride = rows.shape[0] // experts
+    stride = rows.shape[1]
     capacity = stride - extra_rows
 
     def kernel(
@@ -646,6 +647,7 @@
     ):
         gate0, gate1 = gate_ref[:, 0:1], gate_ref[:, 1:2]
         lane_row = lax.broadcasted_iota(jnp.int32, (tokens, stride * experts), 1).astype(f32)
+        rows = rows_ref[...].reshape(stride * experts, width)
         lane_slot = lax.broadcasted_iota(jnp.int32, (tokens, tile), 1).astype(f32)
         grad_ffn = jnp.zeros((tokens, width), f32)
         grad_gate = []
@@ -653,10 +655,10 @@
             first_row = routes_ref[:, k : k + 1].astype(f32) * stride
             place = place_ref[:, k : k + 1]
             back = (lane_row == first_row + place).astype(f32).astype(bf16)
-            grad_ffn = grad_ffn + mm(back, rows_ref[...]) * gate
+            grad_ffn = grad_ffn + mm(back, rows) * gate
             coarse = (lane_row == first_row + capacity).astype(f32)
             fine = (lane_row == first_row + (capacity + 8)).astype(f32)
-            dots = mm((coarse + fine).astype(bf16), rows_ref[:, :tile])
+            dots = mm((coarse + fine).astype(bf16), rows[:, :tile])
             grad_gate.append(jnp.sum(jnp.where(lane_slot == place, dots, 0.0), axis=1, keepdims=True))
         grad_gate0, grad_gate1 = grad_gate
         mean_grad = gate0 * grad_gate0 + gate1 * grad_gate1
@@ -696,76 +698,121 @@
     )(rows, places, gates, routes, cotangent, residual, ffn_low, smalls, w_output)
 
 
-def split_rows(full_ref, me_index, count, shards, give_ref, keep_ref):
+def split_rows(full_ref, me_index, count, shards, main, give_ref, keep_ref):
     for offset in range(count):
         place = lax.bitwise_xor(me_index, offset)
         target = give_ref if offset & 1 else keep_ref
-        target[offset // 2, :shards, :] = full_ref[
+        target[offset // 2, :, :main] = full_ref[
             pl.ds(pl.multiple_of(place * shards, shards), shards), :
         ].astype(bf16)
 
 
-def output_grad_call(me, context_low, branch, count):
-    tokens, width = branch.shape
+def small_tiles(pieces, rows, shards):
+    per_tile = shards // rows
+    return -(-pieces // per_tile), per_tile
+
+
+def first_grads_call(me, dq, dk, dv, normed_t, context_low, branch, grad_router, grad_gain, table, count):
+    tokens, part = dq.shape
+    width, seq = normed_t.shape
     shards = width // count
-
-    def kernel(me_ref, ctx_ref, branch_ref, give_ref, keep_ref, full_ref):
-        full_ref[...] = t_mm(ctx_ref[...], branch_ref[...])
-        split_rows(full_ref, me_ref[0], count, shards, give_ref, keep_ref)
+    experts = grad_router.shape[0]
+    heads, _, buckets = table.shape
+    piece_rows = -(-(experts + 1) // 16) * 16
+    pieces = width // tile + 1
+    tiles, per_tile = small_tiles(pieces, piece_rows, shards)
+    main = width + 3 * part
+
+    def kernel(
+        me_ref, dq_ref, dk_ref, dv_ref, normed_ref, ctx_ref, branch_ref, router_ref, gain_ref, table_ref,
+        give_ref, keep_ref, full_ref,
+    ):
+        own = pl.ds(pl.multiple_of(me_ref[0] * tokens, tokens), tokens)
+        full_ref[:, :width] = t_mm(ctx_ref[...], branch_ref[...])
+        full_ref[:, width : width + part] = mm(normed_ref[:, own], dq_ref[...])
+        full_ref[:, width + part : width + 2 * part] = mm(normed_ref[...], dk_ref[...])
+        full_ref[:, width + 2 * part :] = mm(normed_ref[...], dv_ref[...])
+        split_rows(full_ref, me_ref[0], count, shards, main, give_ref, keep_ref)
+        small = jnp.concatenate(
+            [router_ref[...], gain_ref[...], jnp.zeros((piece_rows - experts - 1, width), f32)], axis=0
+        )
+        rows = [table_ref[head] for head in range(heads)]
+        rows = jnp.concatenate(rows + [jnp.zeros((piece_rows - heads, buckets), f32)], axis=0)
+        rows = jnp.concatenate([rows, jnp.zeros((piece_rows, tile - buckets), f32)], axis=1)
+        blocks = [small[:, at : at + tile] for at in range(0, width, tile)] + [rows]
+        blocks = [block.astype(bf16) for block in blocks]
+        for target in (give_ref, keep_ref):
+            for at in range(count // 2):
+                target[at, :, main:] = jnp.zeros((shards, tiles * tile), bf16)
+                for index, block in enumerate(blocks):
+                    row = index % per_tile * piece_rows
+                    col = main + index // per_tile * tile
+                    target[at, row : row + piece_rows, col : col + tile] = block
 
     vmem = pl.BlockSpec(memory_space=pltpu.VMEM)
     return pl.pallas_call(
         kernel,
-        in_specs=[pl.BlockSpec(memory_space=pltpu.SMEM), vmem, vmem],
-        out_shape=(shape_of((count // 2, shards, width), bf16),) * 2,
-        scratch_shapes=[pltpu.VMEM((width, width), f32)],
+        in_specs=[pl.BlockSpec(memory_space=pltpu.SMEM)] + [vmem] * 9,
+        out_shape=(shape_of((count // 2, shards, main + tiles * tile), bf16),) * 2,
+        scratch_shapes=[pltpu.VMEM((width, main), f32)],
         compiler_params=params(),
-        cost_estimate=cost(2 * tokens * width * width, 4 * width * width),
-        name="output_grad",
-    )(me, context_low, branch)
-
-
-def projection_grad_call(me, dq, dk, dv, normed_t, count):
+        cost_estimate=cost(5 * seq * width * part, 10 * seq * width),
+        name="first_grads",
+    )(me, dq, dk, dv, normed_t, context_low, branch, grad_router, grad_gain, table)
+
+
+def first_smalls(columns, experts, heads, buckets, width, shards):
+    piece_rows = -(-(experts + 1) // 16) * 16
+    pieces = width // tile + 1
+    _, per_tile = small_tiles(pieces, piece_rows, shards)
+    found = []
+    for index in range(pieces):
+        row, col = index % per_tile * piece_rows, index // per_tile * tile
+        found.append(columns[row : row + piece_rows, col : col + tile])
+    wide = jnp.concatenate(found[:-1], axis=1)
+    return wide[:experts], wide[experts], found[-1][:heads, :buckets]
+
+
+def second_grads_call(me, dq, dk, dv, normed_t, table, count):
     tokens, part = dq.shape
     width, seq = normed_t.shape
     shards = width // count
-
-    def kernel(me_ref, dq_ref, dk_ref, dv_ref, normed_ref, give_ref, keep_ref, full_ref):
+    heads, _, buckets = table.shape
+    main = 3 * part
+
+    def kernel(me_ref, dq_ref, dk_ref, dv_ref, normed_ref, table_ref, give_ref, keep_ref, full_ref):
         own = pl.ds(pl.multiple_of(me_ref[0] * tokens, tokens), tokens)
         full_ref[:, :part] = mm(normed_ref[:, own], dq_ref[...])
         full_ref[:, part : 2 * part] = mm(normed_ref[...], dk_ref[...])
         full_ref[:, 2 * part :] = mm(normed_ref[...], dv_ref[...])
-        split_rows(full_ref, me_ref[0], count, shards, give_ref, keep_ref)
+        split_rows(full_ref, me_ref[0], count, shards, main, give_ref, keep_ref)
+        rows = [table_ref[head] for head in range(heads)]
+        rows = jnp.concatenate(rows + [jnp.zeros((16 - heads, buckets), f32)], axis=0)
+        rows = jnp.concatenate([rows, jnp.zeros((16, tile - buckets), f32)], axis=1).astype(bf16)
+        for target in (give_ref, keep_ref):
+            for at in range(count // 2):
+                target[at, :, main:] = jnp.zeros((shards, tile), bf16)
+                target[at, :16, main:] = rows
 
     vmem = pl.BlockSpec(memory_space=pltpu.VMEM)
     return pl.pallas_call(
         kernel,
-        in_specs=[pl.BlockSpec(memory_space=pltpu.SMEM)] + [vmem] * 4,
-        out_shape=(shape_of((count // 2, shards, 3 * part), bf16),) * 2,
-        scratch_shapes=[pltpu.VMEM((width, 3 * part), f32)],
+        in_specs=[pl.BlockSpec(memory_space=pltpu.SMEM)] + [vmem] * 5,
+        out_shape=(shape_of((count // 2, shards, main + tile), bf16),) * 2,
+        scratch_shapes=[pltpu.VMEM((width, main), f32)],
         compiler_params=params(),
         cost_estimate=cost(5 * seq * width * part, 10 * seq * width),
-        name="projection_grad",
-    )(me, dq, dk, dv, normed_t)
-
-
-def project_back_call(me, first, second, normed_t, sequence, weights, tables, grad_router, grad_gain_ffn, count, small):
-    tokens, part = second[0].shape
-    width, seq = normed_t.shape
-    shards = width // count
-    experts = grad_router.shape[0]
-    heads, buckets = 2 * tables[0].shape[0], tables[0].shape[1]
+        name="second_grads",
+    )(me, dq, dk, dv, normed_t, table)
+
+
+def rows_back_call(me, first, second, weights, count):
+    tokens, part = first[0].shape
+    width = weights[0].shape[0]
 
     def kernel(
-        me_ref, dq1_ref, dk1_ref, dv1_ref, dq2_ref, dk2_ref, dv2_ref, normed_ref, tok_ref, wq_ref, wk_ref, wv_ref,
-        table1_ref, table2_ref, router_ref, gain_ffn_ref, give_ref, keep_ref, rows_give_ref, rows_keep_ref, full_ref,
+        me_ref, dq1_ref, dk1_ref, dv1_ref, dq2_ref, dk2_ref, dv2_ref, wq_ref, wk_ref, wv_ref, give_ref, keep_ref,
     ):
-        own = pl.ds(pl.multiple_of(me_ref[0] * tokens, tokens), tokens)
-        full_ref[:, :part] = mm(normed_ref[:, own], dq2_ref[...])
-        full_ref[:, part : 2 * part] = mm(normed_ref[...], dk2_ref[...])
-        full_ref[:, 2 * part :] = mm(normed_ref[...], dv2_ref[...])
-        split_rows(full_ref, me_ref[0], count, shards, give_ref, keep_ref)
-        gain = jnp.zeros((1, width), f32)
         for offset in range(count):
             place = lax.bitwise_xor(me_ref[0], offset)
             at = pl.ds(pl.multiple_of(place * tokens, tokens), tokens)
@@ -773,38 +820,44 @@
             total = total + mm_t(dv1_ref[at, :], wv_ref[:, :part]) + mm_t(dv2_ref[at, :], wv_ref[:, part:])
             if offset == 0:
                 total = total + mm_t(dq1_ref[...], wq_ref[:, :part]) + mm_t(dq2_ref[...], wq_ref[:, part:])
-            target = rows_give_ref if offset & 1 else rows_keep_ref
+            target = give_ref if offset & 1 else keep_ref
             target[offset // 2] = total.astype(bf16)
-            values = tok_ref[at, :].astype(f32)
-            inverse = lax.rsqrt(jnp.mean(values * values, axis=-1, keepdims=True) + eps)
-            gain = gain + jnp.sum(total * values * inverse, axis=0, keepdims=True)
-        wide = jnp.concatenate(
-            [router_ref[...], gain, gain_ffn_ref[...], jnp.zeros((small - experts - 2, width), f32)],
-            axis=0,
-        )
-        table = jnp.concatenate([table1_ref[...], table2_ref[...]], axis=0)
-        table = jnp.concatenate([table, jnp.zeros((small - heads, buckets), f32)], axis=0)
-        extra = jnp.concatenate([table, jnp.zeros((small, 3 * part - width - buckets), f32)], axis=1)
-        extra = jnp.concatenate([wide, extra], axis=1).astype(bf16)
-        for at in range(count // 2):
-            give_ref[at, shards:, :] = extra
-            keep_ref[at, shards:, :] = extra
 
     vmem = pl.BlockSpec(memory_space=pltpu.VMEM)
     return pl.pallas_call(
         kernel,
-        in_specs=[pl.BlockSpec(memory_space=pltpu.SMEM)] + [vmem] * 15,
-        out_shape=(
-            shape_of((count // 2, shards + small, 3 * part), bf16),
-            shape_of((count // 2, shards + small, 3 * part), bf16),
-            shape_of((count // 2, tokens, width), bf16),
-            shape_of((count // 2, tokens, width), bf16),
-        ),
-        scratch_shapes=[pltpu.VMEM((width, 3 * part), f32)],
+        in_specs=[pl.BlockSpec(memory_space=pltpu.SMEM)] + [vmem] * 9,
+        out_shape=(shape_of((count // 2, tokens, width), bf16),) * 2,
         compiler_params=params(),
-        cost_estimate=cost(10 * seq * width * width, 10 * seq * width),
-        name="project_back",
-    )(me, *first, *second, normed_t, sequence, *weights, *tables, grad_router, grad_gain_ffn)
+        cost_estimate=cost(10 * count * tokens * width * width, 10 * count * tokens * width),
+        name="rows_back",
+    )(me, *first, *second, *weights)
+
+
+def finish_call(chain1, chain2, weights, gain, half_cols):
+    shards, width = weights[0].shape
+    rest = width - half_cols
+
+    def kernel(c1_ref, c2_ref, wq_ref, wk_ref, wv_ref, gain_ref, gq_ref, gk_ref, gv_ref, go_ref, out_ref):
+        total = jnp.zeros((shards, 1), f32)
+        go_ref[...] = c1_ref[:, :width].astype(f32)
+        for part, (weight_ref, grad_ref) in enumerate(((wq_ref, gq_ref), (wk_ref, gk_ref), (wv_ref, gv_ref))):
+            left = c1_ref[:, width + part * half_cols : width + (part + 1) * half_cols].astype(f32)
+            right = c2_ref[:, part * rest : (part + 1) * rest].astype(f32)
+            grad_ref[:, :half_cols] = left
+            grad_ref[:, half_cols:] = right
+            weight = weight_ref[...].astype(f32)
+            total = total + jnp.sum(left * weight[:, :half_cols], axis=1, keepdims=True)
+            total = total + jnp.sum(right * weight[:, half_cols:], axis=1, keepdims=True)
+        out_ref[...] = jnp.broadcast_to(total, (shards, tile)).T[0:1, :] / gain_ref[...].astype(f32)
+
+    return pl.pallas_call(
+        kernel,
+        out_shape=(shape_of((shards, width), f32),) * 4 + (shape_of((1, shards), f32),),
+        compiler_params=params(),
+        cost_estimate=cost(6 * shards * width, 30 * shards * width),
+        name="finish",
+    )(chain1, chain2, *weights, gain[None, :])
 
 
 def gather_blocks(value, axis_size):
@@ -831,9 +884,12 @@
     return left_side.astype(f32) + right_side.astype(f32)
 
 
-def scatter_sum(given, kept, axis_size, after_cores=None):
-    total = added(kept, swap(given, "fsdp", axis_size, 1))
-    pieces = {2 * at: total[at] for at in range(axis_size // 2)}
+def core_sum(given, kept, axis_size):
+    arrived = swap(given, "fsdp", axis_size, 1)
+    return {2 * at: added(kept[at], arrived[at]).astype(bf16) for at in range(axis_size // 2)}
+
+
+def far_sum(pieces, axis_size, early=None, late=None, cuts=1):
     for bit in scatter_bits(axis_size):
         if bit == 1:
             continue
@@ -841,15 +897,45 @@
         for offset in sorted(pieces):
             if offset & bit:
                 continue
-            leaving = pieces[offset | bit].astype(bf16)
-            if after_cores is not None:
-                leaving = after_cores(leaving)
-            left[offset] = added(pieces[offset], swap(leaving, "fsdp", axis_size, bit))
+            found = []
+            for leaving in jnp.split(pieces[offset | bit].astype(bf16), cuts, axis=0):
+                if early is not None:
+                    leaving = ordered(leaving, early)[0]
+                found.append(swap(leaving, "fsdp", axis_size, bit))
+                early = found[-1]
+            if late is not None:
+                found[-1] = ordered(found[-1], late)[0]
+            left[offset] = added(pieces[offset], jnp.concatenate(found, axis=0))
         pieces = left
     return pieces[0]
 
 
-def all_sum_expert(value, axis_size, index):
+def far_steps(pieces, axis_size, fractions, early=None):
+    bits = [bit for bit in scatter_bits(axis_size) if bit > 1]
+    for bit in bits[:-1]:
+        pieces = {
+            offset: added(
+                pieces[offset], swap(pieces[offset | bit].astype(bf16), "fsdp", axis_size, bit)
+            )
+            for offset in sorted(pieces)
+            if not offset & bit
+        }
+    bit = bits[-1]
+    rows = pieces[0].shape[0]
+    leaving = pieces[bit].astype(bf16)
+    found, begin = [], 0
+    for step, fraction in enumerate(fractions):
+        end = rows if step == len(fractions) - 1 else begin + rows * fraction // 12
+        part = leaving[begin:end]
+        if early is not None:
+            part = ordered(part, early)[0]
+        early = yield swap(part, "fsdp", axis_size, bit)
+        found.append(early)
+        begin = end
+    yield added(pieces[0], jnp.concatenate(found, axis=0))
+
+
+def all_sum_expert(value, axis_size, index, before_last=None):
     rows = value.shape[0]
     parts = jnp.pad(value.astype(bf16), ((0, -rows % (axis_size // 2)), (0, 0)))
     bit, bits = 1, []
@@ -857,20 +943,25 @@
         bits.append(bit)
         bit *= 2
     inner = bits.pop()
+    first_arrived = None
     for bit in bits:
         low_half, high_half = jnp.split(parts, 2, axis=0)
         upper = (index & bit) != 0
         keep = jnp.where(upper, high_half, low_half)
         give = jnp.where(upper, low_half, high_half)
-        parts = added(keep, swap(give, "expert", axis_size, bit)).astype(bf16)
+        arrived = swap(give, "expert", axis_size, bit)
+        first_arrived = arrived if first_arrived is None else first_arrived
+        parts = added(keep, arrived).astype(bf16)
     parts = added(parts, swap(parts, "expert", axis_size, inner)).astype(bf16)
     for bit in reversed(bits):
+        if bit == 1 and before_last is not None:
+            parts = ordered(parts, before_last)[0]
         other = swap(parts, "expert", axis_size, bit)
         upper = (index & bit) != 0
         parts = jnp.concatenate(
             [jnp.where(upper, other, parts), jnp.where(upper, parts, other)], axis=0
         )
-    return parts[:rows]
+    return parts[:rows], first_arrived
 
 
 def ordered(*values):
@@ -937,6 +1028,7 @@
         wo, context_low, residual, ffn_low, gates, rows_out = dispatch_call(
             me, context, out_blocks, tokens_in, smalls, routes, slot_map, heads
         )(experts)
+        normed_t = ordered(normed, rows_out)[0].T
         rows_in = lax.all_to_all(
             rows_out.reshape(experts, capacity, width),
             "expert",
@@ -944,29 +1036,45 @@
             concat_axis=0,
             tiled=True,
         ).reshape(slots, width)
+        rows_in, normed_t = ordered(rows_in, normed_t)
         active, grad_hidden, made, row_grads = expert_call(
             rows_in, grad_rows_in, w_in[0], w_out[0], experts
         )
         row_grads_back = lax.all_to_all(
             row_grads, "expert", split_axis=0, concat_axis=0, tiled=True
-        ).reshape(-1, width)
+        )
 
         rows_t = rows_in.T
-        normed_t = normed.T
         give = [offset for offset in range(count) if offset & 1]
         keep = [offset for offset in range(count) if not offset & 1]
         router = smalls[:experts]
         in_give, in_keep, out_give, out_keep = expert_grads_call(
             me, rows_t, rows_in, grad_rows_in, active, grad_hidden, router, others, give + keep
         )
-        in_total = added(in_keep, swap(in_give, "fsdp", count, 1)).astype(bf16)
-        out_total = added(out_keep, swap(out_give, "fsdp", count, 1)).astype(bf16)
-        row_grads_back, in_total = ordered(row_grads_back, in_total)
+        in_give, out_give, row_grads_back = ordered(in_give, out_give, row_grads_back)
+        in_pieces = core_sum(in_give, in_keep, count)
+        out_pieces = core_sum(out_give, out_keep, count)
 
         grad_residual, branch, grad_context, grad_router, grad_gain_ffn = combine_call(
             experts, heads, row_grads_back, places, gates, routes, cotangent,
             residual, ffn_low, smalls, wo,
         )
+        pairs = width // tile
+        near = pairs // 2
+        last = max(in_pieces)
+        grad_context, in_pieces[last] = ordered(grad_context, in_pieces[last])
+        *part1, table1 = attend_back_call(
+            queries, keys, values, bias, mask, lse, context, grad_context, bucket_window,
+            bucket_count, head_dim, 0, near,
+        )
+        in_steps = far_steps(in_pieces, count, (5, 3, 4))
+        arrived = next(in_steps)
+        part1[0], arrived = ordered(part1[0], arrived)
+        give1, keep1 = first_grads_call(
+            me, *part1, normed_t, context_low, branch, grad_router, grad_gain_ffn, table1, count
+        )
+        arrived = in_steps.send(arrived)
+        made = ordered(made, give1)[0]
         made_back = lax.all_to_all(
             made.reshape(experts, capacity, width),
             "expert",
@@ -974,59 +1082,28 @@
             concat_axis=0,
             tiled=True,
         ).reshape(slots, width)
-        wo_give, wo_keep = output_grad_call(me, context_low, branch, count)
-        grad_context, wo_give, wo_keep = ordered(grad_context, wo_give, wo_keep)
-
-        def far_sum(total, early, late):
-            pieces = {2 * at: total[at] for at in range(count // 2)}
-            for bit in scatter_bits(count):
-                if bit == 1:
-                    continue
-                left = {}
-                for offset in sorted(pieces):
-                    if offset & bit:
-                        continue
-                    leaving = pieces[offset | bit].astype(bf16)
-                    if early is not None:
-                        leaving = ordered(leaving, early)[0]
-                    arrived = swap(leaving, "fsdp", count, bit)
-                    if late is not None:
-                        arrived = ordered(arrived, late)[0]
-                    left[offset] = added(pieces[offset], arrived)
-                pieces = left
-            return pieces[0]
-
-        pairs = width // tile
-        near = pairs // 2
-        part1 = attend_back_call(
-            queries, keys, values, bias, mask, lse, context, grad_context, bucket_window,
-            bucket_count, head_dim, 0, near,
-        )
-        part2 = attend_back_call(
+        pieces1 = core_sum(give1, keep1, count)
+        last = max(pieces1)
+        grad_context, pieces1[last], arrived = ordered(grad_context, pieces1[last], arrived)
+        *part2, table2 = attend_back_call(
             queries, keys, values, bias, mask, lse, context, grad_context, bucket_window,
             bucket_count, head_dim, near, pairs - near,
         )
-        parts = [part1, part2]
-        in_sum = far_sum(in_total, None, part1[0])
-        small_grad_rows = -(-max(experts + 2, heads) // 32) * 32
-        give1, keep1 = projection_grad_call(me, *parts[0][:3], normed_t, count)
-        normed_last, in_sum, give1 = ordered(normed_t, in_sum, give1)
-        give2, keep2, rows_give, rows_keep = project_back_call(
-            me, parts[0][:3], parts[1][:3], normed_last, sequence, (wq, wk, wv),
-            (parts[0][3][:, :, 0], parts[1][3][:, :, 0]), grad_router, grad_gain_ffn, count, small_grad_rows,
-        )
-
-        wo_sum = scatter_sum(wo_give, wo_keep, count)
-        sum1 = scatter_sum(give1, keep1, count)
-        sum2 = scatter_sum(give2, keep2, count)
-        grad_shards = [in_sum, far_sum(out_total, sum2, None)]
-        chain1 = all_sum_expert(jnp.concatenate([wo_sum, sum1], axis=1), expert_ranks, expert_index)
-        chain2 = all_sum_expert(sum2, expert_ranks, expert_index)
-        chain1 = chain1.astype(f32)
-        chain2 = chain2.astype(f32)
+        give2, keep2 = second_grads_call(me, *part2, normed_t, table2, count)
+        sum1 = far_sum(pieces1, count, None, give2)
+        rows_give, rows_keep = rows_back_call(me, part1, part2, (wq, wk, wv), count)
+        sum2 = far_sum(core_sum(give2, keep2, count), count)
+        arrived = in_steps.send(ordered(arrived, sum1)[0])
+        in_sum = in_steps.send(arrived)
+        out_steps = far_steps(out_pieces, count, (6, 6), arrived)
+        arrived = out_steps.send(ordered(next(out_steps), sum2)[0])
+        out_sum = out_steps.send(arrived)
+        grad_shards = [in_sum, out_sum]
+        chain1, _ = all_sum_expert(sum1, expert_ranks, expert_index)
+        chain2, first_arrived = all_sum_expert(sum2, expert_ranks, expert_index)
         half_cols = near * tile
 
-        grad_normed = scatter_sum(rows_give, rows_keep, count, lambda value: ordered(value, sum2)[0])
+        grad_normed = far_sum(core_sum(rows_give, rows_keep, count), count, sum2)
         inputs = tokens_in.astype(f32)
         inverse = lax.rsqrt(jnp.mean(inputs * inputs, axis=-1, keepdims=True) + eps)
         gain_attn = smalls[experts + heads]
@@ -1034,34 +1111,33 @@
         inner = jnp.mean(scaled * inputs, axis=-1, keepdims=True)
         grad_tokens = grad_residual + inverse * scaled - inputs * inverse**3 * inner
 
-        made_back = ordered(made_back, part2[0])[0]
+        made_back = ordered(made_back, sum2)[0]
         picked0 = mm(back0, made_back)
         picked1 = mm(back1, made_back)
         block_out = (residual + gates[:, 0:1] * picked0 + gates[:, 1:2] * picked1).astype(bf16)
 
-        shards_out = []
-        for part in range(3):
-            left = chain1[:, width + part * half_cols : width + (part + 1) * half_cols]
-            rest = width - half_cols
-            right = chain2[:shards, part * rest : (part + 1) * rest]
-            shards_out.append(jnp.concatenate([left, right], axis=1))
-        shards_out.append(chain1[:, :width])
-        small_out = chain2[shards:]
-        cols = lax.dynamic_slice_in_dim(small_out[:, :width], fsdp_index * shards, shards, 1)
+        rest = width - half_cols
+        *shards_out, grad_gain_attn = finish_call(
+            chain1, chain2, (w_query, w_key, w_value), attn_gain, half_cols
+        )
+        router_sum, gain_sum, table_left = first_smalls(
+            chain1[:, width + 3 * half_cols :].astype(f32), experts, 2 * near, bucket_count, width, shards
+        )
+        table_right = chain2[: heads - 2 * near, 3 * rest : 3 * rest + bucket_count].astype(f32)
         table_cols = lax.dynamic_slice_in_dim(
-            small_out[:heads, width:], fsdp_index * bucket_rows, bucket_rows, 1
+            jnp.concatenate([table_left, table_right], axis=0), fsdp_index * bucket_rows, bucket_rows, 1
         )
         return (
             block_out,
             grad_tokens,
-            cols[experts],
+            grad_gain_attn[0],
             shards_out[0],
             shards_out[1],
             shards_out[2],
             shards_out[3],
             table_cols.T,
-            cols[experts + 1],
-            cols[:experts].T,
+            lax.dynamic_slice_in_dim(gain_sum, fsdp_index * shards, shards, 0),
+            lax.dynamic_slice_in_dim(router_sum, fsdp_index * shards, shards, 1).T,
             grad_shards[0][None],
             grad_shards[1][None],
         )

time: 327 us -> 311 us (0.951)
  blocking collectives: 35.7 us -> 0 us
  starting transfers between devices: 39.2 us -> 51 us
  waiting for transfers between devices: 90.3 us -> 101 us
  other arithmetic: 25.2 us -> 18.8 us
    all_to_all x1 -> x0, blocking collectives: 35.7 us -> none  [per_device(): lax.all_to_all(rows_out.reshape(experts, capacity, width), 'expert', spli...]
    all_to_all x0 -> x1, waiting for transfers between devices: none -> 27.6 us  [per_device(): lax.all_to_all(rows_out.reshape(experts, capacity, width), 'expert', spli...]
    ppermute x28 -> x29, waiting for transfers between devices: 78.4 us -> 59.7 us  [swap(): lax.ppermute(value, axis_name, [(i, i ^ bit) for i in range(axis_size)])]
    all_to_all x0 -> x1, starting transfers between devices: none -> 6.16 us  [per_device(): lax.all_to_all(rows_out.reshape(experts, capacity, width), 'expert', spli...]
    ppermute x28 -> x29, starting transfers between devices: 24.3 us -> 29.5 us  [swap(): lax.ppermute(value, axis_name, [(i, i ^ bit) for i in range(axis_size)])]
    all_to_all x1, waiting for transfers between devices: 10.3 us -> 13.9 us  [per_device(): lax.all_to_all(row_grads, 'expert', split_axis=0, concat_axis=0, tiled=True)]
    pallas_call x3 -> x4, Pallas kernels: 19.8 us -> 23.1 us  [the longest x1 8.07 us: rows_back_call(): pl.pallas_call(kernel, in_specs=[pl.BlockSpec(memory_space=pltpu.SMEM)] +...]
    add x6 -> x4, other arithmetic: 5 us -> 7.18 us  [added(): return left_side.astype(f32) + right_side.astype(f32)]
  transfers between devices with their start and end apart: 31 -> 33, of which waited for: 15 -> 18; matrix products, arithmetic and copies ran while one was open for 11% -> 9% of each run, Pallas kernels for 22% -> 28%
where the time goes in v2:
time: 311 us; the launch traced here: 310 us
  Pallas kernels  116 us (37%)
  waiting for transfers between devices  101 us (32%)
  starting transfers between devices  51 us (16%)
  local copies, waits for them, and re-layouts  19.5 us (6%)
  other arithmetic  18.8 us (6%)
    ppermute x29, waiting for transfers between devices, swap(): lax.ppermute(value, axis_name, [(i, i ^ bit) for i in range(axis_size)])  59.7 us
    ppermute x29, starting transfers between devices, swap(): lax.ppermute(value, axis_name, [(i, i ^ bit) for i in range(axis_size)])  29.5 us
    all_to_all x1, waiting for transfers between devices, per_device(): lax.all_to_all(rows_out.reshape(experts, capacity, width), 'expert', spli...  27.6 us
    pallas_call x1, Pallas kernels, expert_call(): pl.pallas_call(kernel, grid=(steps,), in_specs=[full, full, pl.BlockSpec(...  23.4 us
    pallas_call x2, Pallas kernels, attend_back_call(): pl.pallas_call(kernel, grid=(pairs,), in_specs=[narrow, tall, tall, pl.Bl...  17 us
    pallas_call x1, Pallas kernels, expert_grads_call(): pl.pallas_call(kernel, grid_spec=pltpu.PrefetchScalarGridSpec(num_scalar_...  16.2 us
    all_to_all x1, waiting for transfers between devices, per_device(): lax.all_to_all(row_grads, 'expert', split_axis=0, concat_axis=0, tiled=True)  13.9 us
    pallas_call x1, Pallas kernels, attend_call(): pl.pallas_call(kernel, grid=(pairs,), in_specs=[pl.BlockSpec((tokens, til...  10.2 us
  transfers between devices with their start and end apart: 33, of which 18 were waited for; matrix products, arithmetic and copies ran while one was open for 9% of the time, Pallas kernels for 28%

profile of v2, /device:TPU:0, one launch (start us, length us, event | category | flops | bytes accessed | tf_op | source)
XLA Modules:
  0.0 310.5 jit_solution(14162028207688352354)
XLA Ops:
  3.2 2.6 pack.1.refs_0_
  6.2 2.5 collective-permute-start.1
  10.1 3.5 %route.1 = (bf16[768,256]{1,0:T(8,128)(2,1)}, bf16[256,768]{1,0:T(8,128)(2,1)}, bf16[256,768]{1,0:T(8,128)(2,1)}, bf16[8,112,768]{2,1,0:T(8,128)(2,1)}, f32[256,2]{1,0:T(8,128)}) custom-call(s32[256,2]{1,0:T(8,128)} %copy.33.refs_0_.refs_6_.routes_ref, bf16[256,768]{1,0:T(8,128)(2,1)} %cot_ref.1), custom_call_target="tpu_custom_call" | custom-call | flops 1179648 | bytes 9216 | tf_op jit(solution)/shard_map/route/pallas_call | solution.py:102
  13.6 7.2 %all-to-all-start = ((bf16[8,112,768]{2,1,0:T(8,128)(2,1)}), bf16[8,112,768]{2,1,0:T(8,128)(2,1)S(1)}, u32[]{:S(2)}, u32[]{:S(2)}) async-start(bf16[8,112,768]{2,1,0:T(8,128)(2,1)} %get-tuple-element.99), calls=%async_computation | async-start | bytes 2752512 | tf_op jit(solution)/shard_map/all_to_all | solution.py:1017
  20.8 18.1 %collective-permute-done.1.refs_2_ = bf16[864,768]{1,0:T(8,128)(2,1)} collective-permute-done((bf16[864,768]{1,0:T(8,128)(2,1)}, bf16[864,768]{1,0:T(8,128)(2,1)}, u32[]{:S(2)}, u32[]{:S(2)}) %collective-permute-start.1) | collective-permute-done | bytes 1327136 | tf_op jit(solution)/shard_map/ppermute | solution.py:38
  38.9 1.7 collective-permute-start.4
  40.9 7.4 %collective-permute-done.4.refs_2_ = bf16[192,768]{1,0:T(8,128)(2,1)S(1)} collective-permute-done((bf16[192,768]{1,0:T(8,128)(2,1)S(1)}, bf16[192,768]{1,0:T(8,128)(2,1)S(1)}, u32[]{:S(2)}, u32[]{:S(2)}) %collective-permute-start.4) | collective-permute-done | bytes 294944 | tf_op jit(solution)/shard_map/ppermute | solution.py:38
  50.1 10.1 %project.1 = (bf16[256,768]{1,0:T(8,128)(2,1)}, bf16[1024,768]{1,0:T(8,128)(2,1)}, bf16[1024,768]{1,0:T(8,128)(2,1)}, bf16[1024,768]{1,0:T(8,128)(2,1)}, bf16[10...) custom-call(s32[2]{0:T(128)} %pad_add_fusion.me_ref, ...), custom_call_target="tpu_custom_call" | custom-call | flops 10616832 | bytes 61440 | tf_op jit(solution)/shard_map/project/pallas_call | solution.py:202
  62.0 10.2 %attend.1 = (f32[256,768]{1,0:T(8,128)}, f32[12,1,256]{2,1,0:T(1,128)}) custom-call(bf16[256,768]{1,0:T(8,128)(2,1)} %get-tuple-element.100.q_ref, bf16[1024,768]{1,0:T(8,128)(2,1)} %get-tuple-element.101.k_ref, bf16[1024,768]{1,0:T(8,128)(2,1)} %get-tuple-element.102.v_ref, f32[12,1,1280]{2,1,0:T(1,128)} %get-tuple-element.103.bias_ref, ...), custom_call_target="tpu_custom_call" | custom-call | flops 25165824 | bytes 12288 | tf_op jit(solution)/shard_map/attend/pallas_call | solution.py:268
  72.2 4.2 %dispatch.1 = (bf16[768,768]{1,0:T(8,128)(2,1)}, bf16[256,768]{1,0:T(8,128)(2,1)}, f32[256,768]{1,0:T(8,128)}, bf16[256,768]{1,0:T(8,128)(2,1)}, f32[256,2]{1,0:T(8,128)}, /*index=5*/bf16[768,768]{1,0:T(8,128)(2,1)}) custom-call(s32[2]{0:T(128)} %pad_add_fusion.me_ref, f32[256,768]{1,0:T(8,128)} %get-tuple-element.105.ctx_ref, bf16[192,768]{1,0:T(8,128)(2,1)} %refs_0_, ...), custom_call_target="tpu_custom_call" | custom-call | flops 2359296 | bytes 18432 | tf_op jit(solution)/shard_map/dispatch/pallas_call | solution.py:448
  76.4 6.2 %all-to-all-start.1 = ((bf16[8,96,768]{2,1,0:T(8,128)(2,1)}), bf16[8,96,768]{2,1,0:T(8,128)(2,1)S(1)}, u32[]{:S(2)}, u32[]{:S(2)}) async-start(bf16[8,96,768]{2,1,0:T(8,128)(2,1)} %bitcast.68), calls=%async_computation.1 | async-start | bytes 2359296 | tf_op jit(solution)/shard_map/all_to_all | solution.py:1032
  82.6 1.6 copy.35
  84.3 27.6 %all-to-all-done.1 = bf16[8,96,768]{2,1,0:T(8,128)(2,1)S(1)} async-done(((bf16[8,96,768]{2,1,0:T(8,128)(2,1)}), bf16[8,96,768]{2,1,0:T(8,128)(2,1)S(1)}, u32[]{:S(2)}, u32[]{:S(2)}) %all-to-all-start.1) | async-done | bytes 1179680 | tf_op jit(solution)/shard_map/all_to_all | solution.py:1032
  112.9 23.4 %experts.1 = (bf16[768,3072]{1,0:T(8,128)(2,1)}, bf16[768,3072]{1,0:T(8,128)(2,1)}, bf16[768,768]{1,0:T(8,128)(2,1)}, bf16[8,112,768]{2,1,0:T(8,128)(2,1)}) custom-call(bf16[768,768]{1,0:T(8,128)(2,1)} %bitcast.57, bf16[768,768]{1,0:T(8,128)(2,1)} %bitcast.62, bf16[768,3072]{1,0:T(8,128)(2,1)} %bitcast.66, bf16[3072,768]{1,0:T(8,128)(2,1)} %bitcast.67), custom_call_target="tpu_custom_call" | custom-call | flops 56623104 | bytes 73728 | tf_op jit(solution)/shard_map/experts/pallas_call | solution.py:521
  136.3 3.9 %all-to-all-start.2 = ((bf16[8,112,768]{2,1,0:T(8,128)(2,1)}), bf16[8,112,768]{2,1,0:T(8,128)(2,1)S(1)}, u32[]{:S(2)}, u32[]{:S(2)}) async-start(bf16[8,112,768]{2,1,0:T(8,128)(2,1)} %get-tuple-element.124), calls=%async_computation.2 | async-start | bytes 2752512 | tf_op jit(solution)/shard_map/all_to_all | solution.py:1043
  143.0 16.2 %expert_grads.1 = (bf16[2,192,3072]{2,1,0:T(8,128)(2,1)}, bf16[2,192,3072]{2,1,0:T(8,128)(2,1)}, bf16[2,768,768]{2,1,0:T(8,128)(2,1)}, bf16[2,768,768]{2,1,0:T(8,128)(2,1)}) custom-call(s32[2]{0:T(128)} %pad_add_fusion.me_ref, bf16[768,768]{1,0:T(8,128)(2,1)} %copy.36.xt_ref, bf16[768,768]{1,0:T(8,128)(2,1)} %bitcast.58, bf16[768,768]{1,0:T(8,128)(2,1)} %bitcast.63, ...), custom_call_target="tpu_custom_call" | custom-call | flops 28311552 | bytes 73728 | tf_op jit(solution)/shard_map/expert_grads/pallas_call | solution.py:605
  159.2 13.9 %all-to-all-done.2.rows_ref = bf16[8,112,768]{2,1,0:T(8,128)(2,1)S(1)} async-done(((bf16[8,112,768]{2,1,0:T(8,128)(2,1)}), bf16[8,112,768]{2,1,0:T(8,128)(2,1)S(1)}, u32[]{:S(2)}, u32[]{:S(2)}) %all-to-all-start.2) | async-done | bytes 1376288 | tf_op jit(solution)/shard_map/all_to_all | solution.py:1043
  174.3 5.9 %combine.1 = (f32[256,768]{1,0:T(8,128)}, bf16[256,768]{1,0:T(8,128)(2,1)}, bf16[256,768]{1,0:T(8,128)(2,1)}, f32[8,768]{1,0:T(8,128)}, f32[1,768]{1,0:T(1,128)}) custom-call(bf16[8,112,768]{2,1,0:T(8,128)(2,1)} %copy-done.3, f32[256,2]{1,0:T(8,128)} %get-tuple-element.126.place_ref, f32[256,2]{1,0:T(8,128)} %get-tuple-element.110.gate_ref, ...), custom_call_target="tpu_custom_call" | custom-call | flops 3538944 | bytes 18432 | tf_op jit(solution)/shard_map/combine/pallas_call | solution.py:686
  181.6 1.6 collective-permute-start.7
  183.2 8.5 %attend_back.2 = (bf16[256,384]{1,0:T(8,128)(2,1)}, bf16[1024,384]{1,0:T(8,128)(2,1)}, bf16[1024,384]{1,0:T(8,128)(2,1)}, f32[6,1,32]{2,1,0:T(1,128)}) custom-call(bf16[256,768]{1,0:T(8,128)(2,1)} %get-tuple-element.100.q_ref, bf16[1024,768]{1,0:T(8,128)(2,1)} %get-tuple-element.101.k_ref, bf16[1024,768]{1,0:T(8,128)(2,1)} %get-tuple-element.102.v_ref, ...), custom_call_target="tpu_custom_call" | custom-call | flops 31457280 | bytes 12288 | tf_op jit(solution)/shard_map/attend_back/pallas_call | solution.py:365
  191.7 2.5 collective-permute-done.7
  194.2 6.6 %first_grads.1 = (bf16[2,192,2048]{2,1,0:T(8,128)(2,1)}, bf16[2,192,2048]{2,1,0:T(8,128)(2,1)}) custom-call(s32[2]{0:T(128)} %pad_add_fusion.me_ref, bf16[256,384]{1,0:T(8,128)(2,1)} %get-tuple-element.135.dq_ref.dq1_ref, bf16[1024,384]{1,0:T(8,128)(2,1)} %get-tuple-element.136.dk_ref.dk1_ref, bf16[1024,384]{1,0:T(8,128)(2,1)} %get-tuple-element.137.dv_ref.dv1_ref, ...), custom_call_target="tpu_custom_call" | custom-call | flops 5898240 | bytes 30720 | tf_op jit(solution)/shard_map/first_grads/pallas_call | solution.py:753
  200.8 1.6 collective-permute-start.9
  202.4 2.1 collective-permute-done.8
  204.5 2.7 fusion.5
  207.2 3.1 collective-permute-done.9
  210.3 1.5 collective-permute-start.14
  216.1 4.2 %all-to-all-start.3 = ((bf16[8,96,768]{2,1,0:T(8,128)(2,1)}), bf16[8,96,768]{2,1,0:T(8,128)(2,1)S(1)}, u32[]{:S(2)}, u32[]{:S(2)}) async-start(bf16[8,96,768]{2,1,0:T(8,128)(2,1)} %bitcast.12), calls=%async_computation.3 | async-start | bytes 2359296 | tf_op jit(solution)/shard_map/all_to_all | solution.py:1078
  220.3 8.5 %attend_back.3 = (bf16[256,384]{1,0:T(8,128)(2,1)}, bf16[1024,384]{1,0:T(8,128)(2,1)}, bf16[1024,384]{1,0:T(8,128)(2,1)}, f32[6,1,32]{2,1,0:T(1,128)}) custom-call(bf16[256,768]{1,0:T(8,128)(2,1)} %get-tuple-element.100.q_ref, bf16[1024,768]{1,0:T(8,128)(2,1)} %get-tuple-element.101.k_ref, bf16[1024,768]{1,0:T(8,128)(2,1)} %get-tuple-element.102.v_ref, ...), custom_call_target="tpu_custom_call" | custom-call | flops 31457280 | bytes 12288 | tf_op jit(solution)/shard_map/attend_back/pallas_call | solution.py:365
  228.8 5.3 %second_grads.1 = (bf16[2,192,1280]{2,1,0:T(8,128)(2,1)}, bf16[2,192,1280]{2,1,0:T(8,128)(2,1)}) custom-call(s32[2]{0:T(128)} %pad_add_fusion.me_ref, bf16[256,384]{1,0:T(8,128)(2,1)} %get-tuple-element.150.dq_ref.dq2_ref, bf16[1024,384]{1,0:T(8,128)(2,1)} %get-tuple-element.151.dk_ref.dk2_ref, bf16[1024,384]{1,0:T(8,128)(2,1)} %get-tuple-element.152.dv_ref.dv2_ref, ...), custom_call_target="tpu_custom_call" | custom-call | flops 5898240 | bytes 30720 | tf_op jit(solution)/shard_map/second_grads/pallas_call | solution.py:798
  234.1 8.1 %rows_back.1 = (bf16[2,256,768]{2,1,0:T(8,128)(2,1)}, bf16[2,256,768]{2,1,0:T(8,128)(2,1)}) custom-call(s32[2]{0:T(128)} %pad_add_fusion.me_ref, bf16[256,384]{1,0:T(8,128)(2,1)} %get-tuple-element.135.dq_ref.dq1_ref, bf16[1024,384]{1,0:T(8,128)(2,1)} %get-tuple-element.136.dk_ref.dk1_ref, bf16[1024,384]{1,0:T(8,128)(2,1)} %get-tuple-element.137.dv_ref.dv1_ref, ...), custom_call_target="tpu_custom_call" | custom-call | flops 23592960 | bytes 30720 | tf_op jit(solution)/shard_map/rows_back/pallas_call | solution.py:827
  242.8 1.8 convert_add_fusion.2
  244.7 2.1 collective-permute-start.15
  248.3 1.6 collective-permute-start.11
  249.9 6.2 %collective-permute-done.15 = bf16[96,2048]{1,0:T(8,128)(2,1)S(1)} collective-permute-done((bf16[96,2048]{1,0:T(8,128)(2,1)S(1)}, bf16[96,2048]{1,0:T(8,128)(2,1)S(1)}, u32[]{:S(2)}, u32[]{:S(2)}) %collective-permute-start.15) | collective-permute-done | bytes 393248 | tf_op jit(solution)/shard_map/ppermute | solution.py:38
  256.3 1.8 collective-permute-start.16
  259.3 2.0 convert_add_fusion.1
  262.8 2.4 collective-permute-start.17
  265.2 4.1 %collective-permute-done.11 = bf16[192,1280]{1,0:T(8,128)(2,1)S(1)} collective-permute-done((bf16[192,1280]{1,0:T(8,128)(2,1)S(1)}, bf16[192,1280]{1,0:T(8,128)(2,1)S(1)}, u32[]{:S(2)}, u32[]{:S(2)}) %collective-permute-start.11) | collective-permute-done | bytes 491552 | tf_op jit(solution)/shard_map/ppermute | solution.py:38
  274.6 2.0 collective-permute-start.18
  277.3 1.5 collective-permute-start.21
  278.8 3.4 %collective-permute-done.18 = bf16[48,2048]{1,0:T(8,128)(2,1)S(1)} collective-permute-done((bf16[48,2048]{1,0:T(8,128)(2,1)S(1)}, bf16[48,2048]{1,0:T(8,128)(2,1)S(1)}, u32[]{:S(2)}, u32[]{:S(2)}) %collective-permute-start.18) | collective-permute-done | bytes 196640 | tf_op jit(solution)/shard_map/ppermute | solution.py:38
  284.0 2.4 collective-permute-start.22
  286.4 4.0 %collective-permute-done.13 = bf16[256,768]{1,0:T(8,128)(2,1)S(1)} collective-permute-done((bf16[256,768]{1,0:T(8,128)(2,1)}, bf16[256,768]{1,0:T(8,128)(2,1)S(1)}, u32[]{:S(2)}, u32[]{:S(2)}) %collective-permute-start.13) | collective-permute-done | bytes 393248 | tf_op jit(solution)/shard_map/ppermute | solution.py:38
  293.6 2.6 collective-permute-done.23
  299.7 2.7 collective-permute-done.24
  303.4 3.1 finish.1
  307.3 3.2 %convert_add_fusion = f32[1,768,768]{2,1,0:T(8,128)} fusion(bf16[2,768,768]{2,1,0:T(8,128)(2,1)} %copy-done.7, bf16[1,384,768]{2,1,0:T(8,128)(2,1)S(1)} %bitcast.69, bf16[1,384,768]{2,1,0:T(8,128)(2,1)} %bitcast.28, bf16[2,768,768]{2,1,0:T(8,128)(2,1)S(1)} %copy-done.6), kind=kLoop, calls=%fused_computation | loop fusion | flops 5898240 | bytes 5898240 | tf_op jit(solution)/shard_map/add | solution.py:884
  (167 shorter events, 39.9 us)
Async XLA Ops:
  2.0 11.6 %copy-start.31 = (bf16[1,192]{1,0:T(2,128)(2,1)}, bf16[1,192]{1,0:T(2,128)(2,1)S(1)}, u32[]{:S(2)}) copy-start(bf16[1,192]{1,0:T(2,128)(2,1)S(1)} %stack.21.gain_ref) | copy-start | bytes 1156
  5.8 3.3 %collective-permute-start = (bf16[864,768]{1,0:T(8,128)(2,1)}, bf16[864,768]{1,0:T(8,128)(2,1)S(1)}, u32[]{:S(2)}, u32[]{:S(2)}) collective-permute-start(bf16[864,768]{1,0:T(8,128)(2,1)} %pack.1.refs_0_), channel_id=1, source_target_pairs={{0,1},{1,0},{2,3},{3,2},{4,5},{5,4},{6,7},{7,6},{8,9},{9,8},{10,11... | collective-permute-start | bytes 3981320 | tf_op jit(solution)/shard_map/ppermute | solution.py:38
  6.2 32.6 %collective-permute-start.1 = (bf16[864,768]{1,0:T(8,128)(2,1)}, bf16[864,768]{1,0:T(8,128)(2,1)}, u32[]{:S(2)}, u32[]{:S(2)}) collective-permute-start(bf16[864,768]{1,0:T(8,128)(2,1)} %pack.1.refs_0_), channel_id=1, source_target_pairs={{0,2},{1,3},{2,0},{3,1},{4,6},{5,7},{6,4},{7,5},{8,10},{9,11},{10,... | collective-permute-start | bytes 3981320 | tf_op jit(solution)/shard_map/ppermute | solution.py:38
  10.1 28.8 %copy-start.27 = (bf16[192,768]{1,0:T(8,128)(2,1)S(1)}, bf16[192,768]{1,0:T(8,128)(2,1)}, u32[]{:S(2)}) copy-start(bf16[192,768]{1,0:T(8,128)(2,1)} %refs_0_) | copy-start | bytes 884740
  10.1 38.2 %copy-start.32 = (s32[1024]{0:T(1024)S(1)}, s32[1024]{0:T(1024)}, u32[]{:S(2)}) copy-start(s32[1024]{0:T(1024)} %param.18) | copy-start | bytes 12292
  13.6 46.6 %all-to-all-start = ((bf16[8,112,768]{2,1,0:T(8,128)(2,1)}), bf16[8,112,768]{2,1,0:T(8,128)(2,1)S(1)}, u32[]{:S(2)}, u32[]{:S(2)}) async-start(bf16[8,112,768]{2,1,0:T(8,128)(2,1)} %get-tuple-element.99), calls=%async_computation | async-start | bytes 2752512 | tf_op jit(solution)/shard_map/all_to_all | solution.py:1017
  38.9 10.1 %collective-permute-start.2 = (bf16[864,768]{1,0:T(8,128)(2,1)}, bf16[864,768]{1,0:T(8,128)(2,1)S(1)}, u32[]{:S(2)}, u32[]{:S(2)}) collective-permute-start(bf16[864,768]{1,0:T(8,128)(2,1)} %collective-permute-done.1.refs_2_), channel_id=1, source_target_pairs={{0,1},{1,0},{2,3},{3,2},{4,5},{5,4},{6,7},{7,6},{8,9},{9,8},{10,11... | collective-permute-start | bytes 3981320 | tf_op jit(solution)/shard_map/ppermute | solution.py:38
  38.9 9.4 %collective-permute-start.4 = (bf16[192,768]{1,0:T(8,128)(2,1)S(1)}, bf16[192,768]{1,0:T(8,128)(2,1)S(1)}, u32[]{:S(2)}, u32[]{:S(2)}) collective-permute-start(bf16[192,768]{1,0:T(8,128)(2,1)S(1)} %copy-done.27), channel_id=1, source_target_pairs={{0,2},{1,3},{2,0},{3,1},{4,6},{5,7},{6,4},{7,5},{8,10},{9,11},{10,... | collective-permute-start | bytes 884744 | tf_op jit(solution)/shard_map/ppermute | solution.py:38
  40.6 31.6 %collective-permute-start.3 = (bf16[192,768]{1,0:T(8,128)(2,1)S(1)}, bf16[192,768]{1,0:T(8,128)(2,1)}, u32[]{:S(2)}, u32[]{:S(2)}) collective-permute-start(bf16[192,768]{1,0:T(8,128)(2,1)S(1)} %copy-done.27), channel_id=1, source_target_pairs={{0,1},{1,0},{2,3},{3,2},{4,5},{5,4},{6,7},{7,6},{8,9},{9,8},{10,11... | collective-permute-start | bytes 884744 | tf_op jit(solution)/shard_map/ppermute | solution.py:38
  48.3 23.9 %copy-start.30 = (bf16[192,768]{1,0:T(8,128)(2,1)}, bf16[192,768]{1,0:T(8,128)(2,1)S(1)}, u32[]{:S(2)}) copy-start(bf16[192,768]{1,0:T(8,128)(2,1)S(1)} %collective-permute-done.4.refs_2_) | copy-start | bytes 884740
  48.3 23.9 %collective-permute-start.5 = (bf16[192,768]{1,0:T(8,128)(2,1)S(1)}, bf16[192,768]{1,0:T(8,128)(2,1)}, u32[]{:S(2)}, u32[]{:S(2)}) collective-permute-start(bf16[192,768]{1,0:T(8,128)(2,1)S(1)} %collective-permute-done.4.refs_2_), channel_id=1, source_target_pairs={{0,1},{1,0},{2,3},{3,2},{4,5},{5,4},{6,7},{7,6},{8,9},{9,8},{10,11... | collective-permute-start | bytes 884744 | tf_op jit(solution)/shard_map/ppermute | solution.py:38
  76.4 35.4 %all-to-all-start.1 = ((bf16[8,96,768]{2,1,0:T(8,128)(2,1)}), bf16[8,96,768]{2,1,0:T(8,128)(2,1)S(1)}, u32[]{:S(2)}, u32[]{:S(2)}) async-start(bf16[8,96,768]{2,1,0:T(8,128)(2,1)} %bitcast.68), calls=%async_computation.1 | async-start | bytes 2359296 | tf_op jit(solution)/shard_map/all_to_all | solution.py:1032
  136.3 36.8 %all-to-all-start.2 = ((bf16[8,112,768]{2,1,0:T(8,128)(2,1)}), bf16[8,112,768]{2,1,0:T(8,128)(2,1)S(1)}, u32[]{:S(2)}, u32[]{:S(2)}) async-start(bf16[8,112,768]{2,1,0:T(8,128)(2,1)} %get-tuple-element.124), calls=%async_computation.2 | async-start | bytes 2752512 | tf_op jit(solution)/shard_map/all_to_all | solution.py:1043
  173.1 7.0 %collective-permute-start.6 = (bf16[2,192,3072]{2,1,0:T(8,128)(2,1)}, bf16[2,192,3072]{2,1,0:T(8,128)(2,1)S(1)}, u32[]{:S(2)}, u32[]{:S(2)}) collective-permute-start(bf16[2,192,3072]{2,1,0:T(8,128)(2,1)} %get-tuple-element.131), channel_id=1, source_target_pairs={{0,1},{1,0},{2,3},{3,2},{4,5},{5,4},{6,7},{7,6},{8,9},{9,8},{10,11... | collective-permute-start | bytes 7077896 | tf_op jit(solution)/shard_map/ppermute | solution.py:38
  181.6 12.6 %collective-permute-start.7 = (bf16[80,3072]{1,0:T(8,128)(2,1)S(1)}, bf16[80,3072]{1,0:T(8,128)(2,1)S(1)}, u32[]{:S(2)}, u32[]{:S(2)}) collective-permute-start(bf16[80,3072]{1,0:T(8,128)(2,1)S(1)} %slice.140), channel_id=1, source_target_pairs={{0,2},{1,3},{2,0},{3,1},{4,6},{5,7},{6,4},{7,5},{8,10},{9,11},{10,... | collective-permute-start | bytes 1474568 | tf_op jit(solution)/shard_map/ppermute | solution.py:38
  183.2 30.4 %collective-permute-start.26 = (bf16[2,768,768]{2,1,0:T(8,128)(2,1)}, bf16[2,768,768]{2,1,0:T(8,128)(2,1)S(1)}, u32[]{:S(2)}, u32[]{:S(2)}) collective-permute-start(bf16[2,768,768]{2,1,0:T(8,128)(2,1)} %get-tuple-element.176), channel_id=1, source_target_pairs={{0,1},{1,0},{2,3},{3,2},{4,5},{5,4},{6,7},{7,6},{8,9},{9,8},{10,11... | collective-permute-start | bytes 7077896 | tf_op jit(solution)/shard_map/ppermute | solution.py:38
  200.8 3.8 %collective-permute-start.8 = (bf16[2,192,2048]{2,1,0:T(8,128)(2,1)}, bf16[2,192,2048]{2,1,0:T(8,128)(2,1)}, u32[]{:S(2)}, u32[]{:S(2)}) collective-permute-start(bf16[2,192,2048]{2,1,0:T(8,128)(2,1)} %get-tuple-element.144), channel_id=1, source_target_pairs={{0,1},{1,0},{2,3},{3,2},{4,5},{5,4},{6,7},{7,6},{8,9},{9,8},{10,11... | collective-permute-start | bytes 4718600 | tf_op jit(solution)/shard_map/ppermute | solution.py:38
  200.8 11.8 %copy-start.19 = (f32[256,2]{1,0:T(8,128)S(1)}, f32[256,2]{1,0:T(8,128)}, u32[]{:S(2)}) copy-start(f32[256,2]{1,0:T(8,128)} %get-tuple-element.110.gate_ref) | copy-start | bytes 6148
  200.8 9.5 %collective-permute-start.9 = (bf16[48,3072]{1,0:T(8,128)(2,1)S(1)}, bf16[48,3072]{1,0:T(8,128)(2,1)S(1)}, u32[]{:S(2)}, u32[]{:S(2)}) collective-permute-start(bf16[48,3072]{1,0:T(8,128)(2,1)S(1)} %slice.143), channel_id=1, source_target_pairs={{0,2},{1,3},{2,0},{3,1},{4,6},{5,7},{6,4},{7,5},{8,10},{9,11},{10,... | collective-permute-start | bytes 884744 | tf_op jit(solution)/shard_map/ppermute | solution.py:38
  204.5 9.1 %copy-start.5 = (bf16[2,768,768]{2,1,0:T(8,128)(2,1)S(1)}, bf16[2,768,768]{2,1,0:T(8,128)(2,1)}, u32[]{:S(2)}) copy-start(bf16[2,768,768]{2,1,0:T(8,128)(2,1)} %get-tuple-element.175) | copy-start | bytes 7077892
  210.3 32.5 %collective-permute-start.14 = (bf16[192,2048]{1,0:T(8,128)(2,1)}, bf16[192,2048]{1,0:T(8,128)(2,1)}, u32[]{:S(2)}, u32[]{:S(2)}) collective-permute-start(bf16[192,2048]{1,0:T(8,128)(2,1)} %fusion.5), channel_id=1, source_target_pairs={{0,2},{1,3},{2,0},{3,1},{4,6},{5,7},{6,4},{7,5},{8,10},{9,11},{10,... | collective-permute-start | bytes 2359304 | tf_op jit(solution)/shard_map/ppermute | solution.py:38
  216.1 54.2 %all-to-all-start.3 = ((bf16[8,96,768]{2,1,0:T(8,128)(2,1)}), bf16[8,96,768]{2,1,0:T(8,128)(2,1)S(1)}, u32[]{:S(2)}, u32[]{:S(2)}) async-start(bf16[8,96,768]{2,1,0:T(8,128)(2,1)} %bitcast.12), calls=%async_computation.3 | async-start | bytes 2359296 | tf_op jit(solution)/shard_map/all_to_all | solution.py:1078
  234.1 14.1 %collective-permute-start.10 = (bf16[2,192,1280]{2,1,0:T(8,128)(2,1)}, bf16[2,192,1280]{2,1,0:T(8,128)(2,1)S(1)}, u32[]{:S(2)}, u32[]{:S(2)}) collective-permute-start(bf16[2,192,1280]{2,1,0:T(8,128)(2,1)} %get-tuple-element.155), channel_id=1, source_target_pairs={{0,1},{1,0},{2,3},{3,2},{4,5},{5,4},{6,7},{7,6},{8,9},{9,8},{10,11... | collective-permute-start | bytes 2949128 | tf_op jit(solution)/shard_map/ppermute | solution.py:38
  234.1 8.7 %copy-start.16 = (bf16[2,192,2048]{2,1,0:T(8,128)(2,1)S(1)}, bf16[2,192,2048]{2,1,0:T(8,128)(2,1)}, u32[]{:S(2)}) copy-start(bf16[2,192,2048]{2,1,0:T(8,128)(2,1)} %get-tuple-element.146) | copy-start | bytes 4718596
  242.2 5.1 %collective-permute-start.12 = (bf16[2,256,768]{2,1,0:T(8,128)(2,1)}, bf16[2,256,768]{2,1,0:T(8,128)(2,1)S(1)}, u32[]{:S(2)}, u32[]{:S(2)}) collective-permute-start(bf16[2,256,768]{2,1,0:T(8,128)(2,1)} %get-tuple-element.163), channel_id=1, source_target_pairs={{0,1},{1,0},{2,3},{3,2},{4,5},{5,4},{6,7},{7,6},{8,9},{9,8},{10,11... | collective-permute-start | bytes 2359304 | tf_op jit(solution)/shard_map/ppermute | solution.py:38
  242.8 16.5 %copy-start.24 = (bf16[80,3072]{1,0:T(8,128)(2,1)S(1)}, bf16[80,3072]{1,0:T(8,128)(2,1)}, u32[]{:S(2)}) copy-start(bf16[80,3072]{1,0:T(8,128)(2,1)} %copy-done.23) | copy-start | bytes 1474564
  244.6 14.7 %copy-start.29 = (bf16[48,3072]{1,0:T(8,128)(2,1)S(1)}, bf16[48,3072]{1,0:T(8,128)(2,1)}, u32[]{:S(2)}) copy-start(bf16[48,3072]{1,0:T(8,128)(2,1)} %copy-done.28) | copy-start | bytes 884740
  244.7 11.4 %collective-permute-start.15 = (bf16[96,2048]{1,0:T(8,128)(2,1)S(1)}, bf16[96,2048]{1,0:T(8,128)(2,1)S(1)}, u32[]{:S(2)}, u32[]{:S(2)}) collective-permute-start(bf16[96,2048]{1,0:T(8,128)(2,1)S(1)} %broadcast_select_fusion.2), channel_id=1, source_target_pairs={{0,4},{4,0},{8,12},{12,8},{16,20},{20,16},{24,28},{28,24},{1,5},{5... | collective-permute-start | bytes 1179656 | tf_op jit(solution)/shard_map/ppermute | solution.py:38
  246.8 12.0 %collective-permute-start.25 = (bf16[64,3072]{1,0:T(8,128)(2,1)S(1)}, bf16[64,3072]{1,0:T(8,128)(2,1)S(1)}, u32[]{:S(2)}, u32[]{:S(2)}) collective-permute-start(bf16[64,3072]{1,0:T(8,128)(2,1)S(1)} %copy-done.26), channel_id=1, source_target_pairs={{0,2},{1,3},{2,0},{3,1},{4,6},{5,7},{6,4},{7,5},{8,10},{9,11},{10,... | collective-permute-start | bytes 1179656 | tf_op jit(solution)/shard_map/ppermute | solution.py:38
  247.3 9.0 %copy-start.13 = (bf16[2,256,768]{2,1,0:T(8,128)(2,1)}, bf16[2,256,768]{2,1,0:T(8,128)(2,1)S(1)}, u32[]{:S(2)}) copy-start(bf16[2,256,768]{2,1,0:T(8,128)(2,1)S(1)} %collective-permute-done.12) | copy-start | bytes 2359300
  247.3 12.0 %copy-start.11 = (bf16[2,192,3072]{2,1,0:T(8,128)(2,1)S(1)}, bf16[2,192,3072]{2,1,0:T(8,128)(2,1)}, u32[]{:S(2)}) copy-start(bf16[2,192,3072]{2,1,0:T(8,128)(2,1)} %copy-done.10) | copy-start | bytes 7077892
  248.2 11.1 %copy-start.9 = (bf16[2,192,3072]{2,1,0:T(8,128)(2,1)S(1)}, bf16[2,192,3072]{2,1,0:T(8,128)(2,1)}, u32[]{:S(2)}) copy-start(bf16[2,192,3072]{2,1,0:T(8,128)(2,1)} %get-tuple-element.130) | copy-start | bytes 7077892
  248.3 21.0 %collective-permute-start.11 = (bf16[192,1280]{1,0:T(8,128)(2,1)S(1)}, bf16[192,1280]{1,0:T(8,128)(2,1)S(1)}, u32[]{:S(2)}, u32[]{:S(2)}) collective-permute-start(bf16[192,1280]{1,0:T(8,128)(2,1)S(1)} %fusion.9), channel_id=1, source_target_pairs={{0,2},{1,3},{2,0},{3,1},{4,6},{5,7},{6,4},{7,5},{8,10},{9,11},{10,... | collective-permute-start | bytes 1474568 | tf_op jit(solution)/shard_map/ppermute | solution.py:38
  256.3 6.4 %collective-permute-start.16 = (bf16[48,2048]{1,0:T(8,128)(2,1)S(1)}, bf16[48,2048]{1,0:T(8,128)(2,1)S(1)}, u32[]{:S(2)}, u32[]{:S(2)}) collective-permute-start(bf16[48,2048]{1,0:T(8,128)(2,1)S(1)} %broadcast_select_fusion.8), channel_id=1, source_target_pairs={{0,8},{4,12},{8,0},{12,4},{16,24},{20,28},{24,16},{28,20},{1,9},{5... | collective-permute-start | bytes 589832 | tf_op jit(solution)/shard_map/ppermute | solution.py:38
  258.8 24.3 %collective-permute-start.27 = (bf16[384,768]{1,0:T(8,128)(2,1)}, bf16[384,768]{1,0:T(8,128)(2,1)}, u32[]{:S(2)}, u32[]{:S(2)}) collective-permute-start(bf16[384,768]{1,0:T(8,128)(2,1)} %get-tuple-element.177), channel_id=1, source_target_pairs={{0,2},{1,3},{2,0},{3,1},{4,6},{5,7},{6,4},{7,5},{8,10},{9,11},{10,... | collective-permute-start | bytes 1769480 | tf_op jit(solution)/shard_map/ppermute | solution.py:38
  262.8 10.7 %collective-permute-start.17 = (bf16[48,2048]{1,0:T(8,128)(2,1)S(1)}, bf16[48,2048]{1,0:T(8,128)(2,1)}, u32[]{:S(2)}, u32[]{:S(2)}) collective-permute-start(bf16[48,2048]{1,0:T(8,128)(2,1)S(1)} %add_convert_fusion.14), channel_id=1, source_target_pairs={{0,16},{4,20},{8,24},{12,28},{16,0},{20,4},{24,8},{28,12},{1,17},{... | collective-permute-start | bytes 589832 | tf_op jit(solution)/shard_map/ppermute | solution.py:38
  270.2 20.1 %collective-permute-start.13 = (bf16[256,768]{1,0:T(8,128)(2,1)}, bf16[256,768]{1,0:T(8,128)(2,1)S(1)}, u32[]{:S(2)}, u32[]{:S(2)}) collective-permute-start(bf16[256,768]{1,0:T(8,128)(2,1)} %fusion.11), channel_id=1, source_target_pairs={{0,2},{1,3},{2,0},{3,1},{4,6},{5,7},{6,4},{7,5},{8,10},{9,11},{10,... | collective-permute-start | bytes 1179656 | tf_op jit(solution)/shard_map/ppermute | solution.py:38
  270.7 6.4 %collective-permute-start.20 = (bf16[96,1280]{1,0:T(8,128)(2,1)}, bf16[96,1280]{1,0:T(8,128)(2,1)S(1)}, u32[]{:S(2)}, u32[]{:S(2)}) collective-permute-start(bf16[96,1280]{1,0:T(8,128)(2,1)} %broadcast_select_fusion.5), channel_id=1, source_target_pairs={{0,4},{4,0},{8,12},{12,8},{16,20},{20,16},{24,28},{28,24},{1,5},{5... | collective-permute-start | bytes 737288 | tf_op jit(solution)/shard_map/ppermute | solution.py:38
  274.6 15.8 %copy-start.2 = (bf16[256,768]{1,0:T(8,128)(2,1)S(1)}, bf16[256,768]{1,0:T(8,128)(2,1)}, u32[]{:S(2)}) copy-start(bf16[256,768]{1,0:T(8,128)(2,1)} %refs_4_.1) | copy-start | bytes 1179652
  274.6 15.8 %copy-start.14 = (bf16[2,256,768]{2,1,0:T(8,128)(2,1)S(1)}, bf16[2,256,768]{2,1,0:T(8,128)(2,1)}, u32[]{:S(2)}) copy-start(bf16[2,256,768]{2,1,0:T(8,128)(2,1)} %copy-done.13) | copy-start | bytes 2359300
  274.6 7.6 %collective-permute-start.18 = (bf16[48,2048]{1,0:T(8,128)(2,1)S(1)}, bf16[48,2048]{1,0:T(8,128)(2,1)S(1)}, u32[]{:S(2)}, u32[]{:S(2)}) collective-permute-start(bf16[48,2048]{1,0:T(8,128)(2,1)S(1)} %add_convert_fusion.13), channel_id=1, source_target_pairs={{0,8},{4,12},{8,0},{12,4},{16,24},{20,28},{24,16},{28,20},{1,9},{5... | collective-permute-start | bytes 589832 | tf_op jit(solution)/shard_map/ppermute | solution.py:38
  277.3 6.7 %collective-permute-start.21 = (bf16[48,1280]{1,0:T(8,128)(2,1)S(1)}, bf16[48,1280]{1,0:T(8,128)(2,1)S(1)}, u32[]{:S(2)}, u32[]{:S(2)}) collective-permute-start(bf16[48,1280]{1,0:T(8,128)(2,1)S(1)} %broadcast_select_fusion.11), channel_id=1, source_target_pairs={{0,8},{4,12},{8,0},{12,4},{16,24},{20,28},{24,16},{28,20},{1,9},{5... | collective-permute-start | bytes 368648 | tf_op jit(solution)/shard_map/ppermute | solution.py:38
  282.2 10.1 %copy-start.21 = (f32[256,768]{1,0:T(8,128)S(1)}, f32[256,768]{1,0:T(8,128)}, u32[]{:S(2)}) copy-start(f32[256,768]{1,0:T(8,128)} %get-tuple-element.158) | copy-start | bytes 2359300
  282.3 14.9 %collective-permute-start.19 = (bf16[96,2048]{1,0:T(8,128)(2,1)S(1)}, bf16[96,2048]{1,0:T(8,128)(2,1)S(1)}, u32[]{:S(2)}, u32[]{:S(2)}) collective-permute-start(bf16[96,2048]{1,0:T(8,128)(2,1)S(1)} %pad_maximum_fusion.2), channel_id=1, source_target_pairs={{0,4},{4,0},{8,12},{12,8},{16,20},{20,16},{24,28},{28,24},{1,5},{5... | collective-permute-start | bytes 1179656 | tf_op jit(solution)/shard_map/ppermute | solution.py:38
  283.1 24.2 %collective-permute-start.28 = (bf16[384,768]{1,0:T(8,128)(2,1)S(1)}, bf16[384,768]{1,0:T(8,128)(2,1)S(1)}, u32[]{:S(2)}, u32[]{:S(2)}) collective-permute-start(bf16[384,768]{1,0:T(8,128)(2,1)S(1)} %copy-done.22), channel_id=1, source_target_pairs={{0,2},{1,3},{2,0},{3,1},{4,6},{5,7},{6,4},{7,5},{8,10},{9,11},{10,... | collective-permute-start | bytes 1769480 | tf_op jit(solution)/shard_map/ppermute | solution.py:38
  284.0 7.2 %collective-permute-start.22 = (bf16[48,1280]{1,0:T(8,128)(2,1)S(1)}, bf16[48,1280]{1,0:T(8,128)(2,1)S(1)}, u32[]{:S(2)}, u32[]{:S(2)}) collective-permute-start(bf16[48,1280]{1,0:T(8,128)(2,1)S(1)} %add_convert_fusion.16), channel_id=1, source_target_pairs={{0,16},{4,20},{8,24},{12,28},{16,0},{20,4},{24,8},{28,12},{1,17},{... | collective-permute-start | bytes 368648 | tf_op jit(solution)/shard_map/ppermute | solution.py:38
  291.2 4.9 %collective-permute-start.23 = (bf16[48,1280]{1,0:T(8,128)(2,1)S(1)}, bf16[48,1280]{1,0:T(8,128)(2,1)S(1)}, u32[]{:S(2)}, u32[]{:S(2)}) collective-permute-start(bf16[48,1280]{1,0:T(8,128)(2,1)S(1)} %add_convert_fusion.15), channel_id=1, source_target_pairs={{0,8},{4,12},{8,0},{12,4},{16,24},{20,28},{24,16},{28,20},{1,9},{5... | collective-permute-start | bytes 368648 | tf_op jit(solution)/shard_map/ppermute | solution.py:38
  296.2 6.3 %collective-permute-start.24 = (bf16[96,1280]{1,0:T(8,128)(2,1)S(1)}, bf16[96,1280]{1,0:T(8,128)(2,1)S(1)}, u32[]{:S(2)}, u32[]{:S(2)}) collective-permute-start(bf16[96,1280]{1,0:T(8,128)(2,1)S(1)} %pad_maximum_fusion.3), channel_id=1, source_target_pairs={{0,4},{4,0},{8,12},{12,8},{16,20},{20,16},{24,28},{28,24},{1,5},{5... | collective-permute-start | bytes 737288 | tf_op jit(solution)/shard_map/ppermute | solution.py:38
  (19 other events, 77.5 us)

commit v3 on v2

--- a/solution.py
+++ b/solution.py
@@ -464,18 +464,38 @@
     return run
 
 
-def expert_call(rows, grads, expert_in, expert_out, experts):
+def upstream_call(grads, expert_out):
+    count, width = grads.shape
+    hidden_width = expert_out.shape[0]
+    step_width = 512
+
+    def kernel(g_ref, out_ref, up_ref):
+        up_ref[...] = mm_t(g_ref[...], out_ref[...])
+
+    return pl.pallas_call(
+        kernel,
+        grid=(hidden_width // step_width,),
+        in_specs=[whole_spec((count, width)), pl.BlockSpec((step_width, width), lambda s: (s, 0))],
+        out_specs=pl.BlockSpec((count, step_width), lambda s: (0, s)),
+        out_shape=shape_of((count, hidden_width), f32),
+        compiler_params=params(),
+        cost_estimate=cost(2 * count * width * hidden_width, 6 * count * hidden_width),
+        name="upstream",
+    )(grads, expert_out)
+
+
+def expert_call(rows, grads, upstream, expert_in, expert_out, experts):
     count, width = rows.shape
     capacity = count // experts
     stride = capacity + extra_rows
     hidden_width = expert_in.shape[1]
     step_width = 512
-    chunk_rows = 256
+    chunk_rows = count
     steps = hidden_width // step_width
     half_root = math.sqrt(0.5)
     density = 1.0 / math.sqrt(2.0 * math.pi)
 
-    def kernel(x_ref, g_ref, in_ref, out_ref, active_ref, gh_ref, made_ref, back_ref, made_sum, back_sum):
+    def kernel(x_ref, g_ref, up_ref, in_ref, out_ref, active_ref, gh_ref, made_ref, back_ref, made_sum, back_sum):
         step = pl.program_id(0)
 
         @pl.when(step == 0)
@@ -487,11 +507,10 @@
         def chunk(index):
             at = pl.ds(pl.multiple_of(index * chunk_rows, chunk_rows), chunk_rows)
             hidden = mm(x_ref[at, :], in_ref[...])
-            upstream = mm_t(g_ref[at, :], out_ref[...])
             share = 0.5 + 0.5 * lax.erf(hidden * half_root)
             active = (hidden * share).astype(bf16)
             slope = share + hidden * (jnp.exp(hidden * hidden * -0.5) * density)
-            grad_hidden = (upstream * slope).astype(bf16)
+            grad_hidden = (up_ref[at, :] * slope).astype(bf16)
             active_ref[at, :] = active
             gh_ref[at, :] = grad_hidden
             made_sum[at, :] += mm(active, out_ref[...])
@@ -524,6 +543,7 @@
         in_specs=[
             full,
             full,
+            pl.BlockSpec((count, step_width), lambda s: (0, s)),
             pl.BlockSpec((width, step_width), lambda s: (0, s)),
             pl.BlockSpec((step_width, width), lambda s: (s, 0)),
         ],
@@ -543,7 +563,7 @@
         compiler_params=params(),
         cost_estimate=cost(8 * count * width * hidden_width, 8 * width * hidden_width),
         name="experts",
-    )(rows, grads, expert_in, expert_out)
+    )(rows, grads, upstream, expert_in, expert_out)
 
 
 def offset_place(offsets, step, me_ref):
@@ -860,12 +880,14 @@
     )(chain1, chain2, *weights, gain[None, :])
 
 
-def gather_blocks(value, axis_size):
+def gather_blocks(value, axis_size, late=None):
     blocks = {0: value}
     bit = 2
     while bit < axis_size:
         for offset in sorted(blocks):
             blocks[offset | bit] = swap(blocks[offset], "fsdp", axis_size, bit)
+            if late is not None:
+                blocks[offset | bit] = ordered(blocks[offset | bit], late)[0]
         bit *= 2
     for offset in sorted(blocks):
         blocks[offset | 1] = swap(blocks[offset], "fsdp", axis_size, 1)
@@ -1006,7 +1028,7 @@
             jnp.stack([attn_gain, ffn_gain]), bias_table, w_router.T, small_rows, width,
         )
         blocks = gather_blocks(packed, count)
-        out_blocks = gather_blocks(ordered(w_output, blocks[-2])[0], count)
+        leaving_output = ordered(w_output, blocks[-2])[0]
         routes, blocks[1] = ordered(routes, blocks[1])
         padded_buckets = jnp.concatenate([jnp.full((seq,), -1, jnp.int32), buckets])
         bucket_window = lax.dynamic_slice_in_dim(
@@ -1023,12 +1045,14 @@
         (queries, keys, values, normed, sequence, wq, wk, wv, smalls, bias, mask) = project_call(
             me, blocks, shards, small_rows, bucket_window, heads, bucket_count, experts
         )
+        out_blocks = gather_blocks(leaving_output, count, queries)
         queries, grad_rows_in, others = ordered(queries, grad_rows_in, others)
         context, lse = attend_call(queries, keys, values, bias, mask, head_dim)
         wo, context_low, residual, ffn_low, gates, rows_out = dispatch_call(
             me, context, out_blocks, tokens_in, smalls, routes, slot_map, heads
         )(experts)
         normed_t = ordered(normed, rows_out)[0].T
+        upstream = upstream_call(ordered(grad_rows_in, rows_out)[0], w_out[0])
         rows_in = lax.all_to_all(
             rows_out.reshape(experts, capacity, width),
             "expert",
@@ -1036,9 +1060,9 @@
             concat_axis=0,
             tiled=True,
         ).reshape(slots, width)
-        rows_in, normed_t = ordered(rows_in, normed_t)
+        rows_in, normed_t, upstream = ordered(rows_in, normed_t, upstream)
         active, grad_hidden, made, row_grads = expert_call(
-            rows_in, grad_rows_in, w_in[0], w_out[0], experts
+            rows_in, grad_rows_in, upstream, w_in[0], w_out[0], experts
         )
         row_grads_back = lax.all_to_all(
             row_grads, "expert", split_axis=0, concat_axis=0, tiled=True
@@ -1091,19 +1115,25 @@
         )
         give2, keep2 = second_grads_call(me, *part2, normed_t, table2, count)
         sum1 = far_sum(pieces1, count, None, give2)
-        rows_give, rows_keep = rows_back_call(me, part1, part2, (wq, wk, wv), count)
-        sum2 = far_sum(core_sum(give2, keep2, count), count)
+        pieces2 = core_sum(give2, keep2, count)
+        last = max(pieces2)
+        dv2, pieces2[last] = ordered(part2[2], pieces2[last])
+        rows_give, rows_keep = rows_back_call(
+            me, part1, (part2[0], part2[1], dv2), (wq, wk, wv), count
+        )
+        steps2 = far_steps(pieces2, count, (9, 3))
+        sum2 = steps2.send(steps2.send(ordered(next(steps2), rows_give)[0]))
         arrived = in_steps.send(ordered(arrived, sum1)[0])
         in_sum = in_steps.send(arrived)
+        grad_normed = far_sum(core_sum(rows_give, rows_keep, count), count, sum2)
+        arrived, _ = ordered(arrived, sum2)
         out_steps = far_steps(out_pieces, count, (6, 6), arrived)
-        arrived = out_steps.send(ordered(next(out_steps), sum2)[0])
-        out_sum = out_steps.send(arrived)
+        out_sum = out_steps.send(out_steps.send(ordered(next(out_steps), grad_normed)[0]))
         grad_shards = [in_sum, out_sum]
         chain1, _ = all_sum_expert(sum1, expert_ranks, expert_index)
         chain2, first_arrived = all_sum_expert(sum2, expert_ranks, expert_index)
         half_cols = near * tile
 
-        grad_normed = far_sum(core_sum(rows_give, rows_keep, count), count, sum2)
         inputs = tokens_in.astype(f32)
         inverse = lax.rsqrt(jnp.mean(inputs * inputs, axis=-1, keepdims=True) + eps)
         gain_attn = smalls[experts + heads]

time: 311 us -> 326 us (1.048)
  waiting for transfers between devices: 101 us -> 86.6 us
  starting transfers between devices: 51 us -> 64.7 us
  Pallas kernels: 116 us -> 122 us
  other arithmetic: 18.8 us -> 23.7 us
    all_to_all x1, starting transfers between devices: 3.9 us -> 14.4 us  [per_device(): lax.all_to_all(row_grads, 'expert', split_axis=0, concat_axis=0, tiled=True)]
    all_to_all x1, waiting for transfers between devices: 27.6 us -> 18 us  [per_device(): lax.all_to_all(rows_out.reshape(experts, capacity, width), 'expert', spli...]
    pallas_call x0 -> x1, Pallas kernels: none -> 9.47 us  [upstream_call(): pl.pallas_call(kernel, grid=(hidden_width // step_width,), in_specs=[whol...]
    ppermute x29 -> x30, waiting for transfers between devices: 59.7 us -> 54.5 us  [swap(): lax.ppermute(value, axis_name, [(i, i ^ bit) for i in range(axis_size)])]
    ppermute x29 -> x30, starting transfers between devices: 29.5 us -> 33.1 us  [swap(): lax.ppermute(value, axis_name, [(i, i ^ bit) for i in range(axis_size)])]
    pallas_call x1, Pallas kernels: 23.4 us -> 19.9 us  [expert_call(): pl.pallas_call(kernel, grid=(steps,), in_specs=[full, full, pl.BlockSpec(...]
    unnamed x74 -> x78, local copies, waits for them, and re-layouts: 6.08 us -> 6.78 us
  transfers between devices with their start and end apart: 33 -> 34, of which waited for: 18 -> 18; matrix products, arithmetic and copies ran while one was open for 9% -> 11% of each run, Pallas kernels for 28% -> 30%
where the time goes in v3:
time: 326 us; the launch traced here: 322 us
  Pallas kernels  122 us (37%)
  waiting for transfers between devices  86.6 us (27%)
  starting transfers between devices  64.7 us (20%)
  other arithmetic  23.7 us (7%)
  local copies, waits for them, and re-layouts  21.7 us (7%)
    ppermute x30, waiting for transfers between devices, swap(): lax.ppermute(value, axis_name, [(i, i ^ bit) for i in range(axis_size)])  54.5 us
    ppermute x30, starting transfers between devices, swap(): lax.ppermute(value, axis_name, [(i, i ^ bit) for i in range(axis_size)])  33.1 us
    pallas_call x1, Pallas kernels, expert_call(): pl.pallas_call(kernel, grid=(steps,), in_specs=[full, full, pl.BlockSpec(...  19.9 us
    all_to_all x1, waiting for transfers between devices, per_device(): lax.all_to_all(rows_out.reshape(experts, capacity, width), 'expert', spli...  18 us
    pallas_call x2, Pallas kernels, attend_back_call(): pl.pallas_call(kernel, grid=(pairs,), in_specs=[narrow, tall, tall, pl.Bl...  17 us
    pallas_call x1, Pallas kernels, expert_grads_call(): pl.pallas_call(kernel, grid_spec=pltpu.PrefetchScalarGridSpec(num_scalar_...  16.2 us
    all_to_all x1, starting transfers between devices, per_device(): lax.all_to_all(row_grads, 'expert', split_axis=0, concat_axis=0, tiled=True)  14.4 us
    all_to_all x1, waiting for transfers between devices, per_device(): lax.all_to_all(row_grads, 'expert', split_axis=0, concat_axis=0, tiled=True)  13.9 us
  transfers between devices with their start and end apart: 34, of which 18 were waited for; matrix products, arithmetic and copies ran while one was open for 11% of the time, Pallas kernels for 30%

profile of v3, /device:TPU:0, one launch (start us, length us, event | category | flops | bytes accessed | tf_op | source)
XLA Modules:
  0.0 322.4 jit_solution(5850943700562808104)
XLA Ops:
  3.2 2.6 pack.1.refs_0_
  6.2 2.5 collective-permute-start.1
  10.1 3.5 %route.1 = (bf16[768,256]{1,0:T(8,128)(2,1)}, bf16[256,768]{1,0:T(8,128)(2,1)}, bf16[256,768]{1,0:T(8,128)(2,1)}, bf16[8,112,768]{2,1,0:T(8,128)(2,1)}, f32[256,2]{1,0:T(8,128)}) custom-call(s32[256,2]{1,0:T(8,128)} %copy.33.refs_0_.refs_6_.routes_ref, bf16[256,768]{1,0:T(8,128)(2,1)} %cot_ref.1), custom_call_target="tpu_custom_call" | custom-call | flops 1179648 | bytes 9216 | tf_op jit(solution)/shard_map/route/pallas_call | solution.py:102
  13.6 7.2 %all-to-all-start = ((bf16[8,112,768]{2,1,0:T(8,128)(2,1)}), bf16[8,112,768]{2,1,0:T(8,128)(2,1)S(1)}, u32[]{:S(2)}, u32[]{:S(2)}) async-start(bf16[8,112,768]{2,1,0:T(8,128)(2,1)} %get-tuple-element.105), calls=%async_computation | async-start | bytes 2752512 | tf_op jit(solution)/shard_map/all_to_all | solution.py:1039
  20.8 18.1 %collective-permute-done.1.refs_2_ = bf16[864,768]{1,0:T(8,128)(2,1)} collective-permute-done((bf16[864,768]{1,0:T(8,128)(2,1)}, bf16[864,768]{1,0:T(8,128)(2,1)}, u32[]{:S(2)}, u32[]{:S(2)}) %collective-permute-start.1) | collective-permute-done | bytes 1327136 | tf_op jit(solution)/shard_map/ppermute | solution.py:38
  38.9 1.7 collective-permute-start.4
  43.2 10.1 %project.1 = (bf16[256,768]{1,0:T(8,128)(2,1)}, bf16[1024,768]{1,0:T(8,128)(2,1)}, bf16[1024,768]{1,0:T(8,128)(2,1)}, bf16[1024,768]{1,0:T(8,128)(2,1)}, bf16[10...) custom-call(s32[2]{0:T(128)} %pad_add_fusion.me_ref, ...), custom_call_target="tpu_custom_call" | custom-call | flops 10616832 | bytes 61440 | tf_op jit(solution)/shard_map/project/pallas_call | solution.py:202
  55.7 10.2 %attend.1 = (f32[256,768]{1,0:T(8,128)}, f32[12,1,256]{2,1,0:T(1,128)}) custom-call(bf16[256,768]{1,0:T(8,128)(2,1)} %get-tuple-element.106.q_ref, bf16[1024,768]{1,0:T(8,128)(2,1)} %get-tuple-element.107.k_ref, bf16[1024,768]{1,0:T(8,128)(2,1)} %get-tuple-element.108.v_ref, f32[12,1,1280]{2,1,0:T(1,128)} %get-tuple-element.109.bias_ref, ...), custom_call_target="tpu_custom_call" | custom-call | flops 25165824 | bytes 12288 | tf_op jit(solution)/shard_map/attend/pallas_call | solution.py:268
  66.6 4.2 %dispatch.1 = (bf16[768,768]{1,0:T(8,128)(2,1)}, bf16[256,768]{1,0:T(8,128)(2,1)}, f32[256,768]{1,0:T(8,128)}, bf16[256,768]{1,0:T(8,128)(2,1)}, f32[256,2]{1,0:T(8,128)}, /*index=5*/bf16[768,768]{1,0:T(8,128)(2,1)}) custom-call(s32[2]{0:T(128)} %pad_add_fusion.me_ref, f32[256,768]{1,0:T(8,128)} %get-tuple-element.111.ctx_ref, bf16[192,768]{1,0:T(8,128)(2,1)} %refs_0_, ...), custom_call_target="tpu_custom_call" | custom-call | flops 2359296 | bytes 18432 | tf_op jit(solution)/shard_map/dispatch/pallas_call | solution.py:448
  70.8 5.9 %all-to-all-start.1 = ((bf16[8,96,768]{2,1,0:T(8,128)(2,1)}), bf16[8,96,768]{2,1,0:T(8,128)(2,1)S(1)}, u32[]{:S(2)}, u32[]{:S(2)}) async-start(bf16[8,96,768]{2,1,0:T(8,128)(2,1)} %bitcast.69), calls=%async_computation.1 | async-start | bytes 2359296 | tf_op jit(solution)/shard_map/all_to_all | solution.py:1056
  76.7 1.6 copy.35
  78.3 9.5 %upstream.1.up_ref = f32[768,3072]{1,0:T(8,128)} custom-call(bf16[768,768]{1,0:T(8,128)(2,1)} %bitcast.61, bf16[3072,768]{1,0:T(8,128)(2,1)} %bitcast.59), custom_call_target="tpu_custom_call" | custom-call | flops 14155776 | bytes 55296 | tf_op jit(solution)/shard_map/upstream/pallas_call | solution.py:475
  87.8 18.0 %all-to-all-done.1 = bf16[8,96,768]{2,1,0:T(8,128)(2,1)S(1)} async-done(((bf16[8,96,768]{2,1,0:T(8,128)(2,1)}), bf16[8,96,768]{2,1,0:T(8,128)(2,1)S(1)}, u32[]{:S(2)}, u32[]{:S(2)}) %all-to-all-start.1) | async-done | bytes 1179680 | tf_op jit(solution)/shard_map/all_to_all | solution.py:1056
  106.8 19.9 %experts.1 = (bf16[768,3072]{1,0:T(8,128)(2,1)}, bf16[768,3072]{1,0:T(8,128)(2,1)}, bf16[768,768]{1,0:T(8,128)(2,1)}, bf16[8,112,768]{2,1,0:T(8,128)(2,1)}) custom-call(bf16[768,768]{1,0:T(8,128)(2,1)} %bitcast.56, bf16[768,768]{1,0:T(8,128)(2,1)} %bitcast.62, f32[768,3072]{1,0:T(8,128)} %upstream.1.up_ref, bf16[768,3072]{1,0:T(8,128)(2,1)} %bitcast.68, ...), custom_call_target="tpu_custom_call" | custom-call | flops 56623104 | bytes 73728 | tf_op jit(solution)/shard_map/experts/pallas_call | solution.py:540
  126.7 14.4 %all-to-all-start.2 = ((bf16[8,112,768]{2,1,0:T(8,128)(2,1)}), bf16[8,112,768]{2,1,0:T(8,128)(2,1)S(1)}, u32[]{:S(2)}, u32[]{:S(2)}) async-start(bf16[8,112,768]{2,1,0:T(8,128)(2,1)} %get-tuple-element.133), calls=%async_computation.2 | async-start | bytes 2752512 | tf_op jit(solution)/shard_map/all_to_all | solution.py:1067
  143.9 16.2 %expert_grads.1 = (bf16[2,192,3072]{2,1,0:T(8,128)(2,1)}, bf16[2,192,3072]{2,1,0:T(8,128)(2,1)}, bf16[2,768,768]{2,1,0:T(8,128)(2,1)}, bf16[2,768,768]{2,1,0:T(8,128)(2,1)}) custom-call(s32[2]{0:T(128)} %pad_add_fusion.me_ref, bf16[768,768]{1,0:T(8,128)(2,1)} %copy.36.xt_ref, bf16[768,768]{1,0:T(8,128)(2,1)} %bitcast.57, bf16[768,768]{1,0:T(8,128)(2,1)} %bitcast.63, ...), custom_call_target="tpu_custom_call" | custom-call | flops 28311552 | bytes 73728 | tf_op jit(solution)/shard_map/expert_grads/pallas_call | solution.py:625
  160.1 13.9 %all-to-all-done.2.rows_ref = bf16[8,112,768]{2,1,0:T(8,128)(2,1)S(1)} async-done(((bf16[8,112,768]{2,1,0:T(8,128)(2,1)}), bf16[8,112,768]{2,1,0:T(8,128)(2,1)S(1)}, u32[]{:S(2)}, u32[]{:S(2)}) %all-to-all-start.2) | async-done | bytes 1376288 | tf_op jit(solution)/shard_map/all_to_all | solution.py:1067
  175.0 5.9 %combine.1 = (f32[256,768]{1,0:T(8,128)}, bf16[256,768]{1,0:T(8,128)(2,1)}, bf16[256,768]{1,0:T(8,128)(2,1)}, f32[8,768]{1,0:T(8,128)}, f32[1,768]{1,0:T(1,128)}) custom-call(bf16[8,112,768]{2,1,0:T(8,128)(2,1)} %copy-done.3, f32[256,2]{1,0:T(8,128)} %get-tuple-element.135.place_ref, f32[256,2]{1,0:T(8,128)} %get-tuple-element.117.gate_ref, ...), custom_call_target="tpu_custom_call" | custom-call | flops 3538944 | bytes 18432 | tf_op jit(solution)/shard_map/combine/pallas_call | solution.py:706
  182.4 1.6 collective-permute-start.7
  184.0 8.5 %attend_back.2 = (bf16[256,384]{1,0:T(8,128)(2,1)}, bf16[1024,384]{1,0:T(8,128)(2,1)}, bf16[1024,384]{1,0:T(8,128)(2,1)}, f32[6,1,32]{2,1,0:T(1,128)}) custom-call(bf16[256,768]{1,0:T(8,128)(2,1)} %get-tuple-element.106.q_ref, bf16[1024,768]{1,0:T(8,128)(2,1)} %get-tuple-element.107.k_ref, bf16[1024,768]{1,0:T(8,128)(2,1)} %get-tuple-element.108.v_ref, ...), custom_call_target="tpu_custom_call" | custom-call | flops 31457280 | bytes 12288 | tf_op jit(solution)/shard_map/attend_back/pallas_call | solution.py:365
  192.5 2.5 collective-permute-done.7
  195.0 6.5 %first_grads.1 = (bf16[2,192,2048]{2,1,0:T(8,128)(2,1)}, bf16[2,192,2048]{2,1,0:T(8,128)(2,1)}) custom-call(s32[2]{0:T(128)} %pad_add_fusion.me_ref, bf16[256,384]{1,0:T(8,128)(2,1)} %get-tuple-element.144.dq_ref.dq1_ref, bf16[1024,384]{1,0:T(8,128)(2,1)} %get-tuple-element.145.dk_ref.dk1_ref, bf16[1024,384]{1,0:T(8,128)(2,1)} %get-tuple-element.146.dv_ref.dv1_ref, ...), custom_call_target="tpu_custom_call" | custom-call | flops 5898240 | bytes 30720 | tf_op jit(solution)/shard_map/first_grads/pallas_call | solution.py:773
  201.6 1.6 collective-permute-start.9
  203.2 2.1 collective-permute-done.8
  205.3 2.7 fusion.5
  208.0 3.1 collective-permute-done.9
  217.4 4.2 %all-to-all-start.3 = ((bf16[8,96,768]{2,1,0:T(8,128)(2,1)}), bf16[8,96,768]{2,1,0:T(8,128)(2,1)S(1)}, u32[]{:S(2)}, u32[]{:S(2)}) async-start(bf16[8,96,768]{2,1,0:T(8,128)(2,1)} %bitcast.12), calls=%async_computation.3 | async-start | bytes 2359296 | tf_op jit(solution)/shard_map/all_to_all | solution.py:1102
  221.6 8.5 %attend_back.3 = (bf16[256,384]{1,0:T(8,128)(2,1)}, bf16[1024,384]{1,0:T(8,128)(2,1)}, bf16[1024,384]{1,0:T(8,128)(2,1)}, f32[6,1,32]{2,1,0:T(1,128)}) custom-call(bf16[256,768]{1,0:T(8,128)(2,1)} %get-tuple-element.106.q_ref, bf16[1024,768]{1,0:T(8,128)(2,1)} %get-tuple-element.107.k_ref, bf16[1024,768]{1,0:T(8,128)(2,1)} %get-tuple-element.108.v_ref, ...), custom_call_target="tpu_custom_call" | custom-call | flops 31457280 | bytes 12288 | tf_op jit(solution)/shard_map/attend_back/pallas_call | solution.py:365
  230.1 5.5 %second_grads.1 = (bf16[2,192,1280]{2,1,0:T(8,128)(2,1)}, bf16[2,192,1280]{2,1,0:T(8,128)(2,1)}) custom-call(s32[2]{0:T(128)} %pad_add_fusion.me_ref, bf16[256,384]{1,0:T(8,128)(2,1)} %get-tuple-element.159.dq_ref.dq2_ref, bf16[1024,384]{1,0:T(8,128)(2,1)} %get-tuple-element.160.dk_ref.dk2_ref, bf16[1024,384]{1,0:T(8,128)(2,1)} %get-tuple-element.166.dv_ref.dv2_ref, ...), custom_call_target="tpu_custom_call" | custom-call | flops 5898240 | bytes 30720 | tf_op jit(solution)/shard_map/second_grads/pallas_call | solution.py:818
  235.6 1.8 convert_add_fusion.2
  238.3 2.0 collective-permute-start.16
  240.3 1.5 collective-permute-start.26
  244.0 8.1 %rows_back.1 = (bf16[2,256,768]{2,1,0:T(8,128)(2,1)}, bf16[2,256,768]{2,1,0:T(8,128)(2,1)}) custom-call(s32[2]{0:T(128)} %pad_add_fusion.me_ref, bf16[256,384]{1,0:T(8,128)(2,1)} %get-tuple-element.144.dq_ref.dq1_ref, bf16[1024,384]{1,0:T(8,128)(2,1)} %get-tuple-element.145.dk_ref.dk1_ref, bf16[1024,384]{1,0:T(8,128)(2,1)} %get-tuple-element.146.dv_ref.dv1_ref, ...), custom_call_target="tpu_custom_call" | custom-call | flops 23592960 | bytes 30720 | tf_op jit(solution)/shard_map/rows_back/pallas_call | solution.py:847
  253.5 2.0 collective-permute-start.17
  255.5 3.0 convert_add_fusion.1
  259.7 1.5 collective-permute-start.12
  261.3 2.6 collective-permute-start.18
  269.4 3.2 collective-permute-done.18
  274.0 1.9 collective-permute-start.22
  275.9 5.1 %collective-permute-done.19 = bf16[48,2048]{1,0:T(8,128)(2,1)S(1)} collective-permute-done((bf16[48,2048]{1,0:T(8,128)(2,1)S(1)}, bf16[48,2048]{1,0:T(8,128)(2,1)S(1)}, u32[]{:S(2)}, u32[]{:S(2)}) %collective-permute-start.19) | collective-permute-done | bytes 196640 | tf_op jit(solution)/shard_map/ppermute | solution.py:38
  282.4 2.8 collective-permute-start.23
  286.4 4.3 %collective-permute-done.23 = bf16[48,1280]{1,0:T(8,128)(2,1)S(1)} collective-permute-done((bf16[48,1280]{1,0:T(8,128)(2,1)S(1)}, bf16[48,1280]{1,0:T(8,128)(2,1)S(1)}, u32[]{:S(2)}, u32[]{:S(2)}) %collective-permute-start.23) | collective-permute-done | bytes 122912 | tf_op jit(solution)/shard_map/ppermute | solution.py:38
  292.6 1.6 collective-permute-start.14
  299.5 3.8 %collective-permute-done.14 = bf16[256,768]{1,0:T(8,128)(2,1)S(1)} collective-permute-done((bf16[256,768]{1,0:T(8,128)(2,1)S(1)}, bf16[256,768]{1,0:T(8,128)(2,1)S(1)}, u32[]{:S(2)}, u32[]{:S(2)}) %collective-permute-start.14) | collective-permute-done | bytes 393248 | tf_op jit(solution)/shard_map/ppermute | solution.py:38
  304.7 1.6 collective-permute-start.29
  308.4 3.1 finish.1
  312.2 6.6 %collective-permute-done.29 = bf16[384,768]{1,0:T(8,128)(2,1)S(1)} collective-permute-done((bf16[384,768]{1,0:T(8,128)(2,1)S(1)}, bf16[384,768]{1,0:T(8,128)(2,1)S(1)}, u32[]{:S(2)}, u32[]{:S(2)}) %collective-permute-start.29) | collective-permute-done | bytes 589856 | tf_op jit(solution)/shard_map/ppermute | solution.py:38
  318.8 3.2 convert_add_fusion
  (176 shorter events, 48.8 us)
Async XLA Ops:
  0.6 8.5 %copy-start.35 = (s32[256,2]{0,1:T(2,128)S(1)}, s32[256,2]{0,1:T(2,128)}, u32[]{:S(2)}) copy-start(s32[256,2]{0,1:T(2,128)} %param.17) | copy-start | bytes 6148
  2.0 11.6 %copy-start.33 = (bf16[1,192]{1,0:T(2,128)(2,1)}, bf16[1,192]{1,0:T(2,128)(2,1)S(1)}, u32[]{:S(2)}) copy-start(bf16[1,192]{1,0:T(2,128)(2,1)S(1)} %stack.21.gain_ref) | copy-start | bytes 1156
  5.8 3.3 %collective-permute-start = (bf16[864,768]{1,0:T(8,128)(2,1)}, bf16[864,768]{1,0:T(8,128)(2,1)S(1)}, u32[]{:S(2)}, u32[]{:S(2)}) collective-permute-start(bf16[864,768]{1,0:T(8,128)(2,1)} %pack.1.refs_0_), channel_id=1, source_target_pairs={{0,1},{1,0},{2,3},{3,2},{4,5},{5,4},{6,7},{7,6},{8,9},{9,8},{10,11... | collective-permute-start | bytes 3981320 | tf_op jit(solution)/shard_map/ppermute | solution.py:38
  6.2 32.6 %collective-permute-start.1 = (bf16[864,768]{1,0:T(8,128)(2,1)}, bf16[864,768]{1,0:T(8,128)(2,1)}, u32[]{:S(2)}, u32[]{:S(2)}) collective-permute-start(bf16[864,768]{1,0:T(8,128)(2,1)} %pack.1.refs_0_), channel_id=1, source_target_pairs={{0,2},{1,3},{2,0},{3,1},{4,6},{5,7},{6,4},{7,5},{8,10},{9,11},{10,... | collective-permute-start | bytes 3981320 | tf_op jit(solution)/shard_map/ppermute | solution.py:38
  10.1 28.8 %copy-start.27 = (bf16[192,768]{1,0:T(8,128)(2,1)S(1)}, bf16[192,768]{1,0:T(8,128)(2,1)}, u32[]{:S(2)}) copy-start(bf16[192,768]{1,0:T(8,128)(2,1)} %refs_0_) | copy-start | bytes 884740
  10.1 30.5 %copy-start.34 = (s32[1024]{0:T(1024)S(1)}, s32[1024]{0:T(1024)}, u32[]{:S(2)}) copy-start(s32[1024]{0:T(1024)} %param.18) | copy-start | bytes 12292
  13.6 40.3 %all-to-all-start = ((bf16[8,112,768]{2,1,0:T(8,128)(2,1)}), bf16[8,112,768]{2,1,0:T(8,128)(2,1)S(1)}, u32[]{:S(2)}, u32[]{:S(2)}) async-start(bf16[8,112,768]{2,1,0:T(8,128)(2,1)} %get-tuple-element.105), calls=%async_computation | async-start | bytes 2752512 | tf_op jit(solution)/shard_map/all_to_all | solution.py:1039
  38.9 3.3 %collective-permute-start.2 = (bf16[864,768]{1,0:T(8,128)(2,1)}, bf16[864,768]{1,0:T(8,128)(2,1)S(1)}, u32[]{:S(2)}, u32[]{:S(2)}) collective-permute-start(bf16[864,768]{1,0:T(8,128)(2,1)} %collective-permute-done.1.refs_2_), channel_id=1, source_target_pairs={{0,1},{1,0},{2,3},{3,2},{4,5},{5,4},{6,7},{7,6},{8,9},{9,8},{10,11... | collective-permute-start | bytes 3981320 | tf_op jit(solution)/shard_map/ppermute | solution.py:38
  38.9 14.5 %collective-permute-start.4 = (bf16[192,768]{1,0:T(8,128)(2,1)S(1)}, bf16[192,768]{1,0:T(8,128)(2,1)S(1)}, u32[]{:S(2)}, u32[]{:S(2)}) collective-permute-start(bf16[192,768]{1,0:T(8,128)(2,1)S(1)} %copy-done.27), channel_id=1, source_target_pairs={{0,2},{1,3},{2,0},{3,1},{4,6},{5,7},{6,4},{7,5},{8,10},{9,11},{10,... | collective-permute-start | bytes 884744 | tf_op jit(solution)/shard_map/ppermute | solution.py:38
  41.3 24.6 %collective-permute-start.3 = (bf16[192,768]{1,0:T(8,128)(2,1)S(1)}, bf16[192,768]{1,0:T(8,128)(2,1)}, u32[]{:S(2)}, u32[]{:S(2)}) collective-permute-start(bf16[192,768]{1,0:T(8,128)(2,1)S(1)} %copy-done.27), channel_id=1, source_target_pairs={{0,1},{1,0},{2,3},{3,2},{4,5},{5,4},{6,7},{7,6},{8,9},{9,8},{10,11... | collective-permute-start | bytes 884744 | tf_op jit(solution)/shard_map/ppermute | solution.py:38
  53.3 12.5 %copy-start.30 = (bf16[192,768]{1,0:T(8,128)(2,1)}, bf16[192,768]{1,0:T(8,128)(2,1)S(1)}, u32[]{:S(2)}) copy-start(bf16[192,768]{1,0:T(8,128)(2,1)S(1)} %collective-permute-done.4.refs_2_) | copy-start | bytes 884740
  53.4 12.5 %collective-permute-start.5 = (bf16[192,768]{1,0:T(8,128)(2,1)S(1)}, bf16[192,768]{1,0:T(8,128)(2,1)S(1)}, u32[]{:S(2)}, u32[]{:S(2)}) collective-permute-start(bf16[192,768]{1,0:T(8,128)(2,1)S(1)} %collective-permute-done.4.refs_2_), channel_id=1, source_target_pairs={{0,1},{1,0},{2,3},{3,2},{4,5},{5,4},{6,7},{7,6},{8,9},{9,8},{10,11... | collective-permute-start | bytes 884744 | tf_op jit(solution)/shard_map/ppermute | solution.py:38
  70.8 35.0 %all-to-all-start.1 = ((bf16[8,96,768]{2,1,0:T(8,128)(2,1)}), bf16[8,96,768]{2,1,0:T(8,128)(2,1)S(1)}, u32[]{:S(2)}, u32[]{:S(2)}) async-start(bf16[8,96,768]{2,1,0:T(8,128)(2,1)} %bitcast.69), calls=%async_computation.1 | async-start | bytes 2359296 | tf_op jit(solution)/shard_map/all_to_all | solution.py:1056
  126.7 15.7 %copy-start.1 = (bf16[8,96,768]{2,1,0:T(8,128)(2,1)S(1)}, bf16[8,96,768]{2,1,0:T(8,128)(2,1)}, u32[]{:S(2)}) copy-start(bf16[8,96,768]{2,1,0:T(8,128)(2,1)} %copy-done) | copy-start | bytes 3538948
  126.7 47.2 %all-to-all-start.2 = ((bf16[8,112,768]{2,1,0:T(8,128)(2,1)}), bf16[8,112,768]{2,1,0:T(8,128)(2,1)S(1)}, u32[]{:S(2)}, u32[]{:S(2)}) async-start(bf16[8,112,768]{2,1,0:T(8,128)(2,1)} %get-tuple-element.133), calls=%async_computation.2 | async-start | bytes 2752512 | tf_op jit(solution)/shard_map/all_to_all | solution.py:1067
  173.9 7.1 %collective-permute-start.6 = (bf16[2,192,3072]{2,1,0:T(8,128)(2,1)}, bf16[2,192,3072]{2,1,0:T(8,128)(2,1)S(1)}, u32[]{:S(2)}, u32[]{:S(2)}) collective-permute-start(bf16[2,192,3072]{2,1,0:T(8,128)(2,1)} %get-tuple-element.140), channel_id=1, source_target_pairs={{0,1},{1,0},{2,3},{3,2},{4,5},{5,4},{6,7},{7,6},{8,9},{9,8},{10,11... | collective-permute-start | bytes 7077896 | tf_op jit(solution)/shard_map/ppermute | solution.py:38
  182.4 12.6 %collective-permute-start.7 = (bf16[80,3072]{1,0:T(8,128)(2,1)S(1)}, bf16[80,3072]{1,0:T(8,128)(2,1)S(1)}, u32[]{:S(2)}, u32[]{:S(2)}) collective-permute-start(bf16[80,3072]{1,0:T(8,128)(2,1)S(1)} %slice.146), channel_id=1, source_target_pairs={{0,2},{1,3},{2,0},{3,1},{4,6},{5,7},{6,4},{7,5},{8,10},{9,11},{10,... | collective-permute-start | bytes 1474568 | tf_op jit(solution)/shard_map/ppermute | solution.py:38
  184.0 30.3 %collective-permute-start.27 = (bf16[2,768,768]{2,1,0:T(8,128)(2,1)}, bf16[2,768,768]{2,1,0:T(8,128)(2,1)S(1)}, u32[]{:S(2)}, u32[]{:S(2)}) collective-permute-start(bf16[2,768,768]{2,1,0:T(8,128)(2,1)} %get-tuple-element.189), channel_id=1, source_target_pairs={{0,1},{1,0},{2,3},{3,2},{4,5},{5,4},{6,7},{7,6},{8,9},{9,8},{10,11... | collective-permute-start | bytes 7077896 | tf_op jit(solution)/shard_map/ppermute | solution.py:38
  201.5 3.8 %collective-permute-start.8 = (bf16[2,192,2048]{2,1,0:T(8,128)(2,1)}, bf16[2,192,2048]{2,1,0:T(8,128)(2,1)}, u32[]{:S(2)}, u32[]{:S(2)}) collective-permute-start(bf16[2,192,2048]{2,1,0:T(8,128)(2,1)} %get-tuple-element.153), channel_id=1, source_target_pairs={{0,1},{1,0},{2,3},{3,2},{4,5},{5,4},{6,7},{7,6},{8,9},{9,8},{10,11... | collective-permute-start | bytes 4718600 | tf_op jit(solution)/shard_map/ppermute | solution.py:38
  201.6 11.8 %copy-start.16 = (f32[256,2]{1,0:T(8,128)S(1)}, f32[256,2]{1,0:T(8,128)}, u32[]{:S(2)}) copy-start(f32[256,2]{1,0:T(8,128)} %get-tuple-element.117.gate_ref) | copy-start | bytes 6148
  201.6 9.5 %collective-permute-start.9 = (bf16[48,3072]{1,0:T(8,128)(2,1)S(1)}, bf16[48,3072]{1,0:T(8,128)(2,1)S(1)}, u32[]{:S(2)}, u32[]{:S(2)}) collective-permute-start(bf16[48,3072]{1,0:T(8,128)(2,1)S(1)} %slice.149), channel_id=1, source_target_pairs={{0,2},{1,3},{2,0},{3,1},{4,6},{5,7},{6,4},{7,5},{8,10},{9,11},{10,... | collective-permute-start | bytes 884744 | tf_op jit(solution)/shard_map/ppermute | solution.py:38
  205.3 9.1 %copy-start.5 = (bf16[2,768,768]{2,1,0:T(8,128)(2,1)S(1)}, bf16[2,768,768]{2,1,0:T(8,128)(2,1)}, u32[]{:S(2)}) copy-start(bf16[2,768,768]{2,1,0:T(8,128)(2,1)} %get-tuple-element.188) | copy-start | bytes 7077892
  211.1 24.6 %collective-permute-start.15 = (bf16[192,2048]{1,0:T(8,128)(2,1)}, bf16[192,2048]{1,0:T(8,128)(2,1)}, u32[]{:S(2)}, u32[]{:S(2)}) collective-permute-start(bf16[192,2048]{1,0:T(8,128)(2,1)} %fusion.5), channel_id=1, source_target_pairs={{0,2},{1,3},{2,0},{3,1},{4,6},{5,7},{6,4},{7,5},{8,10},{9,11},{10,... | collective-permute-start | bytes 2359304 | tf_op jit(solution)/shard_map/ppermute | solution.py:38
  216.9 87.9 %collective-permute-start.28 = (bf16[384,768]{1,0:T(8,128)(2,1)}, bf16[384,768]{1,0:T(8,128)(2,1)}, u32[]{:S(2)}, u32[]{:S(2)}) collective-permute-start(bf16[384,768]{1,0:T(8,128)(2,1)} %get-tuple-element.221), channel_id=1, source_target_pairs={{0,2},{1,3},{2,0},{3,1},{4,6},{5,7},{6,4},{7,5},{8,10},{9,11},{10,... | collective-permute-start | bytes 1769480 | tf_op jit(solution)/shard_map/ppermute | solution.py:38
  217.4 49.1 %all-to-all-start.3 = ((bf16[8,96,768]{2,1,0:T(8,128)(2,1)}), bf16[8,96,768]{2,1,0:T(8,128)(2,1)S(1)}, u32[]{:S(2)}, u32[]{:S(2)}) async-start(bf16[8,96,768]{2,1,0:T(8,128)(2,1)} %bitcast.12), calls=%async_computation.3 | async-start | bytes 2359296 | tf_op jit(solution)/shard_map/all_to_all | solution.py:1102
  235.6 6.2 %collective-permute-start.10 = (bf16[2,192,1280]{2,1,0:T(8,128)(2,1)}, bf16[2,192,1280]{2,1,0:T(8,128)(2,1)S(1)}, u32[]{:S(2)}, u32[]{:S(2)}) collective-permute-start(bf16[2,192,1280]{2,1,0:T(8,128)(2,1)} %get-tuple-element.164), channel_id=1, source_target_pairs={{0,1},{1,0},{2,3},{3,2},{4,5},{5,4},{6,7},{7,6},{8,9},{9,8},{10,11... | collective-permute-start | bytes 2949128 | tf_op jit(solution)/shard_map/ppermute | solution.py:38
  238.3 13.9 %collective-permute-start.16 = (bf16[96,2048]{1,0:T(8,128)(2,1)}, bf16[96,2048]{1,0:T(8,128)(2,1)}, u32[]{:S(2)}, u32[]{:S(2)}) collective-permute-start(bf16[96,2048]{1,0:T(8,128)(2,1)} %broadcast_select_fusion.2), channel_id=1, source_target_pairs={{0,4},{4,0},{8,12},{12,8},{16,20},{20,16},{24,28},{28,24},{1,5},{5... | collective-permute-start | bytes 1179656 | tf_op jit(solution)/shard_map/ppermute | solution.py:38
  240.3 15.1 %collective-permute-start.26 = (bf16[64,3072]{1,0:T(8,128)(2,1)}, bf16[64,3072]{1,0:T(8,128)(2,1)}, u32[]{:S(2)}, u32[]{:S(2)}) collective-permute-start(bf16[64,3072]{1,0:T(8,128)(2,1)} %slice.177), channel_id=1, source_target_pairs={{0,2},{1,3},{2,0},{3,1},{4,6},{5,7},{6,4},{7,5},{8,10},{9,11},{10,... | collective-permute-start | bytes 1179656 | tf_op jit(solution)/shard_map/ppermute | solution.py:38
  243.5 16.2 %collective-permute-start.11 = (bf16[144,1280]{1,0:T(8,128)(2,1)}, bf16[144,1280]{1,0:T(8,128)(2,1)}, u32[]{:S(2)}, u32[]{:S(2)}) collective-permute-start(bf16[144,1280]{1,0:T(8,128)(2,1)} %slice.154), channel_id=1, source_target_pairs={{0,2},{1,3},{2,0},{3,1},{4,6},{5,7},{6,4},{7,5},{8,10},{9,11},{10,... | collective-permute-start | bytes 1105928 | tf_op jit(solution)/shard_map/ppermute | solution.py:38
  244.0 11.4 %copy-start.9 = (bf16[2,192,3072]{2,1,0:T(8,128)(2,1)S(1)}, bf16[2,192,3072]{2,1,0:T(8,128)(2,1)}, u32[]{:S(2)}) copy-start(bf16[2,192,3072]{2,1,0:T(8,128)(2,1)} %get-tuple-element.139) | copy-start | bytes 7077892
  244.0 11.4 %copy-start.11 = (bf16[2,192,3072]{2,1,0:T(8,128)(2,1)S(1)}, bf16[2,192,3072]{2,1,0:T(8,128)(2,1)}, u32[]{:S(2)}) copy-start(bf16[2,192,3072]{2,1,0:T(8,128)(2,1)} %copy-done.10) | copy-start | bytes 7077892
  252.1 39.4 %collective-permute-start.13 = (bf16[2,256,768]{2,1,0:T(8,128)(2,1)}, bf16[2,256,768]{2,1,0:T(8,128)(2,1)}, u32[]{:S(2)}, u32[]{:S(2)}) collective-permute-start(bf16[2,256,768]{2,1,0:T(8,128)(2,1)} %get-tuple-element.170), channel_id=1, source_target_pairs={{0,1},{1,0},{2,3},{3,2},{4,5},{5,4},{6,7},{7,6},{8,9},{9,8},{10,11... | collective-permute-start | bytes 2359304 | tf_op jit(solution)/shard_map/ppermute | solution.py:38
  253.5 7.8 %collective-permute-start.17 = (bf16[48,2048]{1,0:T(8,128)(2,1)S(1)}, bf16[48,2048]{1,0:T(8,128)(2,1)S(1)}, u32[]{:S(2)}, u32[]{:S(2)}) collective-permute-start(bf16[48,2048]{1,0:T(8,128)(2,1)S(1)} %broadcast_select_fusion.8), channel_id=1, source_target_pairs={{0,8},{4,12},{8,0},{12,4},{16,24},{20,28},{24,16},{28,20},{1,9},{5... | collective-permute-start | bytes 589832 | tf_op jit(solution)/shard_map/ppermute | solution.py:38
  255.5 9.1 %copy-start.19 = (bf16[2,192,1280]{2,1,0:T(8,128)(2,1)S(1)}, bf16[2,192,1280]{2,1,0:T(8,128)(2,1)}, u32[]{:S(2)}) copy-start(bf16[2,192,1280]{2,1,0:T(8,128)(2,1)} %copy-done.18) | copy-start | bytes 2949124
  258.5 9.2 %copy-start.26 = (bf16[256,768]{1,0:T(8,128)(2,1)S(1)}, bf16[256,768]{1,0:T(8,128)(2,1)}, u32[]{:S(2)}) copy-start(bf16[256,768]{1,0:T(8,128)(2,1)} %get-tuple-element.118) | copy-start | bytes 1179652
  259.7 4.9 %collective-permute-start.12 = (bf16[48,1280]{1,0:T(8,128)(2,1)S(1)}, bf16[48,1280]{1,0:T(8,128)(2,1)S(1)}, u32[]{:S(2)}, u32[]{:S(2)}) collective-permute-start(bf16[48,1280]{1,0:T(8,128)(2,1)S(1)} %copy-done.32), channel_id=1, source_target_pairs={{0,2},{1,3},{2,0},{3,1},{4,6},{5,7},{6,4},{7,5},{8,10},{9,11},{10,... | collective-permute-start | bytes 368648 | tf_op jit(solution)/shard_map/ppermute | solution.py:38
  261.3 11.3 %collective-permute-start.18 = (bf16[48,2048]{1,0:T(8,128)(2,1)S(1)}, bf16[48,2048]{1,0:T(8,128)(2,1)}, u32[]{:S(2)}, u32[]{:S(2)}) collective-permute-start(bf16[48,2048]{1,0:T(8,128)(2,1)S(1)} %add_convert_fusion.14), channel_id=1, source_target_pairs={{0,16},{4,20},{8,24},{12,28},{16,0},{20,4},{24,8},{28,12},{1,17},{... | collective-permute-start | bytes 589832 | tf_op jit(solution)/shard_map/ppermute | solution.py:38
  266.5 7.3 %collective-permute-start.21 = (bf16[96,1280]{1,0:T(8,128)(2,1)}, bf16[96,1280]{1,0:T(8,128)(2,1)S(1)}, u32[]{:S(2)}, u32[]{:S(2)}) collective-permute-start(bf16[96,1280]{1,0:T(8,128)(2,1)} %broadcast_select_fusion.5), channel_id=1, source_target_pairs={{0,4},{4,0},{8,12},{12,8},{16,20},{20,16},{24,28},{28,24},{1,5},{5... | collective-permute-start | bytes 737288 | tf_op jit(solution)/shard_map/ppermute | solution.py:38
  273.6 7.4 %collective-permute-start.19 = (bf16[48,2048]{1,0:T(8,128)(2,1)S(1)}, bf16[48,2048]{1,0:T(8,128)(2,1)S(1)}, u32[]{:S(2)}, u32[]{:S(2)}) collective-permute-start(bf16[48,2048]{1,0:T(8,128)(2,1)S(1)} %add_convert_fusion.13), channel_id=1, source_target_pairs={{0,8},{4,12},{8,0},{12,4},{16,24},{20,28},{24,16},{28,20},{1,9},{5... | collective-permute-start | bytes 589832 | tf_op jit(solution)/shard_map/ppermute | solution.py:38
  273.9 17.6 %copy-start.21 = (bf16[2,256,768]{2,1,0:T(8,128)(2,1)S(1)}, bf16[2,256,768]{2,1,0:T(8,128)(2,1)}, u32[]{:S(2)}) copy-start(bf16[2,256,768]{2,1,0:T(8,128)(2,1)} %get-tuple-element.176) | copy-start | bytes 2359300
  274.0 8.3 %collective-permute-start.22 = (bf16[48,1280]{1,0:T(8,128)(2,1)S(1)}, bf16[48,1280]{1,0:T(8,128)(2,1)S(1)}, u32[]{:S(2)}, u32[]{:S(2)}) collective-permute-start(bf16[48,1280]{1,0:T(8,128)(2,1)S(1)} %broadcast_select_fusion.11), channel_id=1, source_target_pairs={{0,8},{4,12},{8,0},{12,4},{16,24},{20,28},{24,16},{28,20},{1,9},{5... | collective-permute-start | bytes 368648 | tf_op jit(solution)/shard_map/ppermute | solution.py:38
  282.4 8.4 %collective-permute-start.23 = (bf16[48,1280]{1,0:T(8,128)(2,1)S(1)}, bf16[48,1280]{1,0:T(8,128)(2,1)S(1)}, u32[]{:S(2)}, u32[]{:S(2)}) collective-permute-start(bf16[48,1280]{1,0:T(8,128)(2,1)S(1)} %add_convert_fusion.16), channel_id=1, source_target_pairs={{0,16},{4,20},{8,24},{12,28},{16,0},{20,4},{24,8},{28,12},{1,17},{... | collective-permute-start | bytes 368648 | tf_op jit(solution)/shard_map/ppermute | solution.py:38
  285.2 11.8 %collective-permute-start.20 = (bf16[96,2048]{1,0:T(8,128)(2,1)S(1)}, bf16[96,2048]{1,0:T(8,128)(2,1)S(1)}, u32[]{:S(2)}, u32[]{:S(2)}) collective-permute-start(bf16[96,2048]{1,0:T(8,128)(2,1)S(1)} %pad_maximum_fusion.2), channel_id=1, source_target_pairs={{0,4},{4,0},{8,12},{12,8},{16,20},{20,16},{24,28},{28,24},{1,5},{5... | collective-permute-start | bytes 1179656 | tf_op jit(solution)/shard_map/ppermute | solution.py:38
  290.8 4.9 %collective-permute-start.24 = (bf16[48,1280]{1,0:T(8,128)(2,1)S(1)}, bf16[48,1280]{1,0:T(8,128)(2,1)S(1)}, u32[]{:S(2)}, u32[]{:S(2)}) collective-permute-start(bf16[48,1280]{1,0:T(8,128)(2,1)S(1)} %add_convert_fusion.15), channel_id=1, source_target_pairs={{0,8},{4,12},{8,0},{12,4},{16,24},{20,28},{24,16},{28,20},{1,9},{5... | collective-permute-start | bytes 368648 | tf_op jit(solution)/shard_map/ppermute | solution.py:38
  292.6 10.7 %collective-permute-start.14 = (bf16[256,768]{1,0:T(8,128)(2,1)S(1)}, bf16[256,768]{1,0:T(8,128)(2,1)S(1)}, u32[]{:S(2)}, u32[]{:S(2)}) collective-permute-start(bf16[256,768]{1,0:T(8,128)(2,1)S(1)} %fusion.10), channel_id=1, source_target_pairs={{0,2},{1,3},{2,0},{3,1},{4,6},{5,7},{6,4},{7,5},{8,10},{9,11},{10,... | collective-permute-start | bytes 1179656 | tf_op jit(solution)/shard_map/ppermute | solution.py:38
  295.8 10.6 %collective-permute-start.25 = (bf16[96,1280]{1,0:T(8,128)(2,1)S(1)}, bf16[96,1280]{1,0:T(8,128)(2,1)S(1)}, u32[]{:S(2)}, u32[]{:S(2)}) collective-permute-start(bf16[96,1280]{1,0:T(8,128)(2,1)S(1)} %pad_maximum_fusion.3), channel_id=1, source_target_pairs={{0,4},{4,0},{8,12},{12,8},{16,20},{20,16},{24,28},{28,24},{1,5},{5... | collective-permute-start | bytes 737288 | tf_op jit(solution)/shard_map/ppermute | solution.py:38
  304.7 14.0 %collective-permute-start.29 = (bf16[384,768]{1,0:T(8,128)(2,1)S(1)}, bf16[384,768]{1,0:T(8,128)(2,1)S(1)}, u32[]{:S(2)}, u32[]{:S(2)}) collective-permute-start(bf16[384,768]{1,0:T(8,128)(2,1)S(1)} %copy-done.22), channel_id=1, source_target_pairs={{0,2},{1,3},{2,0},{3,1},{4,6},{5,7},{6,4},{7,5},{8,10},{9,11},{10,... | collective-permute-start | bytes 1769480 | tf_op jit(solution)/shard_map/ppermute | solution.py:38
  307.3 11.5 %copy-start.6 = (bf16[2,768,768]{2,1,0:T(8,128)(2,1)S(1)}, bf16[2,768,768]{2,1,0:T(8,128)(2,1)}, u32[]{:S(2)}) copy-start(bf16[2,768,768]{2,1,0:T(8,128)(2,1)} %get-tuple-element.188) | copy-start | bytes 7077892
  (22 other events, 77.1 us)

commit v4 on v3

--- a/solution.py
+++ b/solution.py
@@ -1115,25 +1115,19 @@
         )
         give2, keep2 = second_grads_call(me, *part2, normed_t, table2, count)
         sum1 = far_sum(pieces1, count, None, give2)
-        pieces2 = core_sum(give2, keep2, count)
-        last = max(pieces2)
-        dv2, pieces2[last] = ordered(part2[2], pieces2[last])
-        rows_give, rows_keep = rows_back_call(
-            me, part1, (part2[0], part2[1], dv2), (wq, wk, wv), count
-        )
-        steps2 = far_steps(pieces2, count, (9, 3))
-        sum2 = steps2.send(steps2.send(ordered(next(steps2), rows_give)[0]))
+        rows_give, rows_keep = rows_back_call(me, part1, part2, (wq, wk, wv), count)
+        sum2 = far_sum(core_sum(give2, keep2, count), count)
         arrived = in_steps.send(ordered(arrived, sum1)[0])
         in_sum = in_steps.send(arrived)
-        grad_normed = far_sum(core_sum(rows_give, rows_keep, count), count, sum2)
-        arrived, _ = ordered(arrived, sum2)
         out_steps = far_steps(out_pieces, count, (6, 6), arrived)
-        out_sum = out_steps.send(out_steps.send(ordered(next(out_steps), grad_normed)[0]))
+        arrived = out_steps.send(ordered(next(out_steps), sum2)[0])
+        out_sum = out_steps.send(arrived)
         grad_shards = [in_sum, out_sum]
         chain1, _ = all_sum_expert(sum1, expert_ranks, expert_index)
         chain2, first_arrived = all_sum_expert(sum2, expert_ranks, expert_index)
         half_cols = near * tile
 
+        grad_normed = far_sum(core_sum(rows_give, rows_keep, count), count, sum2)
         inputs = tokens_in.astype(f32)
         inverse = lax.rsqrt(jnp.mean(inputs * inputs, axis=-1, keepdims=True) + eps)
         gain_attn = smalls[experts + heads]

time: 326 us -> 315 us (0.966)
  other arithmetic: 23.7 us -> 18.7 us
  starting transfers between devices: 64.7 us -> 61.3 us
    ppermute x30 -> x29, starting transfers between devices: 33.1 us -> 29.7 us  [swap(): lax.ppermute(value, axis_name, [(i, i ^ bit) for i in range(axis_size)])]
    ppermute x30 -> x29, waiting for transfers between devices: 54.5 us -> 52.9 us  [swap(): lax.ppermute(value, axis_name, [(i, i ^ bit) for i in range(axis_size)])]
    unnamed x78 -> x76, local copies, waits for them, and re-layouts: 6.78 us -> 6.78 us
  transfers between devices with their start and end apart: 34 -> 33, of which waited for: 18 -> 19; matrix products, arithmetic and copies ran while one was open for 11% -> 9% of each run, Pallas kernels for 30% -> 31%
where the time goes in v4:
time: 315 us; the launch traced here: 312 us
  Pallas kernels  122 us (39%)
  waiting for transfers between devices  85.1 us (27%)
  starting transfers between devices  61.3 us (19%)
  local copies, waits for them, and re-layouts  20.2 us (6%)
  other arithmetic  18.7 us (6%)
    ppermute x29, waiting for transfers between devices, swap(): lax.ppermute(value, axis_name, [(i, i ^ bit) for i in range(axis_size)])  52.9 us
    ppermute x29, starting transfers between devices, swap(): lax.ppermute(value, axis_name, [(i, i ^ bit) for i in range(axis_size)])  29.7 us
    pallas_call x1, Pallas kernels, expert_call(): pl.pallas_call(kernel, grid=(steps,), in_specs=[full, full, pl.BlockSpec(...  19.8 us
    all_to_all x1, waiting for transfers between devices, per_device(): lax.all_to_all(rows_out.reshape(experts, capacity, width), 'expert', spli...  18 us
    pallas_call x2, Pallas kernels, attend_back_call(): pl.pallas_call(kernel, grid=(pairs,), in_specs=[narrow, tall, tall, pl.Bl...  17 us
    pallas_call x1, Pallas kernels, expert_grads_call(): pl.pallas_call(kernel, grid_spec=pltpu.PrefetchScalarGridSpec(num_scalar_...  16.2 us
    all_to_all x1, starting transfers between devices, per_device(): lax.all_to_all(row_grads, 'expert', split_axis=0, concat_axis=0, tiled=True)  14.3 us
    all_to_all x1, waiting for transfers between devices, per_device(): lax.all_to_all(row_grads, 'expert', split_axis=0, concat_axis=0, tiled=True)  13.9 us
  transfers between devices with their start and end apart: 33, of which 19 were waited for; matrix products, arithmetic and copies ran while one was open for 9% of the time, Pallas kernels for 31%

profile of v4, /device:TPU:0, one launch (start us, length us, event | category | flops | bytes accessed | tf_op | source)
XLA Modules:
  0.0 311.5 jit_solution(14461515406749332984)
XLA Ops:
  3.1 2.6 pack.1.refs_0_
  6.2 2.5 collective-permute-start.1
  10.0 3.5 %route.1 = (bf16[768,256]{1,0:T(8,128)(2,1)}, bf16[256,768]{1,0:T(8,128)(2,1)}, bf16[256,768]{1,0:T(8,128)(2,1)}, bf16[8,112,768]{2,1,0:T(8,128)(2,1)}, f32[256,2]{1,0:T(8,128)}) custom-call(s32[256,2]{1,0:T(8,128)} %copy.33.refs_0_.refs_6_.routes_ref, bf16[256,768]{1,0:T(8,128)(2,1)} %cot_ref.1), custom_call_target="tpu_custom_call" | custom-call | flops 1179648 | bytes 9216 | tf_op jit(solution)/shard_map/route/pallas_call | solution.py:102
  13.5 7.2 %all-to-all-start = ((bf16[8,112,768]{2,1,0:T(8,128)(2,1)}), bf16[8,112,768]{2,1,0:T(8,128)(2,1)S(1)}, u32[]{:S(2)}, u32[]{:S(2)}) async-start(bf16[8,112,768]{2,1,0:T(8,128)(2,1)} %get-tuple-element.102), calls=%async_computation | async-start | bytes 2752512 | tf_op jit(solution)/shard_map/all_to_all | solution.py:1039
  20.7 18.1 %collective-permute-done.1.refs_2_ = bf16[864,768]{1,0:T(8,128)(2,1)} collective-permute-done((bf16[864,768]{1,0:T(8,128)(2,1)}, bf16[864,768]{1,0:T(8,128)(2,1)}, u32[]{:S(2)}, u32[]{:S(2)}) %collective-permute-start.1) | collective-permute-done | bytes 1327136 | tf_op jit(solution)/shard_map/ppermute | solution.py:38
  38.8 1.7 collective-permute-start.4
  43.2 10.1 %project.1 = (bf16[256,768]{1,0:T(8,128)(2,1)}, bf16[1024,768]{1,0:T(8,128)(2,1)}, bf16[1024,768]{1,0:T(8,128)(2,1)}, bf16[1024,768]{1,0:T(8,128)(2,1)}, bf16[10...) custom-call(s32[2]{0:T(128)} %pad_add_fusion.me_ref, ...), custom_call_target="tpu_custom_call" | custom-call | flops 10616832 | bytes 61440 | tf_op jit(solution)/shard_map/project/pallas_call | solution.py:202
  55.6 10.2 %attend.1 = (f32[256,768]{1,0:T(8,128)}, f32[12,1,256]{2,1,0:T(1,128)}) custom-call(bf16[256,768]{1,0:T(8,128)(2,1)} %get-tuple-element.103.q_ref, bf16[1024,768]{1,0:T(8,128)(2,1)} %get-tuple-element.104.k_ref, bf16[1024,768]{1,0:T(8,128)(2,1)} %get-tuple-element.105.v_ref, f32[12,1,1280]{2,1,0:T(1,128)} %get-tuple-element.106.bias_ref, ...), custom_call_target="tpu_custom_call" | custom-call | flops 25165824 | bytes 12288 | tf_op jit(solution)/shard_map/attend/pallas_call | solution.py:268
  66.5 4.2 %dispatch.1 = (bf16[768,768]{1,0:T(8,128)(2,1)}, bf16[256,768]{1,0:T(8,128)(2,1)}, f32[256,768]{1,0:T(8,128)}, bf16[256,768]{1,0:T(8,128)(2,1)}, f32[256,2]{1,0:T(8,128)}, /*index=5*/bf16[768,768]{1,0:T(8,128)(2,1)}) custom-call(s32[2]{0:T(128)} %pad_add_fusion.me_ref, f32[256,768]{1,0:T(8,128)} %get-tuple-element.108.ctx_ref, bf16[192,768]{1,0:T(8,128)(2,1)} %refs_0_, ...), custom_call_target="tpu_custom_call" | custom-call | flops 2359296 | bytes 18432 | tf_op jit(solution)/shard_map/dispatch/pallas_call | solution.py:448
  70.7 5.9 %all-to-all-start.1 = ((bf16[8,96,768]{2,1,0:T(8,128)(2,1)}), bf16[8,96,768]{2,1,0:T(8,128)(2,1)S(1)}, u32[]{:S(2)}, u32[]{:S(2)}) async-start(bf16[8,96,768]{2,1,0:T(8,128)(2,1)} %bitcast.70), calls=%async_computation.1 | async-start | bytes 2359296 | tf_op jit(solution)/shard_map/all_to_all | solution.py:1056
  76.6 1.6 copy.35
  78.3 9.5 %upstream.1.up_ref = f32[768,3072]{1,0:T(8,128)} custom-call(bf16[768,768]{1,0:T(8,128)(2,1)} %bitcast.62, bf16[3072,768]{1,0:T(8,128)(2,1)} %bitcast.60), custom_call_target="tpu_custom_call" | custom-call | flops 14155776 | bytes 55296 | tf_op jit(solution)/shard_map/upstream/pallas_call | solution.py:475
  87.7 18.0 %all-to-all-done.1 = bf16[8,96,768]{2,1,0:T(8,128)(2,1)S(1)} async-done(((bf16[8,96,768]{2,1,0:T(8,128)(2,1)}), bf16[8,96,768]{2,1,0:T(8,128)(2,1)S(1)}, u32[]{:S(2)}, u32[]{:S(2)}) %all-to-all-start.1) | async-done | bytes 1179680 | tf_op jit(solution)/shard_map/all_to_all | solution.py:1056
  106.7 19.8 %experts.1 = (bf16[768,3072]{1,0:T(8,128)(2,1)}, bf16[768,3072]{1,0:T(8,128)(2,1)}, bf16[768,768]{1,0:T(8,128)(2,1)}, bf16[8,112,768]{2,1,0:T(8,128)(2,1)}) custom-call(bf16[768,768]{1,0:T(8,128)(2,1)} %bitcast.57, bf16[768,768]{1,0:T(8,128)(2,1)} %bitcast.63, f32[768,3072]{1,0:T(8,128)} %upstream.1.up_ref, bf16[768,3072]{1,0:T(8,128)(2,1)} %bitcast.69, ...), custom_call_target="tpu_custom_call" | custom-call | flops 56623104 | bytes 73728 | tf_op jit(solution)/shard_map/experts/pallas_call | solution.py:540
  126.6 14.3 %all-to-all-start.2 = ((bf16[8,112,768]{2,1,0:T(8,128)(2,1)}), bf16[8,112,768]{2,1,0:T(8,128)(2,1)S(1)}, u32[]{:S(2)}, u32[]{:S(2)}) async-start(bf16[8,112,768]{2,1,0:T(8,128)(2,1)} %get-tuple-element.130), calls=%async_computation.2 | async-start | bytes 2752512 | tf_op jit(solution)/shard_map/all_to_all | solution.py:1067
  143.7 16.2 %expert_grads.1 = (bf16[2,192,3072]{2,1,0:T(8,128)(2,1)}, bf16[2,192,3072]{2,1,0:T(8,128)(2,1)}, bf16[2,768,768]{2,1,0:T(8,128)(2,1)}, bf16[2,768,768]{2,1,0:T(8,128)(2,1)}) custom-call(s32[2]{0:T(128)} %pad_add_fusion.me_ref, bf16[768,768]{1,0:T(8,128)(2,1)} %copy.36.xt_ref, bf16[768,768]{1,0:T(8,128)(2,1)} %bitcast.58, bf16[768,768]{1,0:T(8,128)(2,1)} %bitcast.64, ...), custom_call_target="tpu_custom_call" | custom-call | flops 28311552 | bytes 73728 | tf_op jit(solution)/shard_map/expert_grads/pallas_call | solution.py:625
  159.9 13.9 %all-to-all-done.2.rows_ref = bf16[8,112,768]{2,1,0:T(8,128)(2,1)S(1)} async-done(((bf16[8,112,768]{2,1,0:T(8,128)(2,1)}), bf16[8,112,768]{2,1,0:T(8,128)(2,1)S(1)}, u32[]{:S(2)}, u32[]{:S(2)}) %all-to-all-start.2) | async-done | bytes 1376288 | tf_op jit(solution)/shard_map/all_to_all | solution.py:1067
  174.9 5.9 %combine.1 = (f32[256,768]{1,0:T(8,128)}, bf16[256,768]{1,0:T(8,128)(2,1)}, bf16[256,768]{1,0:T(8,128)(2,1)}, f32[8,768]{1,0:T(8,128)}, f32[1,768]{1,0:T(1,128)}) custom-call(bf16[8,112,768]{2,1,0:T(8,128)(2,1)} %copy-done.3, f32[256,2]{1,0:T(8,128)} %get-tuple-element.132.place_ref, f32[256,2]{1,0:T(8,128)} %get-tuple-element.114.gate_ref, ...), custom_call_target="tpu_custom_call" | custom-call | flops 3538944 | bytes 18432 | tf_op jit(solution)/shard_map/combine/pallas_call | solution.py:706
  182.3 1.6 collective-permute-start.7
  183.9 8.5 %attend_back.2 = (bf16[256,384]{1,0:T(8,128)(2,1)}, bf16[1024,384]{1,0:T(8,128)(2,1)}, bf16[1024,384]{1,0:T(8,128)(2,1)}, f32[6,1,32]{2,1,0:T(1,128)}) custom-call(bf16[256,768]{1,0:T(8,128)(2,1)} %get-tuple-element.103.q_ref, bf16[1024,768]{1,0:T(8,128)(2,1)} %get-tuple-element.104.k_ref, bf16[1024,768]{1,0:T(8,128)(2,1)} %get-tuple-element.105.v_ref, ...), custom_call_target="tpu_custom_call" | custom-call | flops 31457280 | bytes 12288 | tf_op jit(solution)/shard_map/attend_back/pallas_call | solution.py:365
  192.3 2.5 collective-permute-done.7
  194.8 6.5 %first_grads.1 = (bf16[2,192,2048]{2,1,0:T(8,128)(2,1)}, bf16[2,192,2048]{2,1,0:T(8,128)(2,1)}) custom-call(s32[2]{0:T(128)} %pad_add_fusion.me_ref, bf16[256,384]{1,0:T(8,128)(2,1)} %get-tuple-element.141.dq_ref.dq1_ref, bf16[1024,384]{1,0:T(8,128)(2,1)} %get-tuple-element.142.dk_ref.dk1_ref, bf16[1024,384]{1,0:T(8,128)(2,1)} %get-tuple-element.143.dv_ref.dv1_ref, ...), custom_call_target="tpu_custom_call" | custom-call | flops 5898240 | bytes 30720 | tf_op jit(solution)/shard_map/first_grads/pallas_call | solution.py:773
  201.4 1.6 collective-permute-start.9
  203.0 2.1 collective-permute-done.8
  205.1 2.7 fusion.5
  207.8 3.1 collective-permute-done.9
  210.9 1.5 collective-permute-start.14
  216.7 4.2 %all-to-all-start.3 = ((bf16[8,96,768]{2,1,0:T(8,128)(2,1)}), bf16[8,96,768]{2,1,0:T(8,128)(2,1)S(1)}, u32[]{:S(2)}, u32[]{:S(2)}) async-start(bf16[8,96,768]{2,1,0:T(8,128)(2,1)} %bitcast.12), calls=%async_computation.3 | async-start | bytes 2359296 | tf_op jit(solution)/shard_map/all_to_all | solution.py:1102
  220.9 8.5 %attend_back.3 = (bf16[256,384]{1,0:T(8,128)(2,1)}, bf16[1024,384]{1,0:T(8,128)(2,1)}, bf16[1024,384]{1,0:T(8,128)(2,1)}, f32[6,1,32]{2,1,0:T(1,128)}) custom-call(bf16[256,768]{1,0:T(8,128)(2,1)} %get-tuple-element.103.q_ref, bf16[1024,768]{1,0:T(8,128)(2,1)} %get-tuple-element.104.k_ref, bf16[1024,768]{1,0:T(8,128)(2,1)} %get-tuple-element.105.v_ref, ...), custom_call_target="tpu_custom_call" | custom-call | flops 31457280 | bytes 12288 | tf_op jit(solution)/shard_map/attend_back/pallas_call | solution.py:365
  229.4 5.3 %second_grads.1 = (bf16[2,192,1280]{2,1,0:T(8,128)(2,1)}, bf16[2,192,1280]{2,1,0:T(8,128)(2,1)}) custom-call(s32[2]{0:T(128)} %pad_add_fusion.me_ref, bf16[256,384]{1,0:T(8,128)(2,1)} %get-tuple-element.156.dq_ref.dq2_ref, bf16[1024,384]{1,0:T(8,128)(2,1)} %get-tuple-element.157.dk_ref.dk2_ref, bf16[1024,384]{1,0:T(8,128)(2,1)} %get-tuple-element.158.dv_ref.dv2_ref, ...), custom_call_target="tpu_custom_call" | custom-call | flops 5898240 | bytes 30720 | tf_op jit(solution)/shard_map/second_grads/pallas_call | solution.py:818
  234.8 8.1 %rows_back.1 = (bf16[2,256,768]{2,1,0:T(8,128)(2,1)}, bf16[2,256,768]{2,1,0:T(8,128)(2,1)}) custom-call(s32[2]{0:T(128)} %pad_add_fusion.me_ref, bf16[256,384]{1,0:T(8,128)(2,1)} %get-tuple-element.141.dq_ref.dq1_ref, bf16[1024,384]{1,0:T(8,128)(2,1)} %get-tuple-element.142.dk_ref.dk1_ref, bf16[1024,384]{1,0:T(8,128)(2,1)} %get-tuple-element.143.dv_ref.dv1_ref, ...), custom_call_target="tpu_custom_call" | custom-call | flops 23592960 | bytes 30720 | tf_op jit(solution)/shard_map/rows_back/pallas_call | solution.py:847
  243.4 1.8 convert_add_fusion.2
  245.3 2.1 collective-permute-start.15
  248.9 1.6 collective-permute-start.11
  250.5 6.3 %collective-permute-done.15 = bf16[96,2048]{1,0:T(8,128)(2,1)S(1)} collective-permute-done((bf16[96,2048]{1,0:T(8,128)(2,1)S(1)}, bf16[96,2048]{1,0:T(8,128)(2,1)S(1)}, u32[]{:S(2)}, u32[]{:S(2)}) %collective-permute-start.15) | collective-permute-done | bytes 393248 | tf_op jit(solution)/shard_map/ppermute | solution.py:38
  257.0 1.8 collective-permute-start.16
  260.0 2.0 convert_add_fusion.1
  263.5 2.4 collective-permute-start.17
  265.9 4.1 %collective-permute-done.11 = bf16[192,1280]{1,0:T(8,128)(2,1)S(1)} collective-permute-done((bf16[192,1280]{1,0:T(8,128)(2,1)S(1)}, bf16[192,1280]{1,0:T(8,128)(2,1)S(1)}, u32[]{:S(2)}, u32[]{:S(2)}) %collective-permute-start.11) | collective-permute-done | bytes 491552 | tf_op jit(solution)/shard_map/ppermute | solution.py:38
  275.3 2.0 collective-permute-start.18
  277.9 1.5 collective-permute-start.21
  279.5 3.4 %collective-permute-done.18 = bf16[48,2048]{1,0:T(8,128)(2,1)S(1)} collective-permute-done((bf16[48,2048]{1,0:T(8,128)(2,1)S(1)}, bf16[48,2048]{1,0:T(8,128)(2,1)S(1)}, u32[]{:S(2)}, u32[]{:S(2)}) %collective-permute-start.18) | collective-permute-done | bytes 196640 | tf_op jit(solution)/shard_map/ppermute | solution.py:38
  284.7 2.4 collective-permute-start.22
  287.1 3.9 %collective-permute-done.13 = bf16[256,768]{1,0:T(8,128)(2,1)S(1)} collective-permute-done((bf16[256,768]{1,0:T(8,128)(2,1)}, bf16[256,768]{1,0:T(8,128)(2,1)S(1)}, u32[]{:S(2)}, u32[]{:S(2)}) %collective-permute-start.13) | collective-permute-done | bytes 393248 | tf_op jit(solution)/shard_map/ppermute | solution.py:38
  294.2 2.6 collective-permute-done.23
  300.4 2.7 collective-permute-done.24
  304.0 3.1 %finish.1 = (f32[192,768]{1,0:T(8,128)}, f32[192,768]{1,0:T(8,128)}, f32[192,768]{1,0:T(8,128)}, f32[192,768]{1,0:T(8,128)}, f32[1,192]{1,0:T(1,128)}) custom-call(bf16[192,2048]{1,0:T(8,128)(2,1)} %pad_maximum_fusion.c1_ref, bf16[192,1280]{1,0:T(8,128)(2,1)} %pad_maximum_fusion.1.c2_ref, bf16[192,768]{1,0:T(8,128)(2,1)} %wq_ref.3, bf16[192,768]{1,0:T(8,128)(2,1)} %wk_ref.3, ...), custom_call_target="tpu_custom_call" | custom-call | flops 3456 | bytes 17280 | tf_op jit(solution)/shard_map/finish/pallas_call | solution.py:874
  307.9 3.2 %convert_add_fusion = f32[1,768,768]{2,1,0:T(8,128)} fusion(bf16[2,768,768]{2,1,0:T(8,128)(2,1)} %copy-done.7, bf16[1,384,768]{2,1,0:T(8,128)(2,1)S(1)} %bitcast.71, bf16[1,384,768]{2,1,0:T(8,128)(2,1)} %bitcast.28, bf16[2,768,768]{2,1,0:T(8,128)(2,1)S(1)} %copy-done.6), kind=kLoop, calls=%fused_computation | loop fusion | flops 5898240 | bytes 5898240 | tf_op jit(solution)/shard_map/add | solution.py:906
  (170 shorter events, 41.5 us)
Async XLA Ops:
  2.0 11.5 %copy-start.32 = (bf16[1,192]{1,0:T(2,128)(2,1)}, bf16[1,192]{1,0:T(2,128)(2,1)S(1)}, u32[]{:S(2)}) copy-start(bf16[1,192]{1,0:T(2,128)(2,1)S(1)} %stack.21.gain_ref) | copy-start | bytes 1156
  5.8 3.3 %collective-permute-start = (bf16[864,768]{1,0:T(8,128)(2,1)}, bf16[864,768]{1,0:T(8,128)(2,1)S(1)}, u32[]{:S(2)}, u32[]{:S(2)}) collective-permute-start(bf16[864,768]{1,0:T(8,128)(2,1)} %pack.1.refs_0_), channel_id=1, source_target_pairs={{0,1},{1,0},{2,3},{3,2},{4,5},{5,4},{6,7},{7,6},{8,9},{9,8},{10,11... | collective-permute-start | bytes 3981320 | tf_op jit(solution)/shard_map/ppermute | solution.py:38
  6.2 32.6 %collective-permute-start.1 = (bf16[864,768]{1,0:T(8,128)(2,1)}, bf16[864,768]{1,0:T(8,128)(2,1)}, u32[]{:S(2)}, u32[]{:S(2)}) collective-permute-start(bf16[864,768]{1,0:T(8,128)(2,1)} %pack.1.refs_0_), channel_id=1, source_target_pairs={{0,2},{1,3},{2,0},{3,1},{4,6},{5,7},{6,4},{7,5},{8,10},{9,11},{10,... | collective-permute-start | bytes 3981320 | tf_op jit(solution)/shard_map/ppermute | solution.py:38
  10.0 28.8 %copy-start.27 = (bf16[192,768]{1,0:T(8,128)(2,1)S(1)}, bf16[192,768]{1,0:T(8,128)(2,1)}, u32[]{:S(2)}) copy-start(bf16[192,768]{1,0:T(8,128)(2,1)} %refs_0_) | copy-start | bytes 884740
  10.0 30.5 %copy-start.33 = (s32[1024]{0:T(1024)S(1)}, s32[1024]{0:T(1024)}, u32[]{:S(2)}) copy-start(s32[1024]{0:T(1024)} %param.18) | copy-start | bytes 12292
  13.5 40.3 %all-to-all-start = ((bf16[8,112,768]{2,1,0:T(8,128)(2,1)}), bf16[8,112,768]{2,1,0:T(8,128)(2,1)S(1)}, u32[]{:S(2)}, u32[]{:S(2)}) async-start(bf16[8,112,768]{2,1,0:T(8,128)(2,1)} %get-tuple-element.102), calls=%async_computation | async-start | bytes 2752512 | tf_op jit(solution)/shard_map/all_to_all | solution.py:1039
  38.8 3.3 %collective-permute-start.2 = (bf16[864,768]{1,0:T(8,128)(2,1)}, bf16[864,768]{1,0:T(8,128)(2,1)S(1)}, u32[]{:S(2)}, u32[]{:S(2)}) collective-permute-start(bf16[864,768]{1,0:T(8,128)(2,1)} %collective-permute-done.1.refs_2_), channel_id=1, source_target_pairs={{0,1},{1,0},{2,3},{3,2},{4,5},{5,4},{6,7},{7,6},{8,9},{9,8},{10,11... | collective-permute-start | bytes 3981320 | tf_op jit(solution)/shard_map/ppermute | solution.py:38
  38.8 14.5 %collective-permute-start.4 = (bf16[192,768]{1,0:T(8,128)(2,1)S(1)}, bf16[192,768]{1,0:T(8,128)(2,1)S(1)}, u32[]{:S(2)}, u32[]{:S(2)}) collective-permute-start(bf16[192,768]{1,0:T(8,128)(2,1)S(1)} %copy-done.27), channel_id=1, source_target_pairs={{0,2},{1,3},{2,0},{3,1},{4,6},{5,7},{6,4},{7,5},{8,10},{9,11},{10,... | collective-permute-start | bytes 884744 | tf_op jit(solution)/shard_map/ppermute | solution.py:38
  41.3 24.5 %collective-permute-start.3 = (bf16[192,768]{1,0:T(8,128)(2,1)S(1)}, bf16[192,768]{1,0:T(8,128)(2,1)}, u32[]{:S(2)}, u32[]{:S(2)}) collective-permute-start(bf16[192,768]{1,0:T(8,128)(2,1)S(1)} %copy-done.27), channel_id=1, source_target_pairs={{0,1},{1,0},{2,3},{3,2},{4,5},{5,4},{6,7},{7,6},{8,9},{9,8},{10,11... | collective-permute-start | bytes 884744 | tf_op jit(solution)/shard_map/ppermute | solution.py:38
  53.3 12.5 %copy-start.30 = (bf16[192,768]{1,0:T(8,128)(2,1)}, bf16[192,768]{1,0:T(8,128)(2,1)S(1)}, u32[]{:S(2)}) copy-start(bf16[192,768]{1,0:T(8,128)(2,1)S(1)} %collective-permute-done.4.refs_2_) | copy-start | bytes 884740
  53.3 12.5 %collective-permute-start.5 = (bf16[192,768]{1,0:T(8,128)(2,1)S(1)}, bf16[192,768]{1,0:T(8,128)(2,1)S(1)}, u32[]{:S(2)}, u32[]{:S(2)}) collective-permute-start(bf16[192,768]{1,0:T(8,128)(2,1)S(1)} %collective-permute-done.4.refs_2_), channel_id=1, source_target_pairs={{0,1},{1,0},{2,3},{3,2},{4,5},{5,4},{6,7},{7,6},{8,9},{9,8},{10,11... | collective-permute-start | bytes 884744 | tf_op jit(solution)/shard_map/ppermute | solution.py:38
  70.7 35.0 %all-to-all-start.1 = ((bf16[8,96,768]{2,1,0:T(8,128)(2,1)}), bf16[8,96,768]{2,1,0:T(8,128)(2,1)S(1)}, u32[]{:S(2)}, u32[]{:S(2)}) async-start(bf16[8,96,768]{2,1,0:T(8,128)(2,1)} %bitcast.70), calls=%async_computation.1 | async-start | bytes 2359296 | tf_op jit(solution)/shard_map/all_to_all | solution.py:1056
  126.5 15.7 %copy-start.1 = (bf16[8,96,768]{2,1,0:T(8,128)(2,1)S(1)}, bf16[8,96,768]{2,1,0:T(8,128)(2,1)}, u32[]{:S(2)}) copy-start(bf16[8,96,768]{2,1,0:T(8,128)(2,1)} %copy-done) | copy-start | bytes 3538948
  126.6 47.2 %all-to-all-start.2 = ((bf16[8,112,768]{2,1,0:T(8,128)(2,1)}), bf16[8,112,768]{2,1,0:T(8,128)(2,1)S(1)}, u32[]{:S(2)}, u32[]{:S(2)}) async-start(bf16[8,112,768]{2,1,0:T(8,128)(2,1)} %get-tuple-element.130), calls=%async_computation.2 | async-start | bytes 2752512 | tf_op jit(solution)/shard_map/all_to_all | solution.py:1067
  173.7 7.1 %collective-permute-start.6 = (bf16[2,192,3072]{2,1,0:T(8,128)(2,1)}, bf16[2,192,3072]{2,1,0:T(8,128)(2,1)S(1)}, u32[]{:S(2)}, u32[]{:S(2)}) collective-permute-start(bf16[2,192,3072]{2,1,0:T(8,128)(2,1)} %get-tuple-element.137), channel_id=1, source_target_pairs={{0,1},{1,0},{2,3},{3,2},{4,5},{5,4},{6,7},{7,6},{8,9},{9,8},{10,11... | collective-permute-start | bytes 7077896 | tf_op jit(solution)/shard_map/ppermute | solution.py:38
  182.3 12.6 %collective-permute-start.7 = (bf16[80,3072]{1,0:T(8,128)(2,1)S(1)}, bf16[80,3072]{1,0:T(8,128)(2,1)S(1)}, u32[]{:S(2)}, u32[]{:S(2)}) collective-permute-start(bf16[80,3072]{1,0:T(8,128)(2,1)S(1)} %slice.140), channel_id=1, source_target_pairs={{0,2},{1,3},{2,0},{3,1},{4,6},{5,7},{6,4},{7,5},{8,10},{9,11},{10,... | collective-permute-start | bytes 1474568 | tf_op jit(solution)/shard_map/ppermute | solution.py:38
  183.9 30.3 %collective-permute-start.26 = (bf16[2,768,768]{2,1,0:T(8,128)(2,1)}, bf16[2,768,768]{2,1,0:T(8,128)(2,1)S(1)}, u32[]{:S(2)}, u32[]{:S(2)}) collective-permute-start(bf16[2,768,768]{2,1,0:T(8,128)(2,1)} %get-tuple-element.182), channel_id=1, source_target_pairs={{0,1},{1,0},{2,3},{3,2},{4,5},{5,4},{6,7},{7,6},{8,9},{9,8},{10,11... | collective-permute-start | bytes 7077896 | tf_op jit(solution)/shard_map/ppermute | solution.py:38
  201.4 3.8 %collective-permute-start.8 = (bf16[2,192,2048]{2,1,0:T(8,128)(2,1)}, bf16[2,192,2048]{2,1,0:T(8,128)(2,1)}, u32[]{:S(2)}, u32[]{:S(2)}) collective-permute-start(bf16[2,192,2048]{2,1,0:T(8,128)(2,1)} %get-tuple-element.150), channel_id=1, source_target_pairs={{0,1},{1,0},{2,3},{3,2},{4,5},{5,4},{6,7},{7,6},{8,9},{9,8},{10,11... | collective-permute-start | bytes 4718600 | tf_op jit(solution)/shard_map/ppermute | solution.py:38
  201.4 11.8 %copy-start.19 = (f32[256,2]{1,0:T(8,128)S(1)}, f32[256,2]{1,0:T(8,128)}, u32[]{:S(2)}) copy-start(f32[256,2]{1,0:T(8,128)} %get-tuple-element.114.gate_ref) | copy-start | bytes 6148
  201.4 9.5 %collective-permute-start.9 = (bf16[48,3072]{1,0:T(8,128)(2,1)S(1)}, bf16[48,3072]{1,0:T(8,128)(2,1)S(1)}, u32[]{:S(2)}, u32[]{:S(2)}) collective-permute-start(bf16[48,3072]{1,0:T(8,128)(2,1)S(1)} %slice.143), channel_id=1, source_target_pairs={{0,2},{1,3},{2,0},{3,1},{4,6},{5,7},{6,4},{7,5},{8,10},{9,11},{10,... | collective-permute-start | bytes 884744 | tf_op jit(solution)/shard_map/ppermute | solution.py:38
  205.1 9.1 %copy-start.5 = (bf16[2,768,768]{2,1,0:T(8,128)(2,1)S(1)}, bf16[2,768,768]{2,1,0:T(8,128)(2,1)}, u32[]{:S(2)}) copy-start(bf16[2,768,768]{2,1,0:T(8,128)(2,1)} %get-tuple-element.181) | copy-start | bytes 7077892
  210.9 32.5 %collective-permute-start.14 = (bf16[192,2048]{1,0:T(8,128)(2,1)}, bf16[192,2048]{1,0:T(8,128)(2,1)}, u32[]{:S(2)}, u32[]{:S(2)}) collective-permute-start(bf16[192,2048]{1,0:T(8,128)(2,1)} %fusion.5), channel_id=1, source_target_pairs={{0,2},{1,3},{2,0},{3,1},{4,6},{5,7},{6,4},{7,5},{8,10},{9,11},{10,... | collective-permute-start | bytes 2359304 | tf_op jit(solution)/shard_map/ppermute | solution.py:38
  216.7 54.2 %all-to-all-start.3 = ((bf16[8,96,768]{2,1,0:T(8,128)(2,1)}), bf16[8,96,768]{2,1,0:T(8,128)(2,1)S(1)}, u32[]{:S(2)}, u32[]{:S(2)}) async-start(bf16[8,96,768]{2,1,0:T(8,128)(2,1)} %bitcast.12), calls=%async_computation.3 | async-start | bytes 2359296 | tf_op jit(solution)/shard_map/all_to_all | solution.py:1102
  234.8 14.1 %collective-permute-start.10 = (bf16[2,192,1280]{2,1,0:T(8,128)(2,1)}, bf16[2,192,1280]{2,1,0:T(8,128)(2,1)S(1)}, u32[]{:S(2)}, u32[]{:S(2)}) collective-permute-start(bf16[2,192,1280]{2,1,0:T(8,128)(2,1)} %get-tuple-element.161), channel_id=1, source_target_pairs={{0,1},{1,0},{2,3},{3,2},{4,5},{5,4},{6,7},{7,6},{8,9},{9,8},{10,11... | collective-permute-start | bytes 2949128 | tf_op jit(solution)/shard_map/ppermute | solution.py:38
  242.8 5.1 %collective-permute-start.12 = (bf16[2,256,768]{2,1,0:T(8,128)(2,1)}, bf16[2,256,768]{2,1,0:T(8,128)(2,1)S(1)}, u32[]{:S(2)}, u32[]{:S(2)}) collective-permute-start(bf16[2,256,768]{2,1,0:T(8,128)(2,1)} %get-tuple-element.169), channel_id=1, source_target_pairs={{0,1},{1,0},{2,3},{3,2},{4,5},{5,4},{6,7},{7,6},{8,9},{9,8},{10,11... | collective-permute-start | bytes 2359304 | tf_op jit(solution)/shard_map/ppermute | solution.py:38
  243.4 16.5 %copy-start.24 = (bf16[80,3072]{1,0:T(8,128)(2,1)S(1)}, bf16[80,3072]{1,0:T(8,128)(2,1)}, u32[]{:S(2)}) copy-start(bf16[80,3072]{1,0:T(8,128)(2,1)} %copy-done.23) | copy-start | bytes 1474564
  245.3 14.7 %copy-start.29 = (bf16[48,3072]{1,0:T(8,128)(2,1)S(1)}, bf16[48,3072]{1,0:T(8,128)(2,1)}, u32[]{:S(2)}) copy-start(bf16[48,3072]{1,0:T(8,128)(2,1)} %copy-done.28) | copy-start | bytes 884740
  245.3 11.5 %collective-permute-start.15 = (bf16[96,2048]{1,0:T(8,128)(2,1)S(1)}, bf16[96,2048]{1,0:T(8,128)(2,1)S(1)}, u32[]{:S(2)}, u32[]{:S(2)}) collective-permute-start(bf16[96,2048]{1,0:T(8,128)(2,1)S(1)} %broadcast_select_fusion.2), channel_id=1, source_target_pairs={{0,4},{4,0},{8,12},{12,8},{16,20},{20,16},{24,28},{28,24},{1,5},{5... | collective-permute-start | bytes 1179656 | tf_op jit(solution)/shard_map/ppermute | solution.py:38
  247.4 12.0 %collective-permute-start.25 = (bf16[64,3072]{1,0:T(8,128)(2,1)S(1)}, bf16[64,3072]{1,0:T(8,128)(2,1)S(1)}, u32[]{:S(2)}, u32[]{:S(2)}) collective-permute-start(bf16[64,3072]{1,0:T(8,128)(2,1)S(1)} %copy-done.26), channel_id=1, source_target_pairs={{0,2},{1,3},{2,0},{3,1},{4,6},{5,7},{6,4},{7,5},{8,10},{9,11},{10,... | collective-permute-start | bytes 1179656 | tf_op jit(solution)/shard_map/ppermute | solution.py:38
  247.9 9.0 %copy-start.13 = (bf16[2,256,768]{2,1,0:T(8,128)(2,1)}, bf16[2,256,768]{2,1,0:T(8,128)(2,1)S(1)}, u32[]{:S(2)}) copy-start(bf16[2,256,768]{2,1,0:T(8,128)(2,1)S(1)} %collective-permute-done.12) | copy-start | bytes 2359300
  247.9 12.0 %copy-start.11 = (bf16[2,192,3072]{2,1,0:T(8,128)(2,1)S(1)}, bf16[2,192,3072]{2,1,0:T(8,128)(2,1)}, u32[]{:S(2)}) copy-start(bf16[2,192,3072]{2,1,0:T(8,128)(2,1)} %copy-done.10) | copy-start | bytes 7077892
  248.8 11.1 %copy-start.9 = (bf16[2,192,3072]{2,1,0:T(8,128)(2,1)S(1)}, bf16[2,192,3072]{2,1,0:T(8,128)(2,1)}, u32[]{:S(2)}) copy-start(bf16[2,192,3072]{2,1,0:T(8,128)(2,1)} %get-tuple-element.136) | copy-start | bytes 7077892
  248.9 21.0 %collective-permute-start.11 = (bf16[192,1280]{1,0:T(8,128)(2,1)S(1)}, bf16[192,1280]{1,0:T(8,128)(2,1)S(1)}, u32[]{:S(2)}, u32[]{:S(2)}) collective-permute-start(bf16[192,1280]{1,0:T(8,128)(2,1)S(1)} %fusion.9), channel_id=1, source_target_pairs={{0,2},{1,3},{2,0},{3,1},{4,6},{5,7},{6,4},{7,5},{8,10},{9,11},{10,... | collective-permute-start | bytes 1474568 | tf_op jit(solution)/shard_map/ppermute | solution.py:38
  257.0 6.4 %collective-permute-start.16 = (bf16[48,2048]{1,0:T(8,128)(2,1)S(1)}, bf16[48,2048]{1,0:T(8,128)(2,1)S(1)}, u32[]{:S(2)}, u32[]{:S(2)}) collective-permute-start(bf16[48,2048]{1,0:T(8,128)(2,1)S(1)} %broadcast_select_fusion.8), channel_id=1, source_target_pairs={{0,8},{4,12},{8,0},{12,4},{16,24},{20,28},{24,16},{28,20},{1,9},{5... | collective-permute-start | bytes 589832 | tf_op jit(solution)/shard_map/ppermute | solution.py:38
  259.4 24.3 %collective-permute-start.27 = (bf16[384,768]{1,0:T(8,128)(2,1)}, bf16[384,768]{1,0:T(8,128)(2,1)}, u32[]{:S(2)}, u32[]{:S(2)}) collective-permute-start(bf16[384,768]{1,0:T(8,128)(2,1)} %get-tuple-element.183), channel_id=1, source_target_pairs={{0,2},{1,3},{2,0},{3,1},{4,6},{5,7},{6,4},{7,5},{8,10},{9,11},{10,... | collective-permute-start | bytes 1769480 | tf_op jit(solution)/shard_map/ppermute | solution.py:38
  263.5 10.7 %collective-permute-start.17 = (bf16[48,2048]{1,0:T(8,128)(2,1)S(1)}, bf16[48,2048]{1,0:T(8,128)(2,1)}, u32[]{:S(2)}, u32[]{:S(2)}) collective-permute-start(bf16[48,2048]{1,0:T(8,128)(2,1)S(1)} %add_convert_fusion.14), channel_id=1, source_target_pairs={{0,16},{4,20},{8,24},{12,28},{16,0},{20,4},{24,8},{28,12},{1,17},{... | collective-permute-start | bytes 589832 | tf_op jit(solution)/shard_map/ppermute | solution.py:38
  270.9 20.1 %collective-permute-start.13 = (bf16[256,768]{1,0:T(8,128)(2,1)}, bf16[256,768]{1,0:T(8,128)(2,1)S(1)}, u32[]{:S(2)}, u32[]{:S(2)}) collective-permute-start(bf16[256,768]{1,0:T(8,128)(2,1)} %fusion.11), channel_id=1, source_target_pairs={{0,2},{1,3},{2,0},{3,1},{4,6},{5,7},{6,4},{7,5},{8,10},{9,11},{10,... | collective-permute-start | bytes 1179656 | tf_op jit(solution)/shard_map/ppermute | solution.py:38
  271.4 6.4 %collective-permute-start.20 = (bf16[96,1280]{1,0:T(8,128)(2,1)}, bf16[96,1280]{1,0:T(8,128)(2,1)S(1)}, u32[]{:S(2)}, u32[]{:S(2)}) collective-permute-start(bf16[96,1280]{1,0:T(8,128)(2,1)} %broadcast_select_fusion.5), channel_id=1, source_target_pairs={{0,4},{4,0},{8,12},{12,8},{16,20},{20,16},{24,28},{28,24},{1,5},{5... | collective-permute-start | bytes 737288 | tf_op jit(solution)/shard_map/ppermute | solution.py:38
  275.2 15.8 %copy-start.2 = (bf16[256,768]{1,0:T(8,128)(2,1)S(1)}, bf16[256,768]{1,0:T(8,128)(2,1)}, u32[]{:S(2)}) copy-start(bf16[256,768]{1,0:T(8,128)(2,1)} %refs_4_.1) | copy-start | bytes 1179652
  275.2 15.8 %copy-start.14 = (bf16[2,256,768]{2,1,0:T(8,128)(2,1)S(1)}, bf16[2,256,768]{2,1,0:T(8,128)(2,1)}, u32[]{:S(2)}) copy-start(bf16[2,256,768]{2,1,0:T(8,128)(2,1)} %copy-done.13) | copy-start | bytes 2359300
  275.3 7.6 %collective-permute-start.18 = (bf16[48,2048]{1,0:T(8,128)(2,1)S(1)}, bf16[48,2048]{1,0:T(8,128)(2,1)S(1)}, u32[]{:S(2)}, u32[]{:S(2)}) collective-permute-start(bf16[48,2048]{1,0:T(8,128)(2,1)S(1)} %add_convert_fusion.13), channel_id=1, source_target_pairs={{0,8},{4,12},{8,0},{12,4},{16,24},{20,28},{24,16},{28,20},{1,9},{5... | collective-permute-start | bytes 589832 | tf_op jit(solution)/shard_map/ppermute | solution.py:38
  277.9 6.7 %collective-permute-start.21 = (bf16[48,1280]{1,0:T(8,128)(2,1)S(1)}, bf16[48,1280]{1,0:T(8,128)(2,1)S(1)}, u32[]{:S(2)}, u32[]{:S(2)}) collective-permute-start(bf16[48,1280]{1,0:T(8,128)(2,1)S(1)} %broadcast_select_fusion.11), channel_id=1, source_target_pairs={{0,8},{4,12},{8,0},{12,4},{16,24},{20,28},{24,16},{28,20},{1,9},{5... | collective-permute-start | bytes 368648 | tf_op jit(solution)/shard_map/ppermute | solution.py:38
  282.9 10.1 %copy-start.21 = (f32[256,768]{1,0:T(8,128)S(1)}, f32[256,768]{1,0:T(8,128)}, u32[]{:S(2)}) copy-start(f32[256,768]{1,0:T(8,128)} %get-tuple-element.164) | copy-start | bytes 2359300
  282.9 14.9 %collective-permute-start.19 = (bf16[96,2048]{1,0:T(8,128)(2,1)S(1)}, bf16[96,2048]{1,0:T(8,128)(2,1)S(1)}, u32[]{:S(2)}, u32[]{:S(2)}) collective-permute-start(bf16[96,2048]{1,0:T(8,128)(2,1)S(1)} %pad_maximum_fusion.2), channel_id=1, source_target_pairs={{0,4},{4,0},{8,12},{12,8},{16,20},{20,16},{24,28},{28,24},{1,5},{5... | collective-permute-start | bytes 1179656 | tf_op jit(solution)/shard_map/ppermute | solution.py:38
  283.7 24.2 %collective-permute-start.28 = (bf16[384,768]{1,0:T(8,128)(2,1)S(1)}, bf16[384,768]{1,0:T(8,128)(2,1)S(1)}, u32[]{:S(2)}, u32[]{:S(2)}) collective-permute-start(bf16[384,768]{1,0:T(8,128)(2,1)S(1)} %copy-done.22), channel_id=1, source_target_pairs={{0,2},{1,3},{2,0},{3,1},{4,6},{5,7},{6,4},{7,5},{8,10},{9,11},{10,... | collective-permute-start | bytes 1769480 | tf_op jit(solution)/shard_map/ppermute | solution.py:38
  284.7 7.2 %collective-permute-start.22 = (bf16[48,1280]{1,0:T(8,128)(2,1)S(1)}, bf16[48,1280]{1,0:T(8,128)(2,1)S(1)}, u32[]{:S(2)}, u32[]{:S(2)}) collective-permute-start(bf16[48,1280]{1,0:T(8,128)(2,1)S(1)} %add_convert_fusion.16), channel_id=1, source_target_pairs={{0,16},{4,20},{8,24},{12,28},{16,0},{20,4},{24,8},{28,12},{1,17},{... | collective-permute-start | bytes 368648 | tf_op jit(solution)/shard_map/ppermute | solution.py:38
  291.9 4.9 %collective-permute-start.23 = (bf16[48,1280]{1,0:T(8,128)(2,1)S(1)}, bf16[48,1280]{1,0:T(8,128)(2,1)S(1)}, u32[]{:S(2)}, u32[]{:S(2)}) collective-permute-start(bf16[48,1280]{1,0:T(8,128)(2,1)S(1)} %add_convert_fusion.15), channel_id=1, source_target_pairs={{0,8},{4,12},{8,0},{12,4},{16,24},{20,28},{24,16},{28,20},{1,9},{5... | collective-permute-start | bytes 368648 | tf_op jit(solution)/shard_map/ppermute | solution.py:38
  296.9 6.3 %collective-permute-start.24 = (bf16[96,1280]{1,0:T(8,128)(2,1)S(1)}, bf16[96,1280]{1,0:T(8,128)(2,1)S(1)}, u32[]{:S(2)}, u32[]{:S(2)}) collective-permute-start(bf16[96,1280]{1,0:T(8,128)(2,1)S(1)} %pad_maximum_fusion.3), channel_id=1, source_target_pairs={{0,4},{4,0},{8,12},{12,8},{16,20},{20,16},{24,28},{28,24},{1,5},{5... | collective-permute-start | bytes 737288 | tf_op jit(solution)/shard_map/ppermute | solution.py:38
  (20 other events, 81.3 us)
